TPU v7x, 32 devices: a whole 2x2x4 slice. The times are simulated.
32 devices in a mesh: seq: 8 (over y, x, core), tp: 4 (over z).
Axes of the slice: x: 2, y: 2, z: 4, core: 2. Of those that a mesh axis runs over, the one named last changes fastest.
Arguments:
- x_codes: int32 [1024, 8192], P('seq', 'tp'), may hold values from -127 to 127
- w_codes: int32 [3, 8192, 8192], P(None, 'tp', 'seq'), may hold values from -127 to 127
- req_mult: int32 [3, 8192], P(None, 'seq'), may hold values from 64 to 255
- req_shift: int32 [3, 8192], P(None, 'seq'), may hold values from 20 to 21
- short_codes: int32 [3, 3, 8192], P(None, None, 'seq'), may hold values from -127 to 127
- residue_codes: int32 [16, 8192], P(None, 'seq'), may hold values from -127 to 127
- rates: float32 [16, 8192], P(None, 'seq'), may hold values from 0.0009765625 to 0.0625
- skip_gain: float32 [8192], P('seq'), may hold values from -4 to 4
Outputs:
- gated: bfloat16 [1024, 8192], P(('seq', 'tp'))
All inputs are finite; a program needn't handle non-finite values.
Results may differ from a plain program's by a relative error of at most 0.0057.
Values may be sent and summed in bfloat16 or wider, within the bound.
No kernel may reach another device: no remote copies, remote signals or barrier semaphores. Data moves between devices by JAX's collectives and lax.ppermute only.
A program may use at most 384 MiB of HBM per device.

v0:
```python
import math

import jax
import jax.numpy as jnp
from jax import lax
from jax.sharding import PartitionSpec as P


def shifted_lag(values, lag):
    if lag == 0:
        return values
    padded = jnp.pad(values, ((0, 0), (0, 0), (lag, 0)))
    return padded[:, :, : values.shape[2]]


def lower_toeplitz(kernel, block):
    chan_dev = kernel.shape[0]
    padded = jnp.concatenate(
        [kernel[:, ::-1], jnp.zeros((chan_dev, block - 1), jnp.float32)], axis=1
    )
    tiled = jnp.tile(padded, (1, block))
    window = tiled[:, block - 1 : block - 1 + block * (2 * block - 2)]
    return window.reshape(chan_dev, block, 2 * block - 2)[:, :, :block]


def modal_conv(drive, residues, decays, block):
    chan_dev, seqlen = drive.shape
    states = residues.shape[0]
    highest = lax.Precision.HIGHEST
    coeffs = (
        residues.astype(jnp.float32)
        * (1.0 / (127.0 * math.sqrt(states)))
        * jnp.sqrt(-jnp.expm1(-2.0 * decays))
    )
    lags = jnp.arange(block).astype(jnp.float32)
    kernel = jnp.sum(
        coeffs[:, :, None] * jnp.exp(-decays[:, :, None] * lags[None, None, :]), axis=0
    )
    toeplitz = lower_toeplitz(kernel, block)
    blocks_count = seqlen // block
    blocks = drive.reshape(chan_dev, blocks_count, block)
    inner = jnp.einsum("cij,cbj->cbi", toeplitz, blocks, precision=highest)
    tails = jnp.exp(-decays[:, :, None] * (block - 1.0 - lags)[None, None, :])
    block_sums = jnp.einsum("ncj,cbj->ncb", tails, blocks, precision=highest)
    block_ids = jnp.arange(blocks_count)
    gaps = (block_ids[:, None] - 1 - block_ids[None, :]).astype(jnp.float32)
    carried = jnp.where(
        gaps[None, None, :, :] >= 0.0,
        jnp.exp(-decays[:, :, None, None] * block * jnp.maximum(gaps, 0.0)[None, None, :, :]),
        0.0,
    )
    starts = jnp.einsum("ncbk,nck->ncb", carried, block_sums, precision=highest)
    heads = coeffs[:, :, None] * jnp.exp(-decays[:, :, None] * (lags + 1.0)[None, None, :])
    outer = jnp.einsum("nci,ncb->cbi", heads, starts, precision=highest)
    return (inner + outer).reshape(chan_dev, seqlen)


def on_device(x_codes, w_codes, req_mult, req_shift, short_codes, residue_codes, rates, skip_gain):
    seq_devs = lax.axis_size("seq")
    tp_devs = lax.axis_size("tp")
    rows_dev = x_codes.shape[0]
    seqlen = rows_dev * seq_devs
    chan_seq = w_codes.shape[2]
    chan_dev = chan_seq // tp_devs
    gathered = lax.all_gather(x_codes.astype(jnp.bfloat16), "seq", axis=0, tiled=True)
    weight_half = w_codes.astype(jnp.bfloat16)
    requant = req_mult.astype(jnp.float32) * jnp.exp2(-req_shift.astype(jnp.float32))
    channel_start = lax.axis_index("tp") * chan_dev
    weight_flat = jnp.transpose(weight_half, (1, 0, 2)).reshape(weight_half.shape[1], 3 * chan_seq)
    totals = lax.psum_scatter(
        jnp.dot(gathered, weight_flat, preferred_element_type=jnp.float32).reshape(
            seqlen // tp_devs * lax.axis_size("tp"), 3, chan_seq
        ),
        "tp",
        scatter_dimension=0,
        tiled=True,
    )
    requanted = jnp.clip(totals * requant[None, :, :], -127.0, 127.0).astype(jnp.bfloat16)
    requanted = lax.all_to_all(requanted, "tp", split_axis=2, concat_axis=0, tiled=True)
    requanted = jnp.transpose(requanted, (1, 2, 0))
    short_taps = lax.dynamic_slice_in_dim(short_codes, channel_start, chan_dev, 2).astype(
        jnp.float32
    ) * (1.0 / 128.0)
    residues = lax.dynamic_slice_in_dim(residue_codes, channel_start, chan_dev, 1)
    decays = lax.dynamic_slice_in_dim(rates, channel_start, chan_dev, 1)
    skip_part = lax.dynamic_slice_in_dim(skip_gain, channel_start, chan_dev, 0)
    values = requanted.astype(jnp.float32) * (1.0 / 64.0)
    featured = short_taps[0][:, :, None] * shifted_lag(values, 0)
    for lag in range(1, short_codes.shape[0]):
        featured = featured + short_taps[lag][:, :, None] * shifted_lag(values, lag)
    queries = featured[0]
    drive = featured[1] * featured[2]
    block = math.gcd(seqlen, 256)
    mixed = modal_conv(drive, residues, decays, block) + skip_part[:, None] * drive
    gated_cols = (queries * mixed).astype(jnp.bfloat16)
    by_rows = jnp.transpose(gated_cols)
    rows_out = seqlen // (seq_devs * tp_devs)
    spread_out = lax.all_to_all(
        by_rows.reshape(seq_devs * tp_devs, rows_out, 1, chan_dev),
        ("seq", "tp"),
        split_axis=0,
        concat_axis=2,
        tiled=True,
    )
    return spread_out.reshape(rows_out, seq_devs * tp_devs * chan_dev)


def solution(mesh):
    placed = (
        P("seq", "tp"),
        P(None, "tp", "seq"),
        P(None, "seq"),
        P(None, "seq"),
        P(None, None, "seq"),
        P(None, "seq"),
        P(None, "seq"),
        P("seq"),
    )
    return jax.shard_map(
        on_device, mesh=mesh, in_specs=placed, out_specs=P(("seq", "tp"), None), check_vma=False
    )
```

profile of v0, /device:TPU:0, one launch (start us, length us, event | category | flops | bytes accessed | tf_op | source)
XLA Modules:
  0.0 795.4 jit_solution(4241394178589676981)
XLA Ops:
  6.5 2.1 convert_element_type.70
  8.6 0.0 all-gather.2.cloned.1.call-update
  8.7 0.0 reduce-scatter.2.cloned.1.call-start
  8.7 25.2 %copy.46 = s32[3,2048,1024]{1,2,0:T(8,128)} copy(s32[3,2048,1024]{2,1,0:T(8,128)} %param.9) | data formatting | bytes 50331648 | tf_op args[1]
  33.9 14.8 %all-gather.2.cloned.1.call-done = bf16[1024,2048]{1,0:T(8,128)(2,1)} async-done(((bf16[128,2048]{1,0:T(8,128)(2,1)}), bf16[1024,2048]{1,0:T(8,128)(2,1)}) %all-gather.2.cloned.1.call-update) | async-done | bytes 4194320 | tf_op jit(solution)/shard_map/all_gather | solution.py:65
  48.7 21.8 %fusion.2 = f32[1024,3,1024]{2,0,1:T(8,128)} fusion(s32[3,2048,1024]{1,2,0:T(8,128)} %copy.46, bf16[1024,2048]{1,0:T(8,128)(2,1)} %all-gather.2.cloned.1.call-done), kind=kOutput, calls=%fused_computation.2 | convolution fusion | flops 12891193344 | bytes 41943040 | tf_op jit(solution)/shard_map/dot_general | solution.py:71
  70.5 0.0 reduce-scatter.2.cloned.1.call-update
  70.5 0.7 copy-done.7
  71.2 0.0 copy-done.8
  71.3 211.3 %reduce-scatter.2.cloned.1.call-done = f32[256,3,1024]{2,0,1:T(8,128)} async-done(((f32[1024,3,1024]{2,0,1:T(8,128)}), f32[256,3,1024]{2,0,1:T(8,128)}) %reduce-scatter.2.cloned.1.call-update) | async-done | bytes 3145744 | tf_op jit(solution)/shard_map/reduce_scatter | solution.py:70
  282.5 2.3 clamp_convert_fusion
  284.9 2.5 copy.47
  287.4 4.9 all-to-all-start
  292.3 1.3 broadcast_multiply_fusion
  293.7 0.1 copy.51
  293.8 0.1 copy.50
  293.9 0.5 copy-done.2
  294.4 0.1 copy-done.4
  294.5 2.9 multiply_reduce_fusion
  297.4 0.4 rev.3
  297.8 0.1 concatenate.3
  297.9 41.4 %tile.4 = f32[256,256,511]{2,1,0:T(8,128)} broadcast(f32[256,511]{1,0:T(8,128)S(1)} %concatenate.3), dimensions={0,2} | broadcast | bytes 134478848 | tf_op jit(solution)/shard_map/tile | solution.py:21
  339.3 117.5 %tile.10 = f32[256,130816]{1,0:T(8,128)} reshape(f32[256,256,511]{2,1,0:T(8,128)} %tile.4) | data formatting | bytes 267911168 | tf_op jit(solution)/shard_map/tile | solution.py:21
  456.8 87.2 %slice.46 = f32[256,130560]{1,0:T(8,128)} slice(f32[256,130816]{1,0:T(8,128)} %tile.10), slice={[0:256], [255:130815]} | slice | bytes 267386880 | tf_op jit(solution)/shard_map/slice | solution.py:22
  544.0 131.2 %reshape.100 = f32[256,256,510]{2,1,0:T(8,128)} reshape(f32[256,130560]{1,0:T(8,128)} %slice.46) | data formatting | bytes 267386880 | tf_op jit(solution)/shard_map/reshape | solution.py:23
  675.2 1.3 dynamic_slice.15
  676.6 0.6 fusion.32
  677.2 0.7 convert_multiply_fusion
  677.9 0.6 convert_compare_fusion
  678.5 0.7 convert_maximum_fusion
  679.2 1.8 copy.48
  681.0 2.0 convert_bitcast_fusion
  682.9 2.4 copy.49
  685.3 0.3 bitcast_multiply_fusion
  685.6 1.0 fusion.15
  686.6 1.6 copy-done
  688.3 0.1 slice_multiply_fusion
  688.4 0.4 copy.52
  688.8 61.1 %fusion = f32[256,4,256]{2,1,0:T(4,128)} fusion(f32[256,4,256]{2,1,0:T(4,128)S(1)} %copy.52, f32[256,256,510]{2,1,0:T(8,128)} %reshape.100), kind=kOutput, calls=%fused_computation | convolution fusion | flops 805306368 | bytes 69206016 | tf_op jit(solution)/shard_map/cij,cbj->cbi/dot_general | solution.py:42
  750.0 4.8 fusion.25
  754.7 1.4 copy.65
  756.1 0.8 multiply_reduce_fusion.1
  756.9 1.0 copy.63
  757.9 5.1 fusion.22
  763.0 2.5 copy.64
  765.6 1.5 fusion.29
  767.1 20.2 %all_to_all.24 = bf16[32,32,1,256]{3,1,2,0:T(8,128)(2,1)S(1)} all-to-all(bf16[32,32,1,256]{3,1,2,0:T(8,128)(2,1)S(1)} %bitcast.69), channel_id=1, replica_groups=mesh['seq'=8,'tp'=4] {'seq','tp'}, dimensions={0} | all-to-all | bytes 1048576 | tf_op jit(solution)/shard_map/all_to_all | solution.py:98
  787.3 0.8 copy.67
  (20 shorter events, 0.1 us)
Async XLA Ops:
  6.5 42.2 %all-gather.2.cloned.1.call-start = ((), (), s32[]{:S(2)}) async-start(), calls=%async_computation.3 | async-start | bytes 4718592 | tf_op jit(solution)/shard_map/all_gather | solution.py:65
  8.7 273.9 %reduce-scatter.2.cloned.1.call-start = ((), (), s32[]{:S(2)}) async-start(), calls=%async_computation.4 | async-start | bytes 15728640 | tf_op jit(solution)/shard_map/reduce_scatter | solution.py:70
  70.5 0.7 copy-start.7
  70.5 0.7 copy-start.8
  287.4 391.7 %all-to-all-start = ((bf16[256,3,1024]{0,1,2:T(4,128)(2,1)}), bf16[256,3,1024]{0,1,2:T(4,128)(2,1)}, u32[]{:S(2)}, u32[]{:S(2)}) async-start(bf16[256,3,1024]{0,1,2:T(4,128)(2,1)} %copy.47), calls=%async_computation.1 | async-start | bytes 4194304 | tf_op jit(solution)/shard_map/all_to_all | solution.py:79
  293.8 0.7 copy-start.2
  293.9 0.6 copy-start.4
  686.6 1.7 copy-start
  688.8 61.1 %copy-start.3 = (f32[16,256]{0,1:T(8,128)S(1)}, f32[16,256]{0,1:T(8,128)}, u32[]{:S(2)}) copy-start(f32[16,256]{0,1:T(8,128)} %copy-done.2) | copy-start | bytes 49156
  688.8 67.3 %copy-start.6 = (f32[16,256]{1,0:T(8,128)S(1)}, f32[16,256]{1,0:T(8,128)}, u32[]{:S(2)}) copy-start(f32[16,256]{1,0:T(8,128)} %get-tuple-element.5) | copy-start | bytes 49156
  750.0 8.0 %copy-start.5 = (f32[16,256]{0,1:T(8,128)S(1)}, f32[16,256]{0,1:T(8,128)}, u32[]{:S(2)}) copy-start(f32[16,256]{0,1:T(8,128)} %copy-done.4) | copy-start | bytes 49156
  754.7 10.8 %copy-start.1 = (f32[3,256,1024]{1,2,0:T(8,128)S(1)}, f32[3,256,1024]{1,2,0:T(8,128)}, u32[]{:S(2)}) copy-start(f32[3,256,1024]{1,2,0:T(8,128)} %copy-done) | copy-start | bytes 9437188
Sparse Core Ops, SparseCore 0:
  9.2 39.4 all-gather.1
  70.7 211.8 reduce-scatter.1
where the time goes:
time: 803 us; the launch traced here: 795 us
  local copies, waits for them, and re-layouts  420 us (52%)
  waiting for transfers between devices  226 us (28%)
  matrix products  92.8 us (12%)
  blocking collectives  20.2 us (3%)
  other arithmetic  16.9 us (2%)
  between operations  14 us (2%)
    reduce_scatter x1, waiting for transfers between devices, on_device(): lax.psum_scatter(jnp.dot(gathered, weight_flat, preferred_element_type=jn...  211 us
    another operation x2, local copies, waits for them, and re-layouts, lower_toeplitz(): tiled = jnp.tile(padded, (1, block))  159 us
    reshape x1, local copies, waits for them, and re-layouts, lower_toeplitz(): return window.reshape(chan_dev, block, 2 * block - 2)[:, :, :block]  131 us
    slice x1, local copies, waits for them, and re-layouts, lower_toeplitz(): window = tiled[:, block - 1:block - 1 + block * (2 * block - 2)]  87.2 us
    dot_general x1, matrix products, modal_conv(): inner = jnp.einsum('cij,cbj->cbi', toeplitz, blocks, precision=highest)  61.1 us
    unnamed x21, local copies, waits for them, and re-layouts  30.4 us
    dot_general x1, matrix products, on_device(): jnp.dot(gathered, weight_flat, preferred_element_type=jnp.float32)  21.8 us
    all_to_all x1, blocking collectives, on_device(): lax.all_to_all(by_rows.reshape(seq_devs * tp_devs, rows_out, 1, chan_dev)...  20.2 us
  transfers between devices with their start and end apart: 3, of which 2 were waited for; matrix products, arithmetic and copies ran while one was open for 52% of the time, Pallas kernels for 0%

commit v1 on v0

v1 whole, which is shorter than its diff:
```python
import functools
import math

import jax
import jax.numpy as jnp
from jax import lax
from jax.experimental import pallas as pl
from jax.experimental.pallas import tpu as pltpu
from jax.sharding import PartitionSpec as P

LANES = 128
WIRE = jnp.float16
WIRE_SCALE = 2.0
OUTER_PAIRS = [(0, 1), (1, 0), (2, 3), (3, 2)]
INNER_PAIRS = [(1, 2), (2, 1)]


def project_kernel(where_ref, x_ref, w_ref, scale_ref, out_ref):
    weights = w_ref[0].astype(jnp.float32).astype(jnp.bfloat16)
    out_ref[...] = (
        jnp.dot(x_ref[...], weights, preferred_element_type=jnp.float32) * scale_ref[0]
    )


def project(rows, w_codes, scale, column_block, width):
    count, features = rows.shape
    kinds = w_codes.shape[0]
    return pl.pallas_call(
        project_kernel,
        grid_spec=pltpu.PrefetchScalarGridSpec(
            num_scalar_prefetch=1,
            grid=(kinds,),
            in_specs=[
                pl.BlockSpec((count, features), lambda k, where: (0, 0)),
                pl.BlockSpec((1, features, width), lambda k, where: (k, 0, where[0])),
                pl.BlockSpec((1, 1, width), lambda k, where: (k, 0, where[0])),
            ],
            out_specs=pl.BlockSpec((count, width), lambda k, where: (0, k)),
        ),
        out_shape=jax.ShapeDtypeStruct((count, kinds * width), jnp.float32),
        compiler_params=pltpu.CompilerParams(vmem_limit_bytes=24 * 2**20),
        cost_estimate=pl.CostEstimate(
            flops=2 * count * features * kinds * width,
            bytes_accessed=4 * features * kinds * width + 4 * count * kinds * width + 2 * count * features,
            transcendentals=0,
        ),
    )(column_block, rows, w_codes, scale)


def conv_kernel(blocks, block_rows, shorts, states, place_ref, query_code_ref, key_code_ref, value_code_ref, taps_ref,
                decay_ref, decay_block_ref, coeff_ref, skip_ref, out_ref, pad_ref, query_ref, drive_ref, mixed_ref,
                sums_ref):
    sublanes = 8
    folds = blocks // sublanes
    place = place_ref[0]
    halo = 8
    for r in range(blocks):
        absolute = lax.bitwise_xor(jnp.int32(r), place)
        before = lax.bitwise_xor(jnp.maximum(absolute - 1, 0), place)
        has_before = jnp.where(absolute > 0, 1.0 / 64.0, 0.0)
        featured = []
        for k, coded_ref in enumerate((query_code_ref, key_code_ref, value_code_ref)):
            tail_start = pl.multiple_of(before * block_rows + block_rows - 16, 16)
            tail = coded_ref[pl.ds(tail_start, 16), :].astype(jnp.float32) * has_before
            pad_ref[k, pl.ds(0, halo), :] = tail[16 - halo:, :]
            now = coded_ref[pl.ds(r * block_rows, block_rows), :].astype(jnp.float32) * (1.0 / 64.0)
            pad_ref[k, pl.ds(halo, block_rows), :] = now
            total = taps_ref[0, pl.ds(k, 1), :] * now
            for lag in range(1, shorts):
                total = total + taps_ref[lag, pl.ds(k, 1), :] * pad_ref[k, pl.ds(halo - lag, block_rows), :]
            featured.append(total)
        query_ref[pl.ds(r * block_rows, block_rows), :] = featured[0]
        drive_ref[pl.ds(r * block_rows, block_rows), :] = featured[1] * featured[2]
    decays = [jnp.broadcast_to(decay_ref[pl.ds(n, 1), :], (sublanes, LANES)) for n in range(states)]
    for fold in range(folds):
        base = fold * sublanes * block_rows

        def local(i, held):
            now = drive_ref[pl.ds(base + i, sublanes, stride=block_rows), :]
            return tuple(held[n] * decays[n] + now for n in range(states))

        zero = jnp.zeros((sublanes, LANES), jnp.float32)
        held = lax.fori_loop(0, block_rows, local, (zero,) * states, unroll=4)
        for n in range(states):
            sums_ref[n, pl.ds(fold * sublanes, sublanes), :] = held[n]
    carry = jnp.zeros((states, LANES), jnp.float32)
    for a in range(blocks):
        r = lax.bitwise_xor(jnp.int32(a), place)
        own = sums_ref[:, pl.ds(r, 1), :].reshape(states, LANES)
        sums_ref[:, pl.ds(r, 1), :] = carry.reshape(states, 1, LANES)
        carry = carry * decay_block_ref[...] + own
    coeffs = [jnp.broadcast_to(coeff_ref[pl.ds(n, 1), :], (sublanes, LANES)) for n in range(states)]
    for fold in range(folds):
        base = fold * sublanes * block_rows

        def whole(i, held):
            now = drive_ref[pl.ds(base + i, sublanes, stride=block_rows), :]
            held = tuple(held[n] * decays[n] + now for n in range(states))
            parts = [held[n] * coeffs[n] for n in range(states)]
            while len(parts) > 1:
                parts = [parts[j] + parts[j + 1] for j in range(0, len(parts), 2)]
            mixed_ref[pl.ds(base + i, sublanes, stride=block_rows), :] = parts[0]
            return held

        start = tuple(sums_ref[n, pl.ds(fold * sublanes, sublanes), :] for n in range(states))
        lax.fori_loop(0, block_rows, whole, start, unroll=4)
    for r in range(blocks):
        rows = pl.ds(r * block_rows, block_rows)
        gated = query_ref[rows, :] * (mixed_ref[rows, :] + skip_ref[...] * drive_ref[rows, :])
        out_ref[lax.bitwise_xor(jnp.int32(r), place)] = gated.astype(jnp.bfloat16)


def hyena(coded, blocks, taps, decay, decay_block, coeff, skip, place, column_start):
    shorts, kinds, _ = taps.shape
    rows, width = coded.shape[0], coded.shape[1] // kinds
    block_rows, states = rows // blocks, decay.shape[0]
    tiles = width // LANES
    scalars = jnp.stack([place, column_start])
    return pl.pallas_call(
        functools.partial(conv_kernel, blocks, block_rows, shorts, states),
        grid_spec=pltpu.PrefetchScalarGridSpec(
            num_scalar_prefetch=1,
            grid=(width // LANES,),
            in_specs=[
                pl.BlockSpec((rows, LANES), lambda c, s: (0, c)),
                pl.BlockSpec((rows, LANES), lambda c, s: (0, tiles + c)),
                pl.BlockSpec((rows, LANES), lambda c, s: (0, 2 * tiles + c)),
                pl.BlockSpec((shorts, kinds, LANES), lambda c, s: (0, 0, s[1] + c)),
                pl.BlockSpec((states, LANES), lambda c, s: (0, s[1] + c)),
                pl.BlockSpec((states, LANES), lambda c, s: (0, s[1] + c)),
                pl.BlockSpec((states, LANES), lambda c, s: (0, s[1] + c)),
                pl.BlockSpec((1, LANES), lambda c, s: (0, s[1] + c)),
            ],
            out_specs=pl.BlockSpec((blocks, block_rows, LANES), lambda c, s: (0, 0, c)),
            scratch_shapes=[
                pltpu.VMEM((3, 8 + block_rows, LANES), jnp.float32),
                pltpu.VMEM((rows, LANES), jnp.float32),
                pltpu.VMEM((rows, LANES), jnp.float32),
                pltpu.VMEM((rows, LANES), jnp.float32),
                pltpu.VMEM((states, blocks, LANES), jnp.float32),
            ],
        ),
        out_shape=jax.ShapeDtypeStruct((blocks, block_rows, width), jnp.bfloat16),
        compiler_params=pltpu.CompilerParams(vmem_limit_bytes=32 * 2**20),
        cost_estimate=pl.CostEstimate(
            flops=6 * rows * width * states, bytes_accessed=8 * rows * width, transcendentals=0
        ),
    )(scalars, coded, coded, coded, taps, decay, decay_block, coeff, skip)


def on_device(x_codes, w_codes, req_mult, req_shift, short_codes, residue_codes, rates, skip_gain):
    seq_devs = lax.axis_size("seq")
    tp_devs = lax.axis_size("tp")
    assert tp_devs == 4
    place = lax.axis_index("seq")
    layer = lax.axis_index("tp")
    outer = (layer == 0) | (layer == 3)
    rows_dev, features = x_codes.shape
    kinds, _, chan_seq = w_codes.shape
    states = rates.shape[0]
    half = chan_seq // 2
    width = math.gcd(half, 256)
    groups = half // width

    def swap(values, mask):
        return lax.ppermute(values, "seq", [(s, s ^ mask) for s in range(seq_devs)])

    own = x_codes.astype(jnp.bfloat16)
    pairs = [jnp.concatenate([own, swap(own, 1)])]
    for mask in range(2, seq_devs, 2):
        far = swap(own, mask)
        pairs.append(jnp.concatenate([far, swap(far, 1)]))

    requant = req_mult.astype(jnp.float32) * jnp.exp2(-req_shift.astype(jnp.float32))
    scale = (requant * WIRE_SCALE).reshape(kinds, 1, chan_seq)
    taps = short_codes.astype(jnp.float32) * (1.0 / 128.0)
    coeff = (
        residue_codes.astype(jnp.float32)
        * (1.0 / (127.0 * math.sqrt(states)))
        * jnp.sqrt(-jnp.expm1(-2.0 * rates))
    )
    decay = jnp.exp(-rates)
    decay_block = jnp.exp(-rates * rows_dev)
    skip = skip_gain.reshape(1, chan_seq)

    pieces = [(g, 0) for g in range(groups)]
    pieces += [(g, q) for g in range(groups) for q in range(1, seq_devs // 2)]
    count = len(pieces)
    half_first = 1 - layer % 2
    half_second = layer % 2

    def partial(index, which):
        g, q = pieces[index]
        block = (which * groups + g).reshape(1).astype(jnp.int32)
        return project(pairs[q], w_codes, scale, block, width)

    first, second = {}, {}
    got_outer, got_inner = {}, {}
    finals = {}
    first[0] = partial(0, half_first)
    gated = [None] * groups
    for t in range(count + 3):
        send_outer = send_inner = None
        if t < count + 2:
            if t < 2:
                send_outer = first[t]
            else:
                send_outer = first[t - 2] + got_inner[t - 1].astype(jnp.float32)
                if t < count:
                    send_outer = jnp.where(outer, first[t], send_outer)
            send_outer = send_outer.astype(WIRE)
        if t >= 1:
            if t < 3:
                mine = second[t - 1]
            elif t <= count:
                mine = jnp.where(outer, second[t - 3], second[t - 1])
            else:
                mine = second[t - 3]
            total = mine + got_outer[t - 1].astype(jnp.float32)
            if t <= count:
                send_inner = total.astype(WIRE)
            if t >= 3:
                finals[t - 3] = jnp.clip(total * (1.0 / WIRE_SCALE), -127.0, 127.0).astype(jnp.bfloat16)
        if send_inner is not None and send_outer is not None:
            send_outer, send_inner = lax.optimization_barrier((send_outer, send_inner))
        if send_outer is not None:
            got_outer[t] = lax.ppermute(send_outer, "tp", OUTER_PAIRS)
        if send_inner is not None:
            got_inner[t] = lax.ppermute(send_inner, "tp", INNER_PAIRS)
        if t + 1 < count:
            first[t + 1] = partial(t + 1, half_first)
        if t < count:
            second[t] = partial(t, half_second)
        for g in range(groups):
            members = [i for i, piece in enumerate(pieces) if piece[0] == g]
            if t - 3 == members[-1]:
                members = sorted(members, key=lambda i: pieces[i][1])
                coded = jnp.concatenate([finals[i] for i in members])
                column_start = (jnp.where(layer == 0, 0, groups) + g) * (width // LANES)
                gated[g] = hyena(coded, seq_devs, taps, decay, decay_block, coeff, skip, place, column_start)

    rows_out = rows_dev // tp_devs
    mine = jnp.concatenate(gated, axis=2).reshape(seq_devs * tp_devs, rows_out, half)
    spread = lax.all_to_all(mine, ("seq", "tp"), split_axis=0, concat_axis=0, tiled=True)
    spread = spread.reshape(seq_devs, tp_devs, rows_out, half)
    spread = jnp.stack([spread[:, 0], spread[:, 3]], axis=1)
    return jnp.transpose(spread, (2, 0, 1, 3)).reshape(rows_out, seq_devs * chan_seq)


def solution(mesh):
    placed = (
        P("seq", "tp"),
        P(None, "tp", "seq"),
        P(None, "seq"),
        P(None, "seq"),
        P(None, None, "seq"),
        P(None, "seq"),
        P(None, "seq"),
        P("seq"),
    )
    return jax.shard_map(
        on_device, mesh=mesh, in_specs=placed, out_specs=P(("seq", "tp"), None), check_vma=False
    )
```

time: 803 us -> 243 us (0.30)
  local copies, waits for them, and re-layouts: 420 us -> 95.1 us
  waiting for transfers between devices: 226 us -> 12.1 us
  matrix products: 92.8 us -> 0 us
  Pallas kernels: 0 us -> 47 us
  starting transfers between devices: 4.97 us -> 45.2 us
  between operations: 14 us -> 0.73 us
    reduce_scatter x1 -> x0, waiting for transfers between devices: 211 us -> none  [on_device(): lax.psum_scatter(jnp.dot(gathered, weight_flat, preferred_element_type=jn...]
    another operation x2 -> x0, local copies, waits for them, and re-layouts: 159 us -> none  [lower_toeplitz(): tiled = jnp.tile(padded, (1, block))]
    reshape x2, local copies, waits for them, and re-layouts: 134 us -> 1.2 us  [the longest x1 1.18 us: on_device(): jnp.transpose(spread, (2, 0, 1, 3)).reshape(rows_out, seq_devs * chan_seq)]
    dot_general x4 -> x0, matrix products: 92.8 us -> none  [the longest x1 61.1 us: modal_conv(): inner = jnp.einsum('cij,cbj->cbi', toeplitz, blocks, precision=highest)]
    slice x1, local copies, waits for them, and re-layouts: 87.2 us -> 0.04 us  [on_device(): spread = jnp.stack([spread[:, 0], spread[:, 3]], axis=1)]
    unnamed x21 -> x43, local copies, waits for them, and re-layouts: 30.4 us -> 93.7 us
    pallas_call x0 -> x18, Pallas kernels: none -> 47 us  [the longest x16 31.8 us: project(): pl.pallas_call(project_kernel, grid_spec=pltpu.PrefetchScalarGridSpec(num...]
    ppermute x0 -> x25, starting transfers between devices: none -> 45.2 us  [the longest x10 33.1 us: on_device(): got_outer[t] = lax.ppermute(send_outer, 'tp', OUTER_PAIRS)]
  transfers between devices with their start and end apart: 3 -> 25, of which waited for: 2 -> 2; matrix products, arithmetic and copies ran while one was open for 52% -> 4% of each run, Pallas kernels for 0% -> 16%
where the time goes in v1:
time: 243 us; the launch traced here: 241 us
  local copies, waits for them, and re-layouts  95.1 us (39%)
  Pallas kernels  47 us (19%)
  starting transfers between devices  45.2 us (19%)
  blocking collectives  28.2 us (12%)
  other arithmetic  12.1 us (5%)
  waiting for transfers between devices  12.1 us (5%)
    unnamed x43, local copies, waits for them, and re-layouts  93.7 us
    ppermute x10, starting transfers between devices, on_device(): got_outer[t] = lax.ppermute(send_outer, 'tp', OUTER_PAIRS)  33.1 us
    pallas_call x16, Pallas kernels, project(): pl.pallas_call(project_kernel, grid_spec=pltpu.PrefetchScalarGridSpec(num...  31.8 us
    all_to_all x1, blocking collectives, on_device(): lax.all_to_all(mine, ('seq', 'tp'), split_axis=0, concat_axis=0, tiled=True)  28.2 us
    pallas_call x2, Pallas kernels, hyena(): pl.pallas_call(functools.partial(conv_kernel, blocks, block_rows, shorts,...  15.2 us
    ppermute x7, waiting for transfers between devices, swap(): return lax.ppermute(values, 'seq', [(s, s ^ mask) for s in range(seq_devs)])  8.54 us
    ppermute x8, starting transfers between devices, on_device(): got_inner[t] = lax.ppermute(send_inner, 'tp', INNER_PAIRS)  6.37 us
    ppermute x7, starting transfers between devices, swap(): return lax.ppermute(values, 'seq', [(s, s ^ mask) for s in range(seq_devs)])  5.74 us
  transfers between devices with their start and end apart: 25, of which 2 were waited for; matrix products, arithmetic and copies ran while one was open for 4% of the time, Pallas kernels for 16%

profile of v1, /device:TPU:0, one launch (start us, length us, event | category | flops | bytes accessed | tf_op | source)
XLA Modules:
  0.0 240.5 jit_solution(11126139775560503935)
XLA Ops:
  0.0 1.3 convert_element_type.147
  1.8 2.6 %collective-permute-start.1 = (bf16[128,2048]{1,0:T(8,128)(2,1)S(1)}, bf16[128,2048]{1,0:T(8,128)(2,1)}, u32[]{:S(2)}, u32[]{:S(2)}) collective-permute-start(bf16[128,2048]{1,0:T(8,128)(2,1)S(1)} %convert_element_type.147), channel_id=1, source_target_pairs={{0,8},{4,12},{8,0},{12,4},{16,24},{20,28},{24,16},{28,20},{1,9},{5... | collective-permute-start | bytes 1572872 | tf_op jit(solution)/shard_map/ppermute | solution.py:166
  5.3 8.2 %copy-done = s32[3,2048,1024]{2,1,0:T(8,128)S(1)} copy-done((s32[3,2048,1024]{2,1,0:T(8,128)S(1)}, s32[3,2048,1024]{2,1,0:T(8,128)}, u32[]{:S(2)}) %copy-start) | copy-done | bytes 25165848
  13.4 2.0 shard_map.85
  16.2 1.6 collective-permute-start.3
  17.8 1.5 collective-permute-start.9
  20.3 8.2 %copy-done.1 = s32[3,2048,1024]{2,1,0:T(8,128)S(1)} copy-done((s32[3,2048,1024]{2,1,0:T(8,128)S(1)}, s32[3,2048,1024]{2,1,0:T(8,128)}, u32[]{:S(2)}) %copy-start.1) | copy-done | bytes 25165848
  28.5 2.0 shard_map.82
  30.5 2.0 shard_map.86
  34.3 8.5 %collective-permute-done.9 = bf16[128,2048]{1,0:T(8,128)(2,1)} collective-permute-done((bf16[128,2048]{1,0:T(8,128)(2,1)S(1)}, bf16[128,2048]{1,0:T(8,128)(2,1)}, u32[]{:S(2)}, u32[]{:S(2)}) %collective-permute-start.9) | collective-permute-done | bytes 524320 | tf_op jit(solution)/shard_map/ppermute | solution.py:166
  42.9 8.2 %copy-done.2 = s32[3,2048,1024]{2,1,0:T(8,128)S(1)} copy-done((s32[3,2048,1024]{2,1,0:T(8,128)S(1)}, s32[3,2048,1024]{2,1,0:T(8,128)}, u32[]{:S(2)}) %copy-start.2) | copy-done | bytes 25165848
  51.0 2.0 shard_map.87
  53.8 8.1 %copy-done.3 = s32[3,2048,1024]{2,1,0:T(8,128)S(1)} copy-done((s32[3,2048,1024]{2,1,0:T(8,128)S(1)}, s32[3,2048,1024]{2,1,0:T(8,128)}, u32[]{:S(2)}) %copy-start.3) | copy-done | bytes 25165848
  61.9 2.0 shard_map.84
  64.2 4.4 %collective-permute-start.6 = (f16[256,768]{1,0:T(8,128)(2,1)S(1)}, f16[256,768]{1,0:T(8,128)(2,1)S(1)}, u32[]{:S(2)}, u32[]{:S(2)}) collective-permute-start(f16[256,768]{1,0:T(8,128)(2,1)S(1)} %select_convert_fusion.5), channel_id=1, source_target_pairs={{0,1},{1,0},{2,3},{3,2},{4,5},{5,4},{6,7},{7,6},{8,9},{9,8},{10,11... | collective-permute-start | bytes 1179656 | tf_op jit(solution)/shard_map/ppermute | solution.py:227
  70.5 2.0 shard_map.83
  72.6 2.0 shard_map.90
  74.6 3.6 %collective-permute-done.6 = f16[256,768]{1,0:T(8,128)(2,1)S(1)} collective-permute-done((f16[256,768]{1,0:T(8,128)(2,1)S(1)}, f16[256,768]{1,0:T(8,128)(2,1)S(1)}, u32[]{:S(2)}, u32[]{:S(2)}) %collective-permute-start.6) | collective-permute-done | bytes 393248 | tf_op jit(solution)/shard_map/ppermute | solution.py:227
  78.5 5.0 %collective-permute-start.13 = (f16[256,768]{1,0:T(8,128)(2,1)S(1)}, f16[256,768]{1,0:T(8,128)(2,1)S(1)}, u32[]{:S(2)}, u32[]{:S(2)}) collective-permute-start(f16[256,768]{1,0:T(8,128)(2,1)S(1)} %select_convert_fusion.4), channel_id=1, source_target_pairs={{0,1},{1,0},{2,3},{3,2},{4,5},{5,4},{6,7},{7,6},{8,9},{9,8},{10,11... | collective-permute-start | bytes 1179656 | tf_op jit(solution)/shard_map/ppermute | solution.py:227
  84.3 2.0 shard_map.91
  86.3 8.1 %copy-done.4 = s32[3,2048,1024]{2,1,0:T(8,128)S(1)} copy-done((s32[3,2048,1024]{2,1,0:T(8,128)S(1)}, s32[3,2048,1024]{2,1,0:T(8,128)}, u32[]{:S(2)}) %copy-start.4) | copy-done | bytes 25165848
  94.4 2.0 shard_map.89
  96.8 2.5 %collective-permute-start.14 = (f16[256,768]{1,0:T(8,128)(2,1)S(1)}, f16[256,768]{1,0:T(8,128)(2,1)S(1)}, u32[]{:S(2)}, u32[]{:S(2)}) collective-permute-start(f16[256,768]{1,0:T(8,128)(2,1)S(1)} %select_convert_fusion.3), channel_id=1, source_target_pairs={{0,1},{1,0},{2,3},{3,2},{4,5},{5,4},{6,7},{7,6},{8,9},{9,8},{10,11... | collective-permute-start | bytes 1179656 | tf_op jit(solution)/shard_map/ppermute | solution.py:227
  99.9 2.0 shard_map.88
  101.9 8.1 %copy-done.5 = s32[3,2048,1024]{2,1,0:T(8,128)S(1)} copy-done((s32[3,2048,1024]{2,1,0:T(8,128)S(1)}, s32[3,2048,1024]{2,1,0:T(8,128)}, u32[]{:S(2)}) %copy-start.5) | copy-done | bytes 25165848
  110.1 2.0 shard_map.93
  113.2 2.2 collective-permute-start.16
  116.1 8.1 %copy-done.6 = s32[3,2048,1024]{2,1,0:T(8,128)S(1)} copy-done((s32[3,2048,1024]{2,1,0:T(8,128)S(1)}, s32[3,2048,1024]{2,1,0:T(8,128)}, u32[]{:S(2)}) %copy-start.6) | copy-done | bytes 25165848
  124.2 2.0 shard_map.92
  126.2 8.1 %copy-done.7 = s32[3,2048,1024]{2,1,0:T(8,128)S(1)} copy-done((s32[3,2048,1024]{2,1,0:T(8,128)S(1)}, s32[3,2048,1024]{2,1,0:T(8,128)}, u32[]{:S(2)}) %copy-start.7) | copy-done | bytes 25165848
  134.4 2.0 shard_map.95
  137.4 2.5 %collective-permute-start.18 = (f16[256,768]{1,0:T(8,128)(2,1)S(1)}, f16[256,768]{1,0:T(8,128)(2,1)S(1)}, u32[]{:S(2)}, u32[]{:S(2)}) collective-permute-start(f16[256,768]{1,0:T(8,128)(2,1)S(1)} %select_convert_fusion.1), channel_id=1, source_target_pairs={{0,1},{1,0},{2,3},{3,2},{4,5},{5,4},{6,7},{7,6},{8,9},{9,8},{10,11... | collective-permute-start | bytes 1179656 | tf_op jit(solution)/shard_map/ppermute | solution.py:227
  140.8 8.1 %copy-done.8 = s32[3,2048,1024]{2,1,0:T(8,128)S(1)} copy-done((s32[3,2048,1024]{2,1,0:T(8,128)S(1)}, s32[3,2048,1024]{2,1,0:T(8,128)}, u32[]{:S(2)}) %copy-start.8) | copy-done | bytes 25165848
  148.9 2.0 shard_map.94
  150.9 8.1 %copy-done.9 = s32[3,2048,1024]{2,1,0:T(8,128)S(1)} copy-done((s32[3,2048,1024]{2,1,0:T(8,128)S(1)}, s32[3,2048,1024]{2,1,0:T(8,128)}, u32[]{:S(2)}) %copy-start.9) | copy-done | bytes 25165848
  159.1 2.0 shard_map.98
  162.9 4.6 %collective-permute-start.20 = (f16[256,768]{1,0:T(8,128)(2,1)S(1)}, f16[256,768]{1,0:T(8,128)(2,1)S(1)}, u32[]{:S(2)}, u32[]{:S(2)}) collective-permute-start(f16[256,768]{1,0:T(8,128)(2,1)S(1)} %select_convert_fusion), channel_id=1, source_target_pairs={{0,1},{1,0},{2,3},{3,2},{4,5},{5,4},{6,7},{7,6},{8,9},{9,8},{10,11... | collective-permute-start | bytes 1179656 | tf_op jit(solution)/shard_map/ppermute | solution.py:227
  167.4 8.2 %copy-done.10 = s32[3,2048,1024]{2,1,0:T(8,128)S(1)} copy-done((s32[3,2048,1024]{2,1,0:T(8,128)S(1)}, s32[3,2048,1024]{2,1,0:T(8,128)}, u32[]{:S(2)}) %copy-start.10) | copy-done | bytes 25165848
  175.6 2.0 shard_map.97
  179.6 1.4 collective-permute-start.23
  181.2 1.4 collective-permute-start.22
  182.6 1.1 add_convert_fusion
  183.8 8.5 %collective-permute-start.24 = (f16[256,768]{1,0:T(8,128)(2,1)S(1)}, f16[256,768]{1,0:T(8,128)(2,1)S(1)}, u32[]{:S(2)}, u32[]{:S(2)}) collective-permute-start(f16[256,768]{1,0:T(8,128)(2,1)S(1)} %add_convert_fusion), channel_id=1, source_target_pairs={{0,1},{1,0},{2,3},{3,2},{4,5},{5,4},{6,7},{7,6},{8,9},{9,8},{10,11... | collective-permute-start | bytes 1179656 | tf_op jit(solution)/shard_map/ppermute | solution.py:227
  192.4 7.6 %shard_map.96 = bf16[8,128,256]{2,1,0:T(8,128)(2,1)S(1)} custom-call(s32[2]{0:T(128)S(1)} %get-tuple-element.54.place_ref, bf16[1024,768]{1,0:T(8,128)(2,1)S(1)} %pad_maximum_fusion.query_code_ref.key_code_ref.value_code_ref, bf16[1024,768]{1,0:T(8,128)(2,1)S(1)} %pad_maximum_fusion.query_code_ref.key_code_ref.value_code_ref, ...), custom_call_target="tpu_custom_call" | custom-call | flops 25165824 | bytes 2097152 | tf_op jit(solution)/shard_map/pallas_call | solution.py:119
  201.1 7.6 %shard_map.99 = bf16[8,128,256]{2,1,0:T(8,128)(2,1)S(1)} custom-call(s32[2]{0:T(128)S(1)} %get-tuple-element.55.place_ref, bf16[1024,768]{1,0:T(8,128)(2,1)S(1)} %pad_maximum_fusion.1.query_code_ref.key_code_ref.value_code_ref, bf16[1024,768]{1,0:T(8,128)(2,1)S(1)} %pad_maximum_fusion.1.query_code_ref.key_code_ref.value_code_ref, ...), custom_call_target="tpu_custom_call" | custom-call | flops 25165824 | bytes 2097152 | tf_op jit(solution)/shard_map/pallas_call | solution.py:119
  208.8 28.2 %all_to_all.5 = bf16[32,32,512]{2,1,0:T(8,128)(2,1)S(1)} all-to-all(bf16[32,32,512]{2,1,0:T(8,128)(2,1)S(1)} %bitcast.14), channel_id=1, replica_groups=mesh['seq'=8,'tp'=4] {'seq','tp'}, dimensions={0} | all-to-all | bytes 2097152 | tf_op jit(solution)/shard_map/all_to_all | solution.py:244
  238.1 1.2 maximum_bitcast_fusion
  239.3 1.2 reshape.47
  (100 shorter events, 19.9 us)
Async XLA Ops:
  1.3 3.9 %collective-permute-start = (bf16[128,2048]{1,0:T(8,128)(2,1)S(1)}, bf16[128,2048]{1,0:T(8,128)(2,1)S(1)}, u32[]{:S(2)}, u32[]{:S(2)}) collective-permute-start(bf16[128,2048]{1,0:T(8,128)(2,1)S(1)} %convert_element_type.147), channel_id=1, source_target_pairs={{0,4},{4,0},{8,12},{12,8},{16,20},{20,16},{24,28},{28,24},{1,5},{5... | collective-permute-start | bytes 1572872 | tf_op jit(solution)/shard_map/ppermute | solution.py:166
  1.8 30.7 %collective-permute-start.1 = (bf16[128,2048]{1,0:T(8,128)(2,1)S(1)}, bf16[128,2048]{1,0:T(8,128)(2,1)}, u32[]{:S(2)}, u32[]{:S(2)}) collective-permute-start(bf16[128,2048]{1,0:T(8,128)(2,1)S(1)} %convert_element_type.147), channel_id=1, source_target_pairs={{0,8},{4,12},{8,0},{12,4},{16,24},{20,28},{24,16},{28,20},{1,9},{5... | collective-permute-start | bytes 1572872 | tf_op jit(solution)/shard_map/ppermute | solution.py:166
  5.3 8.2 %copy-start = (s32[3,2048,1024]{2,1,0:T(8,128)S(1)}, s32[3,2048,1024]{2,1,0:T(8,128)}, u32[]{:S(2)}) copy-start(s32[3,2048,1024]{2,1,0:T(8,128)} %w_ref.31) | copy-start | bytes 75497472
  16.2 16.4 %collective-permute-start.3 = (f16[256,768]{1,0:T(8,128)(2,1)}, f16[256,768]{1,0:T(8,128)(2,1)S(1)}, u32[]{:S(2)}, u32[]{:S(2)}) collective-permute-start(f16[256,768]{1,0:T(8,128)(2,1)} %convert_element_type.151), channel_id=1, source_target_pairs={{0,1},{1,0},{2,3},{3,2},{4,5},{5,4},{6,7},{7,6},{8,9},{9,8},{10,11... | collective-permute-start | bytes 1179656 | tf_op jit(solution)/shard_map/ppermute | solution.py:227
  17.8 25.1 %collective-permute-start.9 = (bf16[128,2048]{1,0:T(8,128)(2,1)S(1)}, bf16[128,2048]{1,0:T(8,128)(2,1)}, u32[]{:S(2)}, u32[]{:S(2)}) collective-permute-start(bf16[128,2048]{1,0:T(8,128)(2,1)S(1)} %convert_element_type.147), channel_id=1, source_target_pairs={{0,16},{4,20},{8,24},{12,28},{16,0},{20,4},{24,8},{28,12},{1,17},{... | collective-permute-start | bytes 1572872 | tf_op jit(solution)/shard_map/ppermute | solution.py:166
  19.3 50.4 %collective-permute-start.7 = (bf16[128,2048]{1,0:T(8,128)(2,1)S(1)}, bf16[128,2048]{1,0:T(8,128)(2,1)S(1)}, u32[]{:S(2)}, u32[]{:S(2)}) collective-permute-start(bf16[128,2048]{1,0:T(8,128)(2,1)S(1)} %convert_element_type.147), channel_id=1, source_target_pairs={{0,24},{4,28},{8,16},{12,20},{16,8},{20,12},{24,0},{28,4},{1,25},{... | collective-permute-start | bytes 1572872 | tf_op jit(solution)/shard_map/ppermute | solution.py:166
  20.3 8.2 %copy-start.1 = (s32[3,2048,1024]{2,1,0:T(8,128)S(1)}, s32[3,2048,1024]{2,1,0:T(8,128)}, u32[]{:S(2)}) copy-start(s32[3,2048,1024]{2,1,0:T(8,128)} %w_ref.31) | copy-start | bytes 75497472
  32.5 21.2 %collective-permute-start.2 = (bf16[128,2048]{1,0:T(8,128)(2,1)}, bf16[128,2048]{1,0:T(8,128)(2,1)S(1)}, u32[]{:S(2)}, u32[]{:S(2)}) collective-permute-start(bf16[128,2048]{1,0:T(8,128)(2,1)} %collective-permute-done.1), channel_id=1, source_target_pairs={{0,4},{4,0},{8,12},{12,8},{16,20},{20,16},{24,28},{28,24},{1,5},{5... | collective-permute-start | bytes 1572872 | tf_op jit(solution)/shard_map/ppermute | solution.py:166
  32.7 31.2 %collective-permute-start.5 = (f16[256,768]{1,0:T(8,128)(2,1)S(1)}, f16[256,768]{1,0:T(8,128)(2,1)S(1)}, u32[]{:S(2)}, u32[]{:S(2)}) collective-permute-start(f16[256,768]{1,0:T(8,128)(2,1)S(1)} %convert_element_type.150), channel_id=1, source_target_pairs={{0,1},{1,0},{2,3},{3,2},{4,5},{5,4},{6,7},{7,6},{8,9},{9,8},{10,11... | collective-permute-start | bytes 1179656 | tf_op jit(solution)/shard_map/ppermute | solution.py:227
  42.8 26.9 %collective-permute-start.10 = (bf16[128,2048]{1,0:T(8,128)(2,1)}, bf16[128,2048]{1,0:T(8,128)(2,1)S(1)}, u32[]{:S(2)}, u32[]{:S(2)}) collective-permute-start(bf16[128,2048]{1,0:T(8,128)(2,1)} %collective-permute-done.9), channel_id=1, source_target_pairs={{0,4},{4,0},{8,12},{12,8},{16,20},{20,16},{24,28},{28,24},{1,5},{5... | collective-permute-start | bytes 1572872 | tf_op jit(solution)/shard_map/ppermute | solution.py:166
  42.9 8.2 %copy-start.2 = (s32[3,2048,1024]{2,1,0:T(8,128)S(1)}, s32[3,2048,1024]{2,1,0:T(8,128)}, u32[]{:S(2)}) copy-start(s32[3,2048,1024]{2,1,0:T(8,128)} %w_ref.31) | copy-start | bytes 75497472
  53.0 11.0 %collective-permute-start.4 = (f16[256,768]{1,0:T(8,128)(2,1)S(1)}, f16[256,768]{1,0:T(8,128)(2,1)S(1)}, u32[]{:S(2)}, u32[]{:S(2)}) collective-permute-start(f16[256,768]{1,0:T(8,128)(2,1)S(1)} %add_convert_fusion.3), channel_id=1, source_target_pairs={{1,2},{2,1},{5,6},{6,5},{9,10},{10,9},{13,14},{14,13},{17,18},{18,... | collective-permute-start | bytes 1179656 | tf_op jit(solution)/shard_map/ppermute | solution.py:229
  53.8 8.2 %copy-start.3 = (s32[3,2048,1024]{2,1,0:T(8,128)S(1)}, s32[3,2048,1024]{2,1,0:T(8,128)}, u32[]{:S(2)}) copy-start(s32[3,2048,1024]{2,1,0:T(8,128)} %w_ref.31) | copy-start | bytes 75497472
  64.2 13.9 %collective-permute-start.6 = (f16[256,768]{1,0:T(8,128)(2,1)S(1)}, f16[256,768]{1,0:T(8,128)(2,1)S(1)}, u32[]{:S(2)}, u32[]{:S(2)}) collective-permute-start(f16[256,768]{1,0:T(8,128)(2,1)S(1)} %select_convert_fusion.5), channel_id=1, source_target_pairs={{0,1},{1,0},{2,3},{3,2},{4,5},{5,4},{6,7},{7,6},{8,9},{9,8},{10,11... | collective-permute-start | bytes 1179656 | tf_op jit(solution)/shard_map/ppermute | solution.py:227
  69.7 13.8 %collective-permute-start.8 = (bf16[128,2048]{1,0:T(8,128)(2,1)S(1)}, bf16[128,2048]{1,0:T(8,128)(2,1)S(1)}, u32[]{:S(2)}, u32[]{:S(2)}) collective-permute-start(bf16[128,2048]{1,0:T(8,128)(2,1)S(1)} %collective-permute-done.7), channel_id=1, source_target_pairs={{0,4},{4,0},{8,12},{12,8},{16,20},{20,16},{24,28},{28,24},{1,5},{5... | collective-permute-start | bytes 1572872 | tf_op jit(solution)/shard_map/ppermute | solution.py:166
  69.8 8.5 %collective-permute-start.11 = (f16[256,768]{1,0:T(8,128)(2,1)S(1)}, f16[256,768]{1,0:T(8,128)(2,1)S(1)}, u32[]{:S(2)}, u32[]{:S(2)}) collective-permute-start(f16[256,768]{1,0:T(8,128)(2,1)S(1)} %add_convert_fusion.2), channel_id=1, source_target_pairs={{1,2},{2,1},{5,6},{6,5},{9,10},{10,9},{13,14},{14,13},{17,18},{18,... | collective-permute-start | bytes 1179656 | tf_op jit(solution)/shard_map/ppermute | solution.py:229
  78.5 17.9 %collective-permute-start.13 = (f16[256,768]{1,0:T(8,128)(2,1)S(1)}, f16[256,768]{1,0:T(8,128)(2,1)S(1)}, u32[]{:S(2)}, u32[]{:S(2)}) collective-permute-start(f16[256,768]{1,0:T(8,128)(2,1)S(1)} %select_convert_fusion.4), channel_id=1, source_target_pairs={{0,1},{1,0},{2,3},{3,2},{4,5},{5,4},{6,7},{7,6},{8,9},{9,8},{10,11... | collective-permute-start | bytes 1179656 | tf_op jit(solution)/shard_map/ppermute | solution.py:227
  83.6 13.1 %collective-permute-start.12 = (f16[256,768]{1,0:T(8,128)(2,1)S(1)}, f16[256,768]{1,0:T(8,128)(2,1)S(1)}, u32[]{:S(2)}, u32[]{:S(2)}) collective-permute-start(f16[256,768]{1,0:T(8,128)(2,1)S(1)} %get-tuple-element.25), channel_id=1, source_target_pairs={{1,2},{2,1},{5,6},{6,5},{9,10},{10,9},{13,14},{14,13},{17,18},{18,... | collective-permute-start | bytes 1179656 | tf_op jit(solution)/shard_map/ppermute | solution.py:229
  86.3 8.2 %copy-start.4 = (s32[3,2048,1024]{2,1,0:T(8,128)S(1)}, s32[3,2048,1024]{2,1,0:T(8,128)}, u32[]{:S(2)}) copy-start(s32[3,2048,1024]{2,1,0:T(8,128)} %w_ref.31) | copy-start | bytes 75497472
  96.8 15.3 %collective-permute-start.14 = (f16[256,768]{1,0:T(8,128)(2,1)S(1)}, f16[256,768]{1,0:T(8,128)(2,1)S(1)}, u32[]{:S(2)}, u32[]{:S(2)}) collective-permute-start(f16[256,768]{1,0:T(8,128)(2,1)S(1)} %select_convert_fusion.3), channel_id=1, source_target_pairs={{0,1},{1,0},{2,3},{3,2},{4,5},{5,4},{6,7},{7,6},{8,9},{9,8},{10,11... | collective-permute-start | bytes 1179656 | tf_op jit(solution)/shard_map/ppermute | solution.py:227
  99.2 13.8 %collective-permute-start.15 = (f16[256,768]{1,0:T(8,128)(2,1)S(1)}, f16[256,768]{1,0:T(8,128)(2,1)S(1)}, u32[]{:S(2)}, u32[]{:S(2)}) collective-permute-start(f16[256,768]{1,0:T(8,128)(2,1)S(1)} %get-tuple-element.28), channel_id=1, source_target_pairs={{1,2},{2,1},{5,6},{6,5},{9,10},{10,9},{13,14},{14,13},{17,18},{18,... | collective-permute-start | bytes 1179656 | tf_op jit(solution)/shard_map/ppermute | solution.py:229
  101.9 8.2 %copy-start.5 = (s32[3,2048,1024]{2,1,0:T(8,128)S(1)}, s32[3,2048,1024]{2,1,0:T(8,128)}, u32[]{:S(2)}) copy-start(s32[3,2048,1024]{2,1,0:T(8,128)} %w_ref.31) | copy-start | bytes 75497472
  113.2 23.2 %collective-permute-start.16 = (f16[256,768]{1,0:T(8,128)(2,1)S(1)}, f16[256,768]{1,0:T(8,128)(2,1)S(1)}, u32[]{:S(2)}, u32[]{:S(2)}) collective-permute-start(f16[256,768]{1,0:T(8,128)(2,1)S(1)} %select_convert_fusion.2), channel_id=1, source_target_pairs={{0,1},{1,0},{2,3},{3,2},{4,5},{5,4},{6,7},{7,6},{8,9},{9,8},{10,11... | collective-permute-start | bytes 1179656 | tf_op jit(solution)/shard_map/ppermute | solution.py:227
  115.4 21.9 %collective-permute-start.17 = (f16[256,768]{1,0:T(8,128)(2,1)S(1)}, f16[256,768]{1,0:T(8,128)(2,1)S(1)}, u32[]{:S(2)}, u32[]{:S(2)}) collective-permute-start(f16[256,768]{1,0:T(8,128)(2,1)S(1)} %get-tuple-element.30), channel_id=1, source_target_pairs={{1,2},{2,1},{5,6},{6,5},{9,10},{10,9},{13,14},{14,13},{17,18},{18,... | collective-permute-start | bytes 1179656 | tf_op jit(solution)/shard_map/ppermute | solution.py:229
  116.0 8.2 %copy-start.6 = (s32[3,2048,1024]{2,1,0:T(8,128)S(1)}, s32[3,2048,1024]{2,1,0:T(8,128)}, u32[]{:S(2)}) copy-start(s32[3,2048,1024]{2,1,0:T(8,128)} %w_ref.31) | copy-start | bytes 75497472
  126.2 8.2 %copy-start.7 = (s32[3,2048,1024]{2,1,0:T(8,128)S(1)}, s32[3,2048,1024]{2,1,0:T(8,128)}, u32[]{:S(2)}) copy-start(s32[3,2048,1024]{2,1,0:T(8,128)} %w_ref.31) | copy-start | bytes 75497472
  137.4 23.6 %collective-permute-start.18 = (f16[256,768]{1,0:T(8,128)(2,1)S(1)}, f16[256,768]{1,0:T(8,128)(2,1)S(1)}, u32[]{:S(2)}, u32[]{:S(2)}) collective-permute-start(f16[256,768]{1,0:T(8,128)(2,1)S(1)} %select_convert_fusion.1), channel_id=1, source_target_pairs={{0,1},{1,0},{2,3},{3,2},{4,5},{5,4},{6,7},{7,6},{8,9},{9,8},{10,11... | collective-permute-start | bytes 1179656 | tf_op jit(solution)/shard_map/ppermute | solution.py:227
  139.9 22.1 %collective-permute-start.19 = (f16[256,768]{1,0:T(8,128)(2,1)S(1)}, f16[256,768]{1,0:T(8,128)(2,1)S(1)}, u32[]{:S(2)}, u32[]{:S(2)}) collective-permute-start(f16[256,768]{1,0:T(8,128)(2,1)S(1)} %get-tuple-element.32), channel_id=1, source_target_pairs={{1,2},{2,1},{5,6},{6,5},{9,10},{10,9},{13,14},{14,13},{17,18},{18,... | collective-permute-start | bytes 1179656 | tf_op jit(solution)/shard_map/ppermute | solution.py:229
  140.8 8.2 %copy-start.8 = (s32[3,2048,1024]{2,1,0:T(8,128)S(1)}, s32[3,2048,1024]{2,1,0:T(8,128)}, u32[]{:S(2)}) copy-start(s32[3,2048,1024]{2,1,0:T(8,128)} %w_ref.31) | copy-start | bytes 75497472
  150.9 8.2 %copy-start.9 = (s32[3,2048,1024]{2,1,0:T(8,128)S(1)}, s32[3,2048,1024]{2,1,0:T(8,128)}, u32[]{:S(2)}) copy-start(s32[3,2048,1024]{2,1,0:T(8,128)} %w_ref.31) | copy-start | bytes 75497472
  162.2 15.4 %collective-permute-start.21 = (f16[256,768]{1,0:T(8,128)(2,1)S(1)}, f16[256,768]{1,0:T(8,128)(2,1)S(1)}, u32[]{:S(2)}, u32[]{:S(2)}) collective-permute-start(f16[256,768]{1,0:T(8,128)(2,1)S(1)} %get-tuple-element.34), channel_id=1, source_target_pairs={{1,2},{2,1},{5,6},{6,5},{9,10},{10,9},{13,14},{14,13},{17,18},{18,... | collective-permute-start | bytes 1179656 | tf_op jit(solution)/shard_map/ppermute | solution.py:229
  162.9 15.6 %collective-permute-start.20 = (f16[256,768]{1,0:T(8,128)(2,1)S(1)}, f16[256,768]{1,0:T(8,128)(2,1)S(1)}, u32[]{:S(2)}, u32[]{:S(2)}) collective-permute-start(f16[256,768]{1,0:T(8,128)(2,1)S(1)} %select_convert_fusion), channel_id=1, source_target_pairs={{0,1},{1,0},{2,3},{3,2},{4,5},{5,4},{6,7},{7,6},{8,9},{9,8},{10,11... | collective-permute-start | bytes 1179656 | tf_op jit(solution)/shard_map/ppermute | solution.py:227
  167.4 8.2 %copy-start.10 = (s32[3,2048,1024]{2,1,0:T(8,128)S(1)}, s32[3,2048,1024]{2,1,0:T(8,128)}, u32[]{:S(2)}) copy-start(s32[3,2048,1024]{2,1,0:T(8,128)} %w_ref.31) | copy-start | bytes 75497472
  177.6 3.4 %copy-start.18 = (s32[3,3,1024]{2,1,0:T(4,128)S(1)}, s32[3,3,1024]{2,1,0:T(4,128)}, u32[]{:S(2)}) copy-start(s32[3,3,1024]{2,1,0:T(4,128)} %param.12) | copy-start | bytes 110596
  177.6 3.5 %copy-start.16 = (f32[16,1024]{1,0:T(8,128)S(1)}, f32[16,1024]{1,0:T(8,128)}, u32[]{:S(2)}) copy-start(f32[16,1024]{1,0:T(8,128)} %param.14) | copy-start | bytes 196612
  177.6 3.5 %copy-start.17 = (s32[16,1024]{1,0:T(8,128)S(1)}, s32[16,1024]{1,0:T(8,128)}, u32[]{:S(2)}) copy-start(s32[16,1024]{1,0:T(8,128)} %param.13) | copy-start | bytes 196612
  179.6 3.1 %collective-permute-start.23 = (f16[256,768]{1,0:T(8,128)(2,1)}, f16[256,768]{1,0:T(8,128)(2,1)}, u32[]{:S(2)}, u32[]{:S(2)}) collective-permute-start(f16[256,768]{1,0:T(8,128)(2,1)} %get-tuple-element.36), channel_id=1, source_target_pairs={{1,2},{2,1},{5,6},{6,5},{9,10},{10,9},{13,14},{14,13},{17,18},{18,... | collective-permute-start | bytes 1179656 | tf_op jit(solution)/shard_map/ppermute | solution.py:229
  181.0 11.3 %copy-start.12 = (bf16[256,768]{1,0:T(8,128)(2,1)S(1)}, bf16[256,768]{1,0:T(8,128)(2,1)}, u32[]{:S(2)}) copy-start(bf16[256,768]{1,0:T(8,128)(2,1)} %get-tuple-element.39) | copy-start | bytes 1179652
  181.0 11.3 %copy-start.13 = (bf16[256,768]{1,0:T(8,128)(2,1)S(1)}, bf16[256,768]{1,0:T(8,128)(2,1)}, u32[]{:S(2)}) copy-start(bf16[256,768]{1,0:T(8,128)(2,1)} %get-tuple-element.41) | copy-start | bytes 1179652
  181.0 11.3 %copy-start.14 = (bf16[256,768]{1,0:T(8,128)(2,1)S(1)}, bf16[256,768]{1,0:T(8,128)(2,1)}, u32[]{:S(2)}) copy-start(bf16[256,768]{1,0:T(8,128)(2,1)} %get-tuple-element.43) | copy-start | bytes 1179652
  181.2 11.2 %copy-start.11 = (f32[1024]{0:T(1024)S(1)}, f32[1024]{0:T(1024)}, u32[]{:S(2)}) copy-start(f32[1024]{0:T(1024)} %param.15) | copy-start | bytes 12292
  181.2 18.8 %collective-permute-start.22 = (f16[256,768]{1,0:T(8,128)(2,1)}, f16[256,768]{1,0:T(8,128)(2,1)S(1)}, u32[]{:S(2)}, u32[]{:S(2)}) collective-permute-start(f16[256,768]{1,0:T(8,128)(2,1)} %add_convert_fusion.1), channel_id=1, source_target_pairs={{0,1},{1,0},{2,3},{3,2},{4,5},{5,4},{6,7},{7,6},{8,9},{9,8},{10,11... | collective-permute-start | bytes 1179656 | tf_op jit(solution)/shard_map/ppermute | solution.py:227
  183.8 16.4 %collective-permute-start.24 = (f16[256,768]{1,0:T(8,128)(2,1)S(1)}, f16[256,768]{1,0:T(8,128)(2,1)S(1)}, u32[]{:S(2)}, u32[]{:S(2)}) collective-permute-start(f16[256,768]{1,0:T(8,128)(2,1)S(1)} %add_convert_fusion), channel_id=1, source_target_pairs={{0,1},{1,0},{2,3},{3,2},{4,5},{5,4},{6,7},{7,6},{8,9},{9,8},{10,11... | collective-permute-start | bytes 1179656 | tf_op jit(solution)/shard_map/ppermute | solution.py:227
  200.0 1.0 copy-start.15

commit v2 on v1

--- a/solution.py
+++ b/solution.py
@@ -15,36 +15,74 @@
 INNER_PAIRS = [(1, 2), (2, 1)]
 
 
-def project_kernel(where_ref, x_ref, w_ref, scale_ref, out_ref):
-    weights = w_ref[0].astype(jnp.float32).astype(jnp.bfloat16)
-    out_ref[...] = (
-        jnp.dot(x_ref[...], weights, preferred_element_type=jnp.float32) * scale_ref[0]
-    )
-
-
-def project(rows, w_codes, scale, column_block, width):
-    count, features = rows.shape
+ANYWHERE = pl.BlockSpec(memory_space=pl.ANY)
+
+
+def pass_kernel(value_ref, *refs):
+    pass
+
+
+def after(value, token):
+    return pl.pallas_call(
+        pass_kernel,
+        in_specs=[ANYWHERE, ANYWHERE],
+        out_specs=ANYWHERE,
+        out_shape=jax.ShapeDtypeStruct(value.shape, value.dtype),
+        input_output_aliases={0: 0},
+    )(value, token)
+
+
+def project_kernel(parts, groups, where_ref, *refs):
+    row_refs = refs[:parts]
+    w_ref, scale_ref, _ = refs[parts : parts + 3]
+    *out_refs, rows_ref = refs[parts + 3 :]
+
+    @pl.when(pl.program_id(0) == 0)
+    def assemble():
+        size = row_refs[0].shape[0]
+        for i, row_ref in enumerate(row_refs):
+            rows_ref[pl.ds(i * size, size), :] = row_ref[...]
+
+    width = w_ref.shape[2] // groups
+    count = out_refs[0].shape[0]
+    for g in range(groups):
+        columns = slice(g * width, (g + 1) * width)
+        weights = w_ref[0, :, columns].astype(jnp.float32).astype(jnp.bfloat16)
+        sums = jnp.dot(rows_ref[...], weights, preferred_element_type=jnp.float32) * scale_ref[0, :, columns]
+        for i, out_ref in enumerate(out_refs[g::groups]):
+            out_ref[...] = sums[i * count : (i + 1) * count]
+
+
+def project(blocks, w_codes, scale, block, groups, width, token):
+    size, features = blocks[0].shape
+    count = size * len(blocks)
+    outs = groups * len(blocks) // 2
     kinds = w_codes.shape[0]
+    columns = groups * width
     return pl.pallas_call(
-        project_kernel,
+        functools.partial(project_kernel, len(blocks), groups),
         grid_spec=pltpu.PrefetchScalarGridSpec(
             num_scalar_prefetch=1,
             grid=(kinds,),
-            in_specs=[
-                pl.BlockSpec((count, features), lambda k, where: (0, 0)),
-                pl.BlockSpec((1, features, width), lambda k, where: (k, 0, where[0])),
-                pl.BlockSpec((1, 1, width), lambda k, where: (k, 0, where[0])),
+            in_specs=[pl.BlockSpec((size, features), lambda k, where: (0, 0))] * len(blocks)
+            + [
+                pl.BlockSpec((1, features, columns), lambda k, where: (k, 0, where[0])),
+                pl.BlockSpec((1, 1, columns), lambda k, where: (k, 0, where[0])),
+                ANYWHERE,
             ],
-            out_specs=pl.BlockSpec((count, width), lambda k, where: (0, k)),
+            out_specs=[pl.BlockSpec((2 * size, width), lambda k, where: (0, k))] * outs,
+            scratch_shapes=[pltpu.VMEM((count, features), jnp.bfloat16)],
         ),
-        out_shape=jax.ShapeDtypeStruct((count, kinds * width), jnp.float32),
-        compiler_params=pltpu.CompilerParams(vmem_limit_bytes=24 * 2**20),
-        cost_estimate=pl.CostEstimate(
-            flops=2 * count * features * kinds * width,
-            bytes_accessed=4 * features * kinds * width + 4 * count * kinds * width + 2 * count * features,
-            transcendentals=0,
-        ),
-    )(column_block, rows, w_codes, scale)
+        out_shape=[jax.ShapeDtypeStruct((2 * size, kinds * width), jnp.float32)] * outs,
+        compiler_params=pltpu.CompilerParams(vmem_limit_bytes=48 * 2**20),
+        cost_estimate=pl.CostEstimate(flops=1, bytes_accessed=1, transcendentals=0),
+    )(
+        block.reshape(1).astype(jnp.int32),
+        *blocks,
+        pltpu.with_memory_space_constraint(w_codes, pltpu.HBM),
+        scale,
+        token,
+    )
 
 
 def conv_kernel(blocks, block_rows, shorts, states, place_ref, query_code_ref, key_code_ref, value_code_ref, taps_ref,
@@ -141,10 +179,8 @@
             ],
         ),
         out_shape=jax.ShapeDtypeStruct((blocks, block_rows, width), jnp.bfloat16),
-        compiler_params=pltpu.CompilerParams(vmem_limit_bytes=32 * 2**20),
-        cost_estimate=pl.CostEstimate(
-            flops=6 * rows * width * states, bytes_accessed=8 * rows * width, transcendentals=0
-        ),
+        compiler_params=pltpu.CompilerParams(vmem_limit_bytes=48 * 2**20),
+        cost_estimate=pl.CostEstimate(flops=1, bytes_accessed=1, transcendentals=0),
     )(scalars, coded, coded, coded, taps, decay, decay_block, coeff, skip)
 
 
@@ -166,10 +202,11 @@
         return lax.ppermute(values, "seq", [(s, s ^ mask) for s in range(seq_devs)])
 
     own = x_codes.astype(jnp.bfloat16)
-    pairs = [jnp.concatenate([own, swap(own, 1)])]
+    far = {mask: swap(own, mask) for mask in range(2, seq_devs, 2)}
+    blocks = {0: own, 1: swap(own, 1)}
     for mask in range(2, seq_devs, 2):
-        far = swap(own, mask)
-        pairs.append(jnp.concatenate([far, swap(far, 1)]))
+        blocks[mask] = swap(own, mask)
+        blocks[mask + 1] = swap(blocks[mask], 1)
 
     requant = req_mult.astype(jnp.float32) * jnp.exp2(-req_shift.astype(jnp.float32))
     scale = (requant * WIRE_SCALE).reshape(kinds, 1, chan_seq)
@@ -183,22 +220,32 @@
     decay_block = jnp.exp(-rates * rows_dev)
     skip = skip_gain.reshape(1, chan_seq)
 
-    pieces = [(g, 0) for g in range(groups)]
-    pieces += [(g, q) for g in range(groups) for q in range(1, seq_devs // 2)]
+    pairs = list(range(2, seq_devs // 2))
+    pieces = [(g, q) for q in (0, 1) for g in range(groups)]
+    pieces += [(g, q) for g in range(groups) for q in pairs]
     count = len(pieces)
     half_first = 1 - layer % 2
     half_second = layer % 2
 
-    def partial(index, which):
-        g, q = pieces[index]
-        block = (which * groups + g).reshape(1).astype(jnp.int32)
-        return project(pairs[q], w_codes, scale, block, width)
+    def partials(store, members, which, token):
+        chosen, members = members
+        taken = [blocks[2 * q + j] for q in members for j in range(2)]
+        block = (which * groups + chosen[0]) // len(chosen)
+        results = project(taken, w_codes, scale, block, len(chosen), width, token)
+        store.update(zip([pieces.index((g, q)) for q in members for g in chosen], results))
+
+    calls = {pieces.index((0, q)): (list(range(groups)), [q]) for q in (0, 1)}
+    for g in range(groups):
+        for i in range(0, len(pairs), 2):
+            calls[pieces.index((g, pairs[i]))] = [g], pairs[i : i + 2]
 
     first, second = {}, {}
     got_outer, got_inner = {}, {}
     finals = {}
-    first[0] = partial(0, half_first)
+    token = jnp.zeros((8, LANES), jnp.float32)
+    partials(first, calls[0], half_first, token)
     gated = [None] * groups
+    ready = [max(i for i, piece in enumerate(pieces) if piece[0] == g) + 3 for g in range(groups)]
     for t in range(count + 3):
         send_outer = send_inner = None
         if t < count + 2:
@@ -221,30 +268,50 @@
                 send_inner = total.astype(WIRE)
             if t >= 3:
                 finals[t - 3] = jnp.clip(total * (1.0 / WIRE_SCALE), -127.0, 127.0).astype(jnp.bfloat16)
+        for g in range(groups):
+            if t == ready[g] + 1 and send_outer is not None:
+                send_outer, gated[g] = lax.optimization_barrier((send_outer, gated[g]))
         if send_inner is not None and send_outer is not None:
             send_outer, send_inner = lax.optimization_barrier((send_outer, send_inner))
         if send_outer is not None:
             got_outer[t] = lax.ppermute(send_outer, "tp", OUTER_PAIRS)
         if send_inner is not None:
             got_inner[t] = lax.ppermute(send_inner, "tp", INNER_PAIRS)
-        if t + 1 < count:
-            first[t + 1] = partial(t + 1, half_first)
-        if t < count:
-            second[t] = partial(t, half_second)
+        if t in calls:
+            partials(second, calls[t], half_second, blocks.get(6, token) if calls[t][1] == [1] else token)
+        if t + 1 in calls:
+            partials(first, calls[t + 1], half_first, blocks.get(4, token) if calls[t + 1][1] == [1] else token)
         for g in range(groups):
             members = [i for i, piece in enumerate(pieces) if piece[0] == g]
-            if t - 3 == members[-1]:
+            if t == ready[g]:
                 members = sorted(members, key=lambda i: pieces[i][1])
                 coded = jnp.concatenate([finals[i] for i in members])
                 column_start = (jnp.where(layer == 0, 0, groups) + g) * (width // LANES)
                 gated[g] = hyena(coded, seq_devs, taps, decay, decay_block, coeff, skip, place, column_start)
 
     rows_out = rows_dev // tp_devs
-    mine = jnp.concatenate(gated, axis=2).reshape(seq_devs * tp_devs, rows_out, half)
-    spread = lax.all_to_all(mine, ("seq", "tp"), split_axis=0, concat_axis=0, tiled=True)
-    spread = spread.reshape(seq_devs, tp_devs, rows_out, half)
-    spread = jnp.stack([spread[:, 0], spread[:, 3]], axis=1)
-    return jnp.transpose(spread, (2, 0, 1, 3)).reshape(rows_out, seq_devs * chan_seq)
+
+    def spread(values):
+        width = values.shape[2]
+        parts = values.reshape(seq_devs, tp_devs, rows_out, width)
+        step = jnp.where(layer < 2, 1, -1)
+
+        def slice_for(distance):
+            target = jnp.clip(layer + distance * step, 0, tp_devs - 1)
+            return lax.dynamic_index_in_dim(parts, target, 1, keepdims=False)
+
+        near = lax.ppermute(slice_for(1), "tp", OUTER_PAIRS)
+        middle = lax.ppermute(slice_for(2), "tp", [(0, 2), (2, 0), (1, 3), (3, 1)])
+        opposite = lax.ppermute(slice_for(3), "tp", [(0, 3), (3, 0)])
+        kept = slice_for(0)
+        low = jnp.where(layer == 0, kept, jnp.where(layer == 1, near, jnp.where(layer == 2, middle, opposite)))
+        high = jnp.where(layer == 3, kept, jnp.where(layer == 2, near, jnp.where(layer == 1, middle, opposite)))
+        return low, high
+
+    halves = [spread(values) for values in gated]
+    mine = jnp.concatenate([low for low, _ in halves] + [high for _, high in halves], axis=2)
+    landed = lax.all_to_all(mine, "seq", split_axis=0, concat_axis=0, tiled=True)
+    return jnp.transpose(landed, (1, 0, 2)).reshape(rows_out, seq_devs * chan_seq)
 
 
 def solution(mesh):

time: 243 us -> 181 us (0.74)
  local copies, waits for them, and re-layouts: 95.1 us -> 2.66 us
  blocking collectives: 28.2 us -> 12.2 us
  other arithmetic: 12.1 us -> 27.5 us
  Pallas kernels: 47 us -> 59.4 us
  waiting for transfers between devices: 12.1 us -> 23 us
  starting transfers between devices: 45.2 us -> 54.1 us
    unnamed x43 -> x64, local copies, waits for them, and re-layouts: 93.7 us -> 1.03 us
    all_to_all x1, blocking collectives: 28.2 us -> 12.2 us  [on_device(): lax.all_to_all(mine, 'seq', split_axis=0, concat_axis=0, tiled=True)]
    ppermute x10, waiting for transfers between devices: 3.58 us -> 17.2 us  [on_device(): got_outer[t] = lax.ppermute(send_outer, 'tp', OUTER_PAIRS)]
    ppermute x0 -> x6, starting transfers between devices: none -> 12.6 us  [the longest x2 6.64 us: spread(): opposite = lax.ppermute(slice_for(3), 'tp', [(0, 3), (3, 0)])]
    pallas_call x16 -> x8, Pallas kernels: 31.8 us -> 44.2 us  [project(): pl.pallas_call(functools.partial(project_kernel, len(blocks), groups), gr...]
    ppermute x7, waiting for transfers between devices: 8.54 us -> 1.2 us  [swap(): return lax.ppermute(values, 'seq', [(s, s ^ mask) for s in range(seq_devs)])]
    convert_element_type x10, other arithmetic: 3.55 us -> 10.6 us  [on_device(): send_outer = send_outer.astype(WIRE)]
    ppermute x10, starting transfers between devices: 33.1 us -> 26.4 us  [on_device(): got_outer[t] = lax.ppermute(send_outer, 'tp', OUTER_PAIRS)]
  transfers between devices with their start and end apart: 25 -> 31, of which waited for: 2 -> 11; matrix products, arithmetic and copies ran while one was open for 4% -> 12% of each run, Pallas kernels for 16% -> 33%
where the time goes in v2:
time: 181 us; the launch traced here: 179 us
  Pallas kernels  59.4 us (33%)
  starting transfers between devices  54.1 us (30%)
  other arithmetic  27.5 us (15%)
  waiting for transfers between devices  23 us (13%)
  blocking collectives  12.2 us (7%)
  local copies, waits for them, and re-layouts  2.66 us (1%)
    pallas_call x8, Pallas kernels, project(): pl.pallas_call(functools.partial(project_kernel, len(blocks), groups), gr...  44.2 us
    ppermute x10, starting transfers between devices, on_device(): got_outer[t] = lax.ppermute(send_outer, 'tp', OUTER_PAIRS)  26.4 us
    ppermute x10, waiting for transfers between devices, on_device(): got_outer[t] = lax.ppermute(send_outer, 'tp', OUTER_PAIRS)  17.2 us
    pallas_call x2, Pallas kernels, hyena(): pl.pallas_call(functools.partial(conv_kernel, blocks, block_rows, shorts,...  15.2 us
    all_to_all x1, blocking collectives, on_device(): lax.all_to_all(mine, 'seq', split_axis=0, concat_axis=0, tiled=True)  12.2 us
    convert_element_type x10, other arithmetic, on_device(): send_outer = send_outer.astype(WIRE)  10.6 us
    convert_element_type x8, other arithmetic, on_device(): jnp.clip(total * (1.0 / WIRE_SCALE), -127.0, 127.0).astype(jnp.bfloat16)  9.32 us
    ppermute x8, starting transfers between devices, on_device(): got_inner[t] = lax.ppermute(send_inner, 'tp', INNER_PAIRS)  8.49 us
  transfers between devices with their start and end apart: 31, of which 11 were waited for; matrix products, arithmetic and copies ran while one was open for 12% of the time, Pallas kernels for 33%

profile of v2, /device:TPU:0, one launch (start us, length us, event | category | flops | bytes accessed | tf_op | source)
XLA Modules:
  0.0 179.5 jit_solution(18400808021310042028)
XLA Ops:
  0.0 1.3 convert_element_type.147.refs_0_
  1.8 2.6 %collective-permute-start.4 = (bf16[128,2048]{1,0:T(8,128)(2,1)S(1)}, bf16[128,2048]{1,0:T(8,128)(2,1)S(1)}, u32[]{:S(2)}, u32[]{:S(2)}) collective-permute-start(bf16[128,2048]{1,0:T(8,128)(2,1)S(1)} %convert_element_type.147.refs_0_), channel_id=1, source_target_pairs={{0,8},{4,12},{8,0},{12,4},{16,24},{20,28},{24,16},{28,20},{1,9},{5... | collective-permute-start | bytes 1572872 | tf_op jit(solution)/shard_map/ppermute | solution.py:202
  5.2 6.1 %shard_map.85 = (f32[256,768]{1,0:T(8,128)S(1)}, f32[256,768]{1,0:T(8,128)S(1)}) custom-call(s32[1]{0:T(128)} %bitcast.2.where_ref, bf16[128,2048]{1,0:T(8,128)(2,1)S(1)} %convert_element_type.147.refs_0_, bf16[128,2048]{1,0:T(8,128)(2,1)S(1)} %collective-permute-done.6.refs_1_, s32[3,2048,1024]{2,1,0:T(8,128)} %refs_4_.7, ...), custom_call_target="tpu_custom_call" | custom-call | flops 1 | bytes 1 | tf_op jit(solution)/shard_map/pallas_call | solution.py:62
  12.3 1.6 collective-permute-start.7
  13.9 1.5 collective-permute-start
  15.4 6.1 %shard_map.86 = (f32[256,768]{1,0:T(8,128)S(1)}, f32[256,768]{1,0:T(8,128)S(1)}) custom-call(s32[1]{0:T(128)} %bitcast.3.where_ref, bf16[128,2048]{1,0:T(8,128)(2,1)S(1)} %convert_element_type.147.refs_0_, bf16[128,2048]{1,0:T(8,128)(2,1)S(1)} %collective-permute-done.6.refs_1_, s32[3,2048,1024]{2,1,0:T(8,128)} %refs_4_.7, ...), custom_call_target="tpu_custom_call" | custom-call | flops 1 | bytes 1 | tf_op jit(solution)/shard_map/pallas_call | solution.py:62
  22.4 1.3 collective-permute-done.7
  24.6 1.4 collective-permute-start.8
  26.0 3.7 %collective-permute-start.9 = (f16[256,768]{1,0:T(8,128)(2,1)}, f16[256,768]{1,0:T(8,128)(2,1)}, u32[]{:S(2)}, u32[]{:S(2)}) collective-permute-start(f16[256,768]{1,0:T(8,128)(2,1)} %convert_element_type.150), channel_id=1, source_target_pairs={{0,1},{1,0},{2,3},{3,2},{4,5},{5,4},{6,7},{7,6},{8,9},{9,8},{10,11... | collective-permute-start | bytes 1179656 | tf_op jit(solution)/shard_map/ppermute | solution.py:277
  29.7 1.9 %collective-permute-start.2 = (bf16[128,2048]{1,0:T(8,128)(2,1)S(1)}, bf16[128,2048]{1,0:T(8,128)(2,1)S(1)}, u32[]{:S(2)}, u32[]{:S(2)}) collective-permute-start(bf16[128,2048]{1,0:T(8,128)(2,1)S(1)} %convert_element_type.147.refs_0_), channel_id=1, source_target_pairs={{0,24},{4,28},{8,16},{12,20},{16,8},{20,12},{24,0},{28,4},{1,25},{... | collective-permute-start | bytes 1572872 | tf_op jit(solution)/shard_map/ppermute | solution.py:202
  31.7 6.3 %shard_map.84 = (f32[256,768]{1,0:T(8,128)S(1)}, f32[256,768]{1,0:T(8,128)S(1)}) custom-call(s32[1]{0:T(128)} %bitcast.2.where_ref, bf16[128,2048]{1,0:T(8,128)(2,1)S(1)} %collective-permute-done.4.refs_0_, bf16[128,2048]{1,0:T(8,128)(2,1)S(1)} %collective-permute-done.5.refs_1_, s32[3,2048,1024]{2,1,0:T(8,128)} %refs_4_.7, ...), custom_call_target="tpu_custom_call" | custom-call | flops 1 | bytes 1 | tf_op jit(solution)/shard_map/pallas_call | solution.py:62
  38.0 1.2 select_convert_fusion.5
  42.0 1.2 collective-permute-done.2.refs_2_.refs_4_
  43.2 6.1 %shard_map.87 = (f32[256,768]{1,0:T(8,128)S(1)}, f32[256,768]{1,0:T(8,128)S(1)}) custom-call(s32[1]{0:T(128)} %bitcast.3.where_ref, bf16[128,2048]{1,0:T(8,128)(2,1)S(1)} %collective-permute-done.4.refs_0_, bf16[128,2048]{1,0:T(8,128)(2,1)S(1)} %copy-done.24, s32[3,2048,1024]{2,1,0:T(8,128)} %refs_4_.7, f32[3,1,1024]{2,1,0:T(1,128)S(1)} %reshape.36.refs_5_.refs_3_, ...), custom_call_target="tpu_custom_call" | custom-call | flops 1 | bytes 1 | tf_op jit(solution)/shard_map/pallas_call | solution.py:62
  51.0 2.8 %collective-permute-start.13 = (f16[256,768]{1,0:T(8,128)(2,1)S(1)}, f16[256,768]{1,0:T(8,128)(2,1)S(1)}, u32[]{:S(2)}, u32[]{:S(2)}) collective-permute-start(f16[256,768]{1,0:T(8,128)(2,1)S(1)} %select_convert_fusion.4), channel_id=1, source_target_pairs={{0,1},{1,0},{2,3},{3,2},{4,5},{5,4},{6,7},{7,6},{8,9},{9,8},{10,11... | collective-permute-start | bytes 1179656 | tf_op jit(solution)/shard_map/ppermute | solution.py:277
  54.4 4.9 %shard_map.83 = (f32[256,768]{1,0:T(8,128)S(1)}, f32[256,768]{1,0:T(8,128)S(1)}) custom-call(s32[1]{0:T(128)} %bitcast.1.where_ref, bf16[128,2048]{1,0:T(8,128)(2,1)S(1)} %collective-permute-done.refs_0_.refs_4_, bf16[128,2048]{1,0:T(8,128)(2,1)S(1)} %collective-permute-done.1.refs_1_, bf16[128,2048]{1,0:T(8,128)(2,1)S(1)} %collective-permute-done.2.refs_2_.refs_4_, ...), custom_call_target="tpu_custom_call" | custom-call | flops 1 | bytes 1 | tf_op jit(solution)/shard_map/pallas_call | solution.py:62
  59.3 2.8 %collective-permute-done.13 = f16[256,768]{1,0:T(8,128)(2,1)S(1)} collective-permute-done((f16[256,768]{1,0:T(8,128)(2,1)S(1)}, f16[256,768]{1,0:T(8,128)(2,1)S(1)}, u32[]{:S(2)}, u32[]{:S(2)}) %collective-permute-start.13) | collective-permute-done | bytes 393248 | tf_op jit(solution)/shard_map/ppermute | solution.py:277
  63.2 2.8 %collective-permute-start.15 = (f16[256,768]{1,0:T(8,128)(2,1)S(1)}, f16[256,768]{1,0:T(8,128)(2,1)S(1)}, u32[]{:S(2)}, u32[]{:S(2)}) collective-permute-start(f16[256,768]{1,0:T(8,128)(2,1)S(1)} %select_convert_fusion.3), channel_id=1, source_target_pairs={{0,1},{1,0},{2,3},{3,2},{4,5},{5,4},{6,7},{7,6},{8,9},{9,8},{10,11... | collective-permute-start | bytes 1179656 | tf_op jit(solution)/shard_map/ppermute | solution.py:277
  66.6 4.9 %shard_map.88 = (f32[256,768]{1,0:T(8,128)S(1)}, f32[256,768]{1,0:T(8,128)S(1)}) custom-call(s32[1]{0:T(128)} %bitcast.4.where_ref, bf16[128,2048]{1,0:T(8,128)(2,1)S(1)} %collective-permute-done.refs_0_.refs_4_, bf16[128,2048]{1,0:T(8,128)(2,1)S(1)} %collective-permute-done.1.refs_1_, bf16[128,2048]{1,0:T(8,128)(2,1)S(1)} %collective-permute-done.2.refs_2_.refs_4_, ...), custom_call_target="tpu_custom_call" | custom-call | flops 1 | bytes 1 | tf_op jit(solution)/shard_map/pallas_call | solution.py:62
  71.5 2.0 %collective-permute-done.15 = f16[256,768]{1,0:T(8,128)(2,1)S(1)} collective-permute-done((f16[256,768]{1,0:T(8,128)(2,1)S(1)}, f16[256,768]{1,0:T(8,128)(2,1)S(1)}, u32[]{:S(2)}, u32[]{:S(2)}) %collective-permute-start.15) | collective-permute-done | bytes 393248 | tf_op jit(solution)/shard_map/ppermute | solution.py:277
  75.4 3.3 %collective-permute-start.17 = (f16[256,768]{1,0:T(8,128)(2,1)}, f16[256,768]{1,0:T(8,128)(2,1)}, u32[]{:S(2)}, u32[]{:S(2)}) collective-permute-start(f16[256,768]{1,0:T(8,128)(2,1)} %select_convert_fusion.2), channel_id=1, source_target_pairs={{0,1},{1,0},{2,3},{3,2},{4,5},{5,4},{6,7},{7,6},{8,9},{9,8},{10,11... | collective-permute-start | bytes 1179656 | tf_op jit(solution)/shard_map/ppermute | solution.py:277
  79.4 5.0 %shard_map.82 = (f32[256,768]{1,0:T(8,128)S(1)}, f32[256,768]{1,0:T(8,128)S(1)}) custom-call(s32[1]{0:T(128)} %bitcast.where_ref, bf16[128,2048]{1,0:T(8,128)(2,1)S(1)} %collective-permute-done.refs_0_.refs_4_, bf16[128,2048]{1,0:T(8,128)(2,1)S(1)} %collective-permute-done.1.refs_1_, bf16[128,2048]{1,0:T(8,128)(2,1)S(1)} %collective-permute-done.2.refs_2_.refs_4_, ...), custom_call_target="tpu_custom_call" | custom-call | flops 1 | bytes 1 | tf_op jit(solution)/shard_map/pallas_call | solution.py:62
  84.5 2.0 %collective-permute-done.17 = f16[256,768]{1,0:T(8,128)(2,1)} collective-permute-done((f16[256,768]{1,0:T(8,128)(2,1)}, f16[256,768]{1,0:T(8,128)(2,1)}, u32[]{:S(2)}, u32[]{:S(2)}) %collective-permute-start.17) | collective-permute-done | bytes 393248 | tf_op jit(solution)/shard_map/ppermute | solution.py:277
  86.4 2.1 %clamp_convert_fusion.2 = (bf16[256,768]{1,0:T(8,128)(2,1)}, f16[256,768]{1,0:T(8,128)(2,1)}) fusion(f16[256,768]{1,0:T(8,128)(2,1)} %collective-permute-done.17, f32[256,768]{1,0:T(8,128)S(1)} %copy-done.20, f32[256,768]{1,0:T(8,128)S(1)} %copy-done.17, pred[]{:T(512)S(6)} %or.3), kind=kLoop, calls=%fused_computation.4 | loop fusion | flops 1376256 | bytes 2752513 | tf_op jit(solution)/shard_map/convert_element_type | solution.py:270
  89.4 1.8 collective-permute-start.19
  91.2 1.4 collective-permute-start.18
  92.6 4.9 %shard_map.89 = (f32[256,768]{1,0:T(8,128)S(1)}, f32[256,768]{1,0:T(8,128)S(1)}) custom-call(s32[1]{0:T(128)} %bitcast.5.where_ref, bf16[128,2048]{1,0:T(8,128)(2,1)S(1)} %collective-permute-done.refs_0_.refs_4_, bf16[128,2048]{1,0:T(8,128)(2,1)S(1)} %collective-permute-done.1.refs_1_, bf16[128,2048]{1,0:T(8,128)(2,1)S(1)} %collective-permute-done.2.refs_2_.refs_4_, ...), custom_call_target="tpu_custom_call" | custom-call | flops 1 | bytes 1 | tf_op jit(solution)/shard_map/pallas_call | solution.py:62
  99.2 2.2 %clamp_convert_fusion.5 = (bf16[256,768]{1,0:T(8,128)(2,1)}, f16[256,768]{1,0:T(8,128)(2,1)}) fusion(f16[256,768]{1,0:T(8,128)(2,1)} %copy-done.28, f32[256,768]{1,0:T(8,128)S(1)} %copy-done.22, f32[256,768]{1,0:T(8,128)S(1)} %get-tuple-element.64, pred[]{:T(512)S(6)} %or.3), kind=kLoop, calls=%fused_computation.7 | loop fusion | flops 1376256 | bytes 2752513 | tf_op jit(solution)/shard_map/convert_element_type | solution.py:270
  101.4 1.9 %select_convert_fusion = f16[256,768]{1,0:T(8,128)(2,1)} fusion(f32[256,768]{1,0:T(8,128)S(1)} %copy-done.3, f32[256,768]{1,0:T(8,128)S(1)} %get-tuple-element.41, f16[256,768]{1,0:T(8,128)(2,1)} %collective-permute-done.18, pred[]{:T(512)S(6)} %or.3), kind=kLoop, calls=%fused_computation.14 | loop fusion | flops 786432 | bytes 2359297 | tf_op jit(solution)/shard_map/convert_element_type | solution.py:258
  103.3 1.6 collective-permute-start.20
  104.8 3.8 %collective-permute-start.21 = (f16[256,768]{1,0:T(8,128)(2,1)}, f16[256,768]{1,0:T(8,128)(2,1)S(1)}, u32[]{:S(2)}, u32[]{:S(2)}) collective-permute-start(f16[256,768]{1,0:T(8,128)(2,1)} %select_convert_fusion), channel_id=1, source_target_pairs={{0,1},{1,0},{2,3},{3,2},{4,5},{5,4},{6,7},{7,6},{8,9},{9,8},{10,11... | collective-permute-start | bytes 1179656 | tf_op jit(solution)/shard_map/ppermute | solution.py:277
  108.6 1.8 %add_convert_fusion.1 = f16[256,768]{1,0:T(8,128)(2,1)} fusion(f32[256,768]{1,0:T(8,128)S(1)} %copy-done.7, f16[256,768]{1,0:T(8,128)(2,1)} %collective-permute-done.20), kind=kLoop, calls=%fused_computation.12 | loop fusion | flops 589824 | bytes 1572864 | tf_op jit(solution)/shard_map/convert_element_type | solution.py:258
  110.5 4.1 %collective-permute-done.21 = f16[256,768]{1,0:T(8,128)(2,1)S(1)} collective-permute-done((f16[256,768]{1,0:T(8,128)(2,1)}, f16[256,768]{1,0:T(8,128)(2,1)S(1)}, u32[]{:S(2)}, u32[]{:S(2)}) %collective-permute-start.21) | collective-permute-done | bytes 393248 | tf_op jit(solution)/shard_map/ppermute | solution.py:277
  115.5 1.4 collective-permute-start.22
  117.1 5.8 %collective-permute-start.26 = (f16[256,768]{1,0:T(8,128)(2,1)}, f16[256,768]{1,0:T(8,128)(2,1)}, u32[]{:S(2)}, u32[]{:S(2)}) collective-permute-start(f16[256,768]{1,0:T(8,128)(2,1)} %add_convert_fusion.1), channel_id=1, source_target_pairs={{0,1},{1,0},{2,3},{3,2},{4,5},{5,4},{6,7},{7,6},{8,9},{9,8},{10,11... | collective-permute-start | bytes 1179656 | tf_op jit(solution)/shard_map/ppermute | solution.py:277
  122.8 1.1 pad_maximum_fusion.query_code_ref.key_code_ref.value_code_ref
  124.0 7.6 %shard_map.90 = bf16[8,128,256]{2,1,0:T(8,128)(2,1)S(1)} custom-call(s32[2]{0:T(128)S(1)} %pad_add_fusion.place_ref, bf16[1024,768]{1,0:T(8,128)(2,1)S(1)} %pad_maximum_fusion.query_code_ref.key_code_ref.value_code_ref, bf16[1024,768]{1,0:T(8,128)(2,1)S(1)} %pad_maximum_fusion.query_code_ref.key_code_ref.value_code_ref, ...), custom_call_target="tpu_custom_call" | custom-call | flops 1 | bytes 1 | tf_op jit(solution)/shard_map/pallas_call | solution.py:157
  131.6 1.9 %add_convert_fusion = f16[256,768]{1,0:T(8,128)(2,1)} fusion(f32[256,768]{1,0:T(8,128)S(1)} %copy-done.3, f16[256,768]{1,0:T(8,128)(2,1)} %collective-permute-done.22), kind=kLoop, calls=%fused_computation.10 | loop fusion | flops 589824 | bytes 1572864 | tf_op jit(solution)/shard_map/convert_element_type | solution.py:258
  134.4 2.0 %collective-permute-start.23 = (bf16[8,32,256]{2,1,0:T(8,128)(2,1)}, bf16[8,32,256]{2,1,0:T(8,128)(2,1)S(1)}, u32[]{:S(2)}, u32[]{:S(2)}) collective-permute-start(bf16[8,32,256]{2,1,0:T(8,128)(2,1)} %get-tuple-element.91), channel_id=1, source_target_pairs={{0,1},{1,0},{2,3},{3,2},{4,5},{5,4},{6,7},{7,6},{8,9},{9,8},{10,11... | collective-permute-start | bytes 393224 | tf_op jit(solution)/shard_map/ppermute | solution.py:303
  137.1 3.5 %collective-permute-start.25 = (bf16[8,32,256]{2,1,0:T(8,128)(2,1)}, bf16[8,32,256]{2,1,0:T(8,128)(2,1)}, u32[]{:S(2)}, u32[]{:S(2)}) collective-permute-start(bf16[8,32,256]{2,1,0:T(8,128)(2,1)} %get-tuple-element.89), channel_id=1, source_target_pairs={{0,3},{3,0},{4,7},{7,4},{8,11},{11,8},{12,15},{15,12},{16,19},{19,... | collective-permute-start | bytes 393224 | tf_op jit(solution)/shard_map/ppermute | solution.py:305
  140.7 1.1 clamp_convert_fusion.1
  141.8 3.7 %collective-permute-done.27 = f16[256,768]{1,0:T(8,128)(2,1)S(1)} collective-permute-done((f16[256,768]{1,0:T(8,128)(2,1)}, f16[256,768]{1,0:T(8,128)(2,1)S(1)}, u32[]{:S(2)}, u32[]{:S(2)}) %collective-permute-start.27) | collective-permute-done | bytes 393248 | tf_op jit(solution)/shard_map/ppermute | solution.py:277
  145.6 1.2 pad_maximum_fusion.1.query_code_ref.key_code_ref.value_code_ref
  146.8 7.6 %shard_map.91 = bf16[8,128,256]{2,1,0:T(8,128)(2,1)S(1)} custom-call(s32[2]{0:T(128)S(1)} %pad_add_fusion.1.place_ref, bf16[1024,768]{1,0:T(8,128)(2,1)S(1)} %pad_maximum_fusion.1.query_code_ref.key_code_ref.value_code_ref, bf16[1024,768]{1,0:T(8,128)(2,1)S(1)} %pad_maximum_fusion.1.query_code_ref.key_code_ref.value_code_ref, ...), custom_call_target="tpu_custom_call" | custom-call | flops 1 | bytes 1 | tf_op jit(solution)/shard_map/pallas_call | solution.py:157
  154.5 3.2 %collective-permute-start.29 = (bf16[8,32,256]{2,1,0:T(8,128)(2,1)S(1)}, bf16[8,32,256]{2,1,0:T(8,128)(2,1)S(1)}, u32[]{:S(2)}, u32[]{:S(2)}) collective-permute-start(bf16[8,32,256]{2,1,0:T(8,128)(2,1)S(1)} %get-tuple-element.93), channel_id=1, source_target_pairs={{0,2},{2,0},{1,3},{3,1},{4,6},{6,4},{5,7},{7,5},{8,10},{10,8},{9,1... | collective-permute-start | bytes 393224 | tf_op jit(solution)/shard_map/ppermute | solution.py:304
  157.7 3.1 %collective-permute-start.30 = (bf16[8,32,256]{2,1,0:T(8,128)(2,1)S(1)}, bf16[8,32,256]{2,1,0:T(8,128)(2,1)S(1)}, u32[]{:S(2)}, u32[]{:S(2)}) collective-permute-start(bf16[8,32,256]{2,1,0:T(8,128)(2,1)S(1)} %get-tuple-element.92), channel_id=1, source_target_pairs={{0,3},{3,0},{4,7},{7,4},{8,11},{11,8},{12,15},{15,12},{16,19},{19,... | collective-permute-start | bytes 393224 | tf_op jit(solution)/shard_map/ppermute | solution.py:305
  162.1 4.3 %collective-permute-done.30 = bf16[8,32,256]{2,1,0:T(8,128)(2,1)S(1)} collective-permute-done((bf16[8,32,256]{2,1,0:T(8,128)(2,1)S(1)}, bf16[8,32,256]{2,1,0:T(8,128)(2,1)S(1)}, u32[]{:S(2)}, u32[]{:S(2)}) %collective-permute-start.30) | collective-permute-done | bytes 131104 | tf_op jit(solution)/shard_map/ppermute | solution.py:305
  166.5 12.2 %all_to_all.5 = bf16[8,32,1024]{2,1,0:T(8,128)(2,1)S(1)} all-to-all(bf16[8,32,1024]{2,1,0:T(8,128)(2,1)S(1)} %pad_maximum_fusion.2), channel_id=1, replica_groups=mesh['seq'=8,'tp'=4] {'seq'}, dimensions={0} | all-to-all | bytes 1048576 | tf_op jit(solution)/shard_map/all_to_all | solution.py:313
  (125 shorter events, 21.2 us)
Async XLA Ops:
  1.3 3.9 %collective-permute-start.6 = (bf16[128,2048]{1,0:T(8,128)(2,1)S(1)}, bf16[128,2048]{1,0:T(8,128)(2,1)S(1)}, u32[]{:S(2)}, u32[]{:S(2)}) collective-permute-start(bf16[128,2048]{1,0:T(8,128)(2,1)S(1)} %convert_element_type.147.refs_0_), channel_id=1, source_target_pairs={{0,4},{4,0},{8,12},{12,8},{16,20},{20,16},{24,28},{28,24},{1,5},{5... | collective-permute-start | bytes 1572872 | tf_op jit(solution)/shard_map/ppermute | solution.py:202
  1.8 20.6 %collective-permute-start.4 = (bf16[128,2048]{1,0:T(8,128)(2,1)S(1)}, bf16[128,2048]{1,0:T(8,128)(2,1)S(1)}, u32[]{:S(2)}, u32[]{:S(2)}) collective-permute-start(bf16[128,2048]{1,0:T(8,128)(2,1)S(1)} %convert_element_type.147.refs_0_), channel_id=1, source_target_pairs={{0,8},{4,12},{8,0},{12,4},{16,24},{20,28},{24,16},{28,20},{1,9},{5... | collective-permute-start | bytes 1572872 | tf_op jit(solution)/shard_map/ppermute | solution.py:202
  12.3 11.4 %collective-permute-start.7 = (f16[256,768]{1,0:T(8,128)(2,1)}, f16[256,768]{1,0:T(8,128)(2,1)S(1)}, u32[]{:S(2)}, u32[]{:S(2)}) collective-permute-start(f16[256,768]{1,0:T(8,128)(2,1)} %convert_element_type.151), channel_id=1, source_target_pairs={{0,1},{1,0},{2,3},{3,2},{4,5},{5,4},{6,7},{7,6},{8,9},{9,8},{10,11... | collective-permute-start | bytes 1179656 | tf_op jit(solution)/shard_map/ppermute | solution.py:277
  13.9 17.8 %collective-permute-start = (bf16[128,2048]{1,0:T(8,128)(2,1)S(1)}, bf16[128,2048]{1,0:T(8,128)(2,1)S(1)}, u32[]{:S(2)}, u32[]{:S(2)}) collective-permute-start(bf16[128,2048]{1,0:T(8,128)(2,1)S(1)} %convert_element_type.147.refs_0_), channel_id=1, source_target_pairs={{0,16},{4,20},{8,24},{12,28},{16,0},{20,4},{24,8},{28,12},{1,17},{... | collective-permute-start | bytes 1572872 | tf_op jit(solution)/shard_map/ppermute | solution.py:202
  21.5 8.2 %copy-start.14 = (f32[256,768]{1,0:T(8,128)}, f32[256,768]{1,0:T(8,128)S(1)}, u32[]{:S(2)}) copy-start(f32[256,768]{1,0:T(8,128)S(1)} %get-tuple-element.47) | copy-start | bytes 2359300
  22.4 9.3 %collective-permute-start.5 = (bf16[128,2048]{1,0:T(8,128)(2,1)S(1)}, bf16[128,2048]{1,0:T(8,128)(2,1)S(1)}, u32[]{:S(2)}, u32[]{:S(2)}) collective-permute-start(bf16[128,2048]{1,0:T(8,128)(2,1)S(1)} %collective-permute-done.4.refs_0_), channel_id=1, source_target_pairs={{0,4},{4,0},{8,12},{12,8},{16,20},{20,16},{24,28},{28,24},{1,5},{5... | collective-permute-start | bytes 1572872 | tf_op jit(solution)/shard_map/ppermute | solution.py:202
  24.6 13.4 %collective-permute-start.8 = (f16[256,768]{1,0:T(8,128)(2,1)}, f16[256,768]{1,0:T(8,128)(2,1)}, u32[]{:S(2)}, u32[]{:S(2)}) collective-permute-start(f16[256,768]{1,0:T(8,128)(2,1)} %add_convert_fusion.3), channel_id=1, source_target_pairs={{1,2},{2,1},{5,6},{6,5},{9,10},{10,9},{13,14},{14,13},{17,18},{18,... | collective-permute-start | bytes 1179656 | tf_op jit(solution)/shard_map/ppermute | solution.py:279
  26.0 13.2 %collective-permute-start.9 = (f16[256,768]{1,0:T(8,128)(2,1)}, f16[256,768]{1,0:T(8,128)(2,1)}, u32[]{:S(2)}, u32[]{:S(2)}) collective-permute-start(f16[256,768]{1,0:T(8,128)(2,1)} %convert_element_type.150), channel_id=1, source_target_pairs={{0,1},{1,0},{2,3},{3,2},{4,5},{5,4},{6,7},{7,6},{8,9},{9,8},{10,11... | collective-permute-start | bytes 1179656 | tf_op jit(solution)/shard_map/ppermute | solution.py:277
  29.7 13.5 %collective-permute-start.2 = (bf16[128,2048]{1,0:T(8,128)(2,1)S(1)}, bf16[128,2048]{1,0:T(8,128)(2,1)S(1)}, u32[]{:S(2)}, u32[]{:S(2)}) collective-permute-start(bf16[128,2048]{1,0:T(8,128)(2,1)S(1)} %convert_element_type.147.refs_0_), channel_id=1, source_target_pairs={{0,24},{4,28},{8,16},{12,20},{16,8},{20,12},{24,0},{28,4},{1,25},{... | collective-permute-start | bytes 1572872 | tf_op jit(solution)/shard_map/ppermute | solution.py:202
  31.7 7.6 %copy-start.13 = (f32[256,768]{1,0:T(8,128)S(1)}, f32[256,768]{1,0:T(8,128)}, u32[]{:S(2)}) copy-start(f32[256,768]{1,0:T(8,128)} %copy-done.12) | copy-start | bytes 2359300
  40.3 9.6 %copy-start.15 = (f32[256,768]{1,0:T(8,128)S(1)}, f32[256,768]{1,0:T(8,128)}, u32[]{:S(2)}) copy-start(f32[256,768]{1,0:T(8,128)} %copy-done.14) | copy-start | bytes 2359300
  40.3 9.6 %collective-permute-start.11 = (f16[256,768]{1,0:T(8,128)(2,1)S(1)}, f16[256,768]{1,0:T(8,128)(2,1)S(1)}, u32[]{:S(2)}, u32[]{:S(2)}) collective-permute-start(f16[256,768]{1,0:T(8,128)(2,1)S(1)} %select_convert_fusion.5), channel_id=1, source_target_pairs={{0,1},{1,0},{2,3},{3,2},{4,5},{5,4},{6,7},{7,6},{8,9},{9,8},{10,11... | collective-permute-start | bytes 1179656 | tf_op jit(solution)/shard_map/ppermute | solution.py:277
  41.3 9.6 %collective-permute-start.10 = (f16[256,768]{1,0:T(8,128)(2,1)S(1)}, f16[256,768]{1,0:T(8,128)(2,1)S(1)}, u32[]{:S(2)}, u32[]{:S(2)}) collective-permute-start(f16[256,768]{1,0:T(8,128)(2,1)S(1)} %add_convert_fusion.2), channel_id=1, source_target_pairs={{1,2},{2,1},{5,6},{6,5},{9,10},{10,9},{13,14},{14,13},{17,18},{18,... | collective-permute-start | bytes 1179656 | tf_op jit(solution)/shard_map/ppermute | solution.py:279
  42.0 12.4 %collective-permute-start.1 = (bf16[128,2048]{1,0:T(8,128)(2,1)S(1)}, bf16[128,2048]{1,0:T(8,128)(2,1)S(1)}, u32[]{:S(2)}, u32[]{:S(2)}) collective-permute-start(bf16[128,2048]{1,0:T(8,128)(2,1)S(1)} %collective-permute-done.refs_0_.refs_4_), channel_id=1, source_target_pairs={{0,4},{4,0},{8,12},{12,8},{16,20},{20,16},{24,28},{28,24},{1,5},{5... | collective-permute-start | bytes 1572872 | tf_op jit(solution)/shard_map/ppermute | solution.py:202
  43.2 11.2 %collective-permute-start.3 = (bf16[128,2048]{1,0:T(8,128)(2,1)S(1)}, bf16[128,2048]{1,0:T(8,128)(2,1)S(1)}, u32[]{:S(2)}, u32[]{:S(2)}) collective-permute-start(bf16[128,2048]{1,0:T(8,128)(2,1)S(1)} %collective-permute-done.2.refs_2_.refs_4_), channel_id=1, source_target_pairs={{0,4},{4,0},{8,12},{12,8},{16,20},{20,16},{24,28},{28,24},{1,5},{5... | collective-permute-start | bytes 1572872 | tf_op jit(solution)/shard_map/ppermute | solution.py:202
  49.3 12.8 %copy-start.19 = (f32[256,768]{1,0:T(8,128)}, f32[256,768]{1,0:T(8,128)S(1)}, u32[]{:S(2)}) copy-start(f32[256,768]{1,0:T(8,128)S(1)} %get-tuple-element.55) | copy-start | bytes 2359300
  51.0 11.1 %collective-permute-start.13 = (f16[256,768]{1,0:T(8,128)(2,1)S(1)}, f16[256,768]{1,0:T(8,128)(2,1)S(1)}, u32[]{:S(2)}, u32[]{:S(2)}) collective-permute-start(f16[256,768]{1,0:T(8,128)(2,1)S(1)} %select_convert_fusion.4), channel_id=1, source_target_pairs={{0,1},{1,0},{2,3},{3,2},{4,5},{5,4},{6,7},{7,6},{8,9},{9,8},{10,11... | collective-permute-start | bytes 1179656 | tf_op jit(solution)/shard_map/ppermute | solution.py:277
  53.7 9.3 %collective-permute-start.12 = (f16[256,768]{1,0:T(8,128)(2,1)S(1)}, f16[256,768]{1,0:T(8,128)(2,1)S(1)}, u32[]{:S(2)}, u32[]{:S(2)}) collective-permute-start(f16[256,768]{1,0:T(8,128)(2,1)S(1)} %get-tuple-element.54), channel_id=1, source_target_pairs={{1,2},{2,1},{5,6},{6,5},{9,10},{10,9},{13,14},{14,13},{17,18},{18,... | collective-permute-start | bytes 1179656 | tf_op jit(solution)/shard_map/ppermute | solution.py:279
  63.2 10.3 %collective-permute-start.15 = (f16[256,768]{1,0:T(8,128)(2,1)S(1)}, f16[256,768]{1,0:T(8,128)(2,1)S(1)}, u32[]{:S(2)}, u32[]{:S(2)}) collective-permute-start(f16[256,768]{1,0:T(8,128)(2,1)S(1)} %select_convert_fusion.3), channel_id=1, source_target_pairs={{0,1},{1,0},{2,3},{3,2},{4,5},{5,4},{6,7},{7,6},{8,9},{9,8},{10,11... | collective-permute-start | bytes 1179656 | tf_op jit(solution)/shard_map/ppermute | solution.py:277
  65.9 8.6 %collective-permute-start.14 = (f16[256,768]{1,0:T(8,128)(2,1)S(1)}, f16[256,768]{1,0:T(8,128)(2,1)S(1)}, u32[]{:S(2)}, u32[]{:S(2)}) collective-permute-start(f16[256,768]{1,0:T(8,128)(2,1)S(1)} %get-tuple-element.57), channel_id=1, source_target_pairs={{1,2},{2,1},{5,6},{6,5},{9,10},{10,9},{13,14},{14,13},{17,18},{18,... | collective-permute-start | bytes 1179656 | tf_op jit(solution)/shard_map/ppermute | solution.py:279
  75.4 11.0 %collective-permute-start.17 = (f16[256,768]{1,0:T(8,128)(2,1)}, f16[256,768]{1,0:T(8,128)(2,1)}, u32[]{:S(2)}, u32[]{:S(2)}) collective-permute-start(f16[256,768]{1,0:T(8,128)(2,1)} %select_convert_fusion.2), channel_id=1, source_target_pairs={{0,1},{1,0},{2,3},{3,2},{4,5},{5,4},{6,7},{7,6},{8,9},{9,8},{10,11... | collective-permute-start | bytes 1179656 | tf_op jit(solution)/shard_map/ppermute | solution.py:277
  78.7 9.8 %collective-permute-start.16 = (f16[256,768]{1,0:T(8,128)(2,1)}, f16[256,768]{1,0:T(8,128)(2,1)S(1)}, u32[]{:S(2)}, u32[]{:S(2)}) collective-permute-start(f16[256,768]{1,0:T(8,128)(2,1)} %get-tuple-element.60), channel_id=1, source_target_pairs={{1,2},{2,1},{5,6},{6,5},{9,10},{10,9},{13,14},{14,13},{17,18},{18,... | collective-permute-start | bytes 1179656 | tf_op jit(solution)/shard_map/ppermute | solution.py:279
  79.4 7.0 %copy-start.17 = (f32[256,768]{1,0:T(8,128)S(1)}, f32[256,768]{1,0:T(8,128)}, u32[]{:S(2)}) copy-start(f32[256,768]{1,0:T(8,128)} %copy-done.16) | copy-start | bytes 2359300
  79.4 7.0 %copy-start.20 = (f32[256,768]{1,0:T(8,128)S(1)}, f32[256,768]{1,0:T(8,128)}, u32[]{:S(2)}) copy-start(f32[256,768]{1,0:T(8,128)} %copy-done.19) | copy-start | bytes 2359300
  89.4 9.0 %collective-permute-start.19 = (f16[256,768]{1,0:T(8,128)(2,1)}, f16[256,768]{1,0:T(8,128)(2,1)S(1)}, u32[]{:S(2)}, u32[]{:S(2)}) collective-permute-start(f16[256,768]{1,0:T(8,128)(2,1)} %select_convert_fusion.1), channel_id=1, source_target_pairs={{0,1},{1,0},{2,3},{3,2},{4,5},{5,4},{6,7},{7,6},{8,9},{9,8},{10,11... | collective-permute-start | bytes 1179656 | tf_op jit(solution)/shard_map/ppermute | solution.py:277
  91.2 10.1 %collective-permute-start.18 = (f16[256,768]{1,0:T(8,128)(2,1)}, f16[256,768]{1,0:T(8,128)(2,1)}, u32[]{:S(2)}, u32[]{:S(2)}) collective-permute-start(f16[256,768]{1,0:T(8,128)(2,1)} %get-tuple-element.63), channel_id=1, source_target_pairs={{1,2},{2,1},{5,6},{6,5},{9,10},{10,9},{13,14},{14,13},{17,18},{18,... | collective-permute-start | bytes 1179656 | tf_op jit(solution)/shard_map/ppermute | solution.py:279
  92.6 6.6 %copy-start.22 = (f32[256,768]{1,0:T(8,128)S(1)}, f32[256,768]{1,0:T(8,128)}, u32[]{:S(2)}) copy-start(f32[256,768]{1,0:T(8,128)} %copy-done.21) | copy-start | bytes 2359300
  97.6 11.1 %copy-start.31 = (s32[3,3,1024]{2,1,0:T(4,128)S(1)}, s32[3,3,1024]{2,1,0:T(4,128)}, u32[]{:S(2)}) copy-start(s32[3,3,1024]{2,1,0:T(4,128)} %param.12) | copy-start | bytes 110596
  97.6 11.1 %copy-start.7 = (f32[256,768]{1,0:T(8,128)S(1)}, f32[256,768]{1,0:T(8,128)}, u32[]{:S(2)}) copy-start(f32[256,768]{1,0:T(8,128)} %copy-done.6) | copy-start | bytes 2359300
  99.2 15.4 %copy-start.18 = (f32[256,768]{1,0:T(8,128)S(1)}, f32[256,768]{1,0:T(8,128)}, u32[]{:S(2)}) copy-start(f32[256,768]{1,0:T(8,128)} %copy-done.16) | copy-start | bytes 2359300
  101.3 15.7 %copy-start.29 = (f32[16,1024]{1,0:T(8,128)S(1)}, f32[16,1024]{1,0:T(8,128)}, u32[]{:S(2)}) copy-start(f32[16,1024]{1,0:T(8,128)} %param.14) | copy-start | bytes 196612
  101.3 15.7 %copy-start.30 = (s32[16,1024]{1,0:T(8,128)S(1)}, s32[16,1024]{1,0:T(8,128)}, u32[]{:S(2)}) copy-start(s32[16,1024]{1,0:T(8,128)} %param.13) | copy-start | bytes 196612
  103.3 19.6 %copy-start.26 = (bf16[256,768]{1,0:T(8,128)(2,1)S(1)}, bf16[256,768]{1,0:T(8,128)(2,1)}, u32[]{:S(2)}) copy-start(bf16[256,768]{1,0:T(8,128)(2,1)} %get-tuple-element.77) | copy-start | bytes 1179652
  103.3 19.6 %copy-start.27 = (bf16[256,768]{1,0:T(8,128)(2,1)S(1)}, bf16[256,768]{1,0:T(8,128)(2,1)}, u32[]{:S(2)}) copy-start(bf16[256,768]{1,0:T(8,128)(2,1)} %get-tuple-element.79) | copy-start | bytes 1179652
  103.3 5.4 %collective-permute-start.20 = (f16[256,768]{1,0:T(8,128)(2,1)}, f16[256,768]{1,0:T(8,128)(2,1)}, u32[]{:S(2)}, u32[]{:S(2)}) collective-permute-start(f16[256,768]{1,0:T(8,128)(2,1)} %get-tuple-element.66), channel_id=1, source_target_pairs={{1,2},{2,1},{5,6},{6,5},{9,10},{10,9},{13,14},{14,13},{17,18},{18,... | collective-permute-start | bytes 1179656 | tf_op jit(solution)/shard_map/ppermute | solution.py:279
  104.8 9.7 %collective-permute-start.21 = (f16[256,768]{1,0:T(8,128)(2,1)}, f16[256,768]{1,0:T(8,128)(2,1)S(1)}, u32[]{:S(2)}, u32[]{:S(2)}) collective-permute-start(f16[256,768]{1,0:T(8,128)(2,1)} %select_convert_fusion), channel_id=1, source_target_pairs={{0,1},{1,0},{2,3},{3,2},{4,5},{5,4},{6,7},{7,6},{8,9},{9,8},{10,11... | collective-permute-start | bytes 1179656 | tf_op jit(solution)/shard_map/ppermute | solution.py:277
  110.5 13.5 %copy-start.25 = (f32[1024]{0:T(1024)S(1)}, f32[1024]{0:T(1024)}, u32[]{:S(2)}) copy-start(f32[1024]{0:T(1024)} %param.15) | copy-start | bytes 12292
  115.5 16.1 %collective-permute-start.22 = (f16[256,768]{1,0:T(8,128)(2,1)}, f16[256,768]{1,0:T(8,128)(2,1)}, u32[]{:S(2)}, u32[]{:S(2)}) collective-permute-start(f16[256,768]{1,0:T(8,128)(2,1)} %get-tuple-element.69), channel_id=1, source_target_pairs={{1,2},{2,1},{5,6},{6,5},{9,10},{10,9},{13,14},{14,13},{17,18},{18,... | collective-permute-start | bytes 1179656 | tf_op jit(solution)/shard_map/ppermute | solution.py:279
  117.1 23.6 %collective-permute-start.26 = (f16[256,768]{1,0:T(8,128)(2,1)}, f16[256,768]{1,0:T(8,128)(2,1)}, u32[]{:S(2)}, u32[]{:S(2)}) collective-permute-start(f16[256,768]{1,0:T(8,128)(2,1)} %add_convert_fusion.1), channel_id=1, source_target_pairs={{0,1},{1,0},{2,3},{3,2},{4,5},{5,4},{6,7},{7,6},{8,9},{9,8},{10,11... | collective-permute-start | bytes 1179656 | tf_op jit(solution)/shard_map/ppermute | solution.py:277
  124.0 16.7 %copy-start.11 = (f32[256,768]{1,0:T(8,128)S(1)}, f32[256,768]{1,0:T(8,128)}, u32[]{:S(2)}) copy-start(f32[256,768]{1,0:T(8,128)} %copy-done.10) | copy-start | bytes 2359300
  131.6 13.9 %copy-start.9 = (f32[256,768]{1,0:T(8,128)S(1)}, f32[256,768]{1,0:T(8,128)}, u32[]{:S(2)}) copy-start(f32[256,768]{1,0:T(8,128)} %copy-done.8) | copy-start | bytes 2359300
  133.5 12.0 %collective-permute-start.27 = (f16[256,768]{1,0:T(8,128)(2,1)}, f16[256,768]{1,0:T(8,128)(2,1)S(1)}, u32[]{:S(2)}, u32[]{:S(2)}) collective-permute-start(f16[256,768]{1,0:T(8,128)(2,1)} %add_convert_fusion), channel_id=1, source_target_pairs={{0,1},{1,0},{2,3},{3,2},{4,5},{5,4},{6,7},{7,6},{8,9},{9,8},{10,11... | collective-permute-start | bytes 1179656 | tf_op jit(solution)/shard_map/ppermute | solution.py:277
  134.4 23.4 %collective-permute-start.23 = (bf16[8,32,256]{2,1,0:T(8,128)(2,1)}, bf16[8,32,256]{2,1,0:T(8,128)(2,1)S(1)}, u32[]{:S(2)}, u32[]{:S(2)}) collective-permute-start(bf16[8,32,256]{2,1,0:T(8,128)(2,1)} %get-tuple-element.91), channel_id=1, source_target_pairs={{0,1},{1,0},{2,3},{3,2},{4,5},{5,4},{6,7},{7,6},{8,9},{9,8},{10,11... | collective-permute-start | bytes 393224 | tf_op jit(solution)/shard_map/ppermute | solution.py:303
  136.4 24.5 %collective-permute-start.24 = (bf16[8,32,256]{2,1,0:T(8,128)(2,1)}, bf16[8,32,256]{2,1,0:T(8,128)(2,1)S(1)}, u32[]{:S(2)}, u32[]{:S(2)}) collective-permute-start(bf16[8,32,256]{2,1,0:T(8,128)(2,1)} %get-tuple-element.90), channel_id=1, source_target_pairs={{0,2},{2,0},{1,3},{3,1},{4,6},{6,4},{5,7},{7,5},{8,10},{10,8},{9,1... | collective-permute-start | bytes 393224 | tf_op jit(solution)/shard_map/ppermute | solution.py:304
  137.1 23.7 %collective-permute-start.25 = (bf16[8,32,256]{2,1,0:T(8,128)(2,1)}, bf16[8,32,256]{2,1,0:T(8,128)(2,1)}, u32[]{:S(2)}, u32[]{:S(2)}) collective-permute-start(bf16[8,32,256]{2,1,0:T(8,128)(2,1)} %get-tuple-element.89), channel_id=1, source_target_pairs={{0,3},{3,0},{4,7},{7,4},{8,11},{11,8},{12,15},{15,12},{16,19},{19,... | collective-permute-start | bytes 393224 | tf_op jit(solution)/shard_map/ppermute | solution.py:305
  154.5 7.3 %collective-permute-start.28 = (bf16[8,32,256]{2,1,0:T(8,128)(2,1)S(1)}, bf16[8,32,256]{2,1,0:T(8,128)(2,1)S(1)}, u32[]{:S(2)}, u32[]{:S(2)}) collective-permute-start(bf16[8,32,256]{2,1,0:T(8,128)(2,1)S(1)} %get-tuple-element.94), channel_id=1, source_target_pairs={{0,1},{1,0},{2,3},{3,2},{4,5},{5,4},{6,7},{7,6},{8,9},{9,8},{10,11... | collective-permute-start | bytes 393224 | tf_op jit(solution)/shard_map/ppermute | solution.py:303
  154.5 7.6 %collective-permute-start.29 = (bf16[8,32,256]{2,1,0:T(8,128)(2,1)S(1)}, bf16[8,32,256]{2,1,0:T(8,128)(2,1)S(1)}, u32[]{:S(2)}, u32[]{:S(2)}) collective-permute-start(bf16[8,32,256]{2,1,0:T(8,128)(2,1)S(1)} %get-tuple-element.93), channel_id=1, source_target_pairs={{0,2},{2,0},{1,3},{3,1},{4,6},{6,4},{5,7},{7,5},{8,10},{10,8},{9,1... | collective-permute-start | bytes 393224 | tf_op jit(solution)/shard_map/ppermute | solution.py:304
  157.7 8.6 %collective-permute-start.30 = (bf16[8,32,256]{2,1,0:T(8,128)(2,1)S(1)}, bf16[8,32,256]{2,1,0:T(8,128)(2,1)S(1)}, u32[]{:S(2)}, u32[]{:S(2)}) collective-permute-start(bf16[8,32,256]{2,1,0:T(8,128)(2,1)S(1)} %get-tuple-element.92), channel_id=1, source_target_pairs={{0,3},{3,0},{4,7},{7,4},{8,11},{11,8},{12,15},{15,12},{16,19},{19,... | collective-permute-start | bytes 393224 | tf_op jit(solution)/shard_map/ppermute | solution.py:305
  (15 other events, 65.1 us)

commit v3 on v2

--- a/solution.py
+++ b/solution.py
@@ -49,8 +49,9 @@
         columns = slice(g * width, (g + 1) * width)
         weights = w_ref[0, :, columns].astype(jnp.float32).astype(jnp.bfloat16)
         sums = jnp.dot(rows_ref[...], weights, preferred_element_type=jnp.float32) * scale_ref[0, :, columns]
+        start = pl.multiple_of(pl.program_id(0) * width, width)
         for i, out_ref in enumerate(out_refs[g::groups]):
-            out_ref[...] = sums[i * count : (i + 1) * count]
+            out_ref[:, pl.ds(start, width)] = sums[i * count : (i + 1) * count]
 
 
 def project(blocks, w_codes, scale, block, groups, width, token):
@@ -70,11 +71,11 @@
                 pl.BlockSpec((1, 1, columns), lambda k, where: (k, 0, where[0])),
                 ANYWHERE,
             ],
-            out_specs=[pl.BlockSpec((2 * size, width), lambda k, where: (0, k))] * outs,
+            out_specs=[pl.BlockSpec(memory_space=pltpu.VMEM)] * outs,
             scratch_shapes=[pltpu.VMEM((count, features), jnp.bfloat16)],
         ),
-        out_shape=[jax.ShapeDtypeStruct((2 * size, kinds * width), jnp.float32)] * outs,
-        compiler_params=pltpu.CompilerParams(vmem_limit_bytes=48 * 2**20),
+        out_shape=[pltpu.VMEM((2 * size, kinds * width), jnp.float32)] * outs,
+        compiler_params=pltpu.CompilerParams(vmem_limit_bytes=24 * 2**20),
         cost_estimate=pl.CostEstimate(flops=1, bytes_accessed=1, transcendentals=0),
     )(
         block.reshape(1).astype(jnp.int32),
@@ -85,23 +86,29 @@
     )
 
 
-def conv_kernel(blocks, block_rows, shorts, states, place_ref, query_code_ref, key_code_ref, value_code_ref, taps_ref,
-                decay_ref, decay_block_ref, coeff_ref, skip_ref, out_ref, pad_ref, query_ref, drive_ref, mixed_ref,
-                sums_ref):
+def conv_kernel(blocks, block_rows, shorts, states, place_ref, *refs):
+    kinds = 3
+    code_refs = refs[: kinds * blocks // 2]
+    taps_ref, decay_ref, decay_block_ref, coeff_ref, skip_ref, out_ref = refs[len(code_refs) : len(code_refs) + 6]
+    pad_ref, query_ref, drive_ref, mixed_ref, sums_ref, tails_ref = refs[len(code_refs) + 6 :]
     sublanes = 8
     folds = blocks // sublanes
     place = place_ref[0]
     halo = 8
     for r in range(blocks):
+        for k in range(kinds):
+            code_ref = code_refs[r // 2 * kinds + k]
+            last = code_ref[pl.ds(r % 2 * block_rows + block_rows - 16, 16), :].astype(jnp.float32)
+            tails_ref[r * kinds + k] = last[16 - halo :, :]
+    for r in range(blocks):
         absolute = lax.bitwise_xor(jnp.int32(r), place)
         before = lax.bitwise_xor(jnp.maximum(absolute - 1, 0), place)
         has_before = jnp.where(absolute > 0, 1.0 / 64.0, 0.0)
         featured = []
-        for k, coded_ref in enumerate((query_code_ref, key_code_ref, value_code_ref)):
-            tail_start = pl.multiple_of(before * block_rows + block_rows - 16, 16)
-            tail = coded_ref[pl.ds(tail_start, 16), :].astype(jnp.float32) * has_before
-            pad_ref[k, pl.ds(0, halo), :] = tail[16 - halo:, :]
-            now = coded_ref[pl.ds(r * block_rows, block_rows), :].astype(jnp.float32) * (1.0 / 64.0)
+        for k in range(kinds):
+            code_ref = code_refs[r // 2 * kinds + k]
+            pad_ref[k, pl.ds(0, halo), :] = tails_ref[before * kinds + k] * has_before
+            now = code_ref[pl.ds(r % 2 * block_rows, block_rows), :].astype(jnp.float32) * (1.0 / 64.0)
             pad_ref[k, pl.ds(halo, block_rows), :] = now
             total = taps_ref[0, pl.ds(k, 1), :] * now
             for lag in range(1, shorts):
@@ -118,7 +125,7 @@
             return tuple(held[n] * decays[n] + now for n in range(states))
 
         zero = jnp.zeros((sublanes, LANES), jnp.float32)
-        held = lax.fori_loop(0, block_rows, local, (zero,) * states, unroll=4)
+        held = lax.fori_loop(0, block_rows, local, (zero,) * states, unroll=8)
         for n in range(states):
             sums_ref[n, pl.ds(fold * sublanes, sublanes), :] = held[n]
     carry = jnp.zeros((states, LANES), jnp.float32)
@@ -141,7 +148,7 @@
             return held
 
         start = tuple(sums_ref[n, pl.ds(fold * sublanes, sublanes), :] for n in range(states))
-        lax.fori_loop(0, block_rows, whole, start, unroll=4)
+        lax.fori_loop(0, block_rows, whole, start, unroll=8)
     for r in range(blocks):
         rows = pl.ds(r * block_rows, block_rows)
         gated = query_ref[rows, :] * (mixed_ref[rows, :] + skip_ref[...] * drive_ref[rows, :])
@@ -150,19 +157,21 @@
 
 def hyena(coded, blocks, taps, decay, decay_block, coeff, skip, place, column_start):
     shorts, kinds, _ = taps.shape
-    rows, width = coded.shape[0], coded.shape[1] // kinds
+    rows, width = coded[0].shape[0] * len(coded), coded[0].shape[1] // kinds
     block_rows, states = rows // blocks, decay.shape[0]
     tiles = width // LANES
     scalars = jnp.stack([place, column_start])
+
+    def code_spec(k):
+        return pl.BlockSpec((2 * block_rows, LANES), lambda c, s: (0, k * tiles + c))
+
     return pl.pallas_call(
         functools.partial(conv_kernel, blocks, block_rows, shorts, states),
         grid_spec=pltpu.PrefetchScalarGridSpec(
             num_scalar_prefetch=1,
             grid=(width // LANES,),
             in_specs=[
-                pl.BlockSpec((rows, LANES), lambda c, s: (0, c)),
-                pl.BlockSpec((rows, LANES), lambda c, s: (0, tiles + c)),
-                pl.BlockSpec((rows, LANES), lambda c, s: (0, 2 * tiles + c)),
+                *[code_spec(k) for _ in coded for k in range(kinds)],
                 pl.BlockSpec((shorts, kinds, LANES), lambda c, s: (0, 0, s[1] + c)),
                 pl.BlockSpec((states, LANES), lambda c, s: (0, s[1] + c)),
                 pl.BlockSpec((states, LANES), lambda c, s: (0, s[1] + c)),
@@ -176,12 +185,13 @@
                 pltpu.VMEM((rows, LANES), jnp.float32),
                 pltpu.VMEM((rows, LANES), jnp.float32),
                 pltpu.VMEM((states, blocks, LANES), jnp.float32),
+                pltpu.VMEM((blocks * kinds, 8, LANES), jnp.float32),
             ],
         ),
         out_shape=jax.ShapeDtypeStruct((blocks, block_rows, width), jnp.bfloat16),
-        compiler_params=pltpu.CompilerParams(vmem_limit_bytes=48 * 2**20),
+        compiler_params=pltpu.CompilerParams(vmem_limit_bytes=24 * 2**20),
         cost_estimate=pl.CostEstimate(flops=1, bytes_accessed=1, transcendentals=0),
-    )(scalars, coded, coded, coded, taps, decay, decay_block, coeff, skip)
+    )(scalars, *[piece for piece in coded for _ in range(kinds)], taps, decay, decay_block, coeff, skip)
 
 
 def on_device(x_codes, w_codes, req_mult, req_shift, short_codes, residue_codes, rates, skip_gain):
@@ -285,7 +295,7 @@
             members = [i for i, piece in enumerate(pieces) if piece[0] == g]
             if t == ready[g]:
                 members = sorted(members, key=lambda i: pieces[i][1])
-                coded = jnp.concatenate([finals[i] for i in members])
+                coded = [finals[i] for i in members]
                 column_start = (jnp.where(layer == 0, 0, groups) + g) * (width // LANES)
                 gated[g] = hyena(coded, seq_devs, taps, decay, decay_block, coeff, skip, place, column_start)
 

time: 181 us -> 178 us (0.983)
  other arithmetic: 27.5 us -> 21.7 us
    convert_element_type x2 -> x4, other arithmetic: 1.94 us -> 5.02 us  [on_device(): send_inner = total.astype(WIRE)]
    convert_element_type x8 -> x6, other arithmetic: 9.32 us -> 6.28 us  [on_device(): jnp.clip(total * (1.0 / WIRE_SCALE), -127.0, 127.0).astype(jnp.bfloat16)]
    convert_element_type x10, other arithmetic: 10.6 us -> 8 us  [on_device(): send_outer = send_outer.astype(WIRE)]
    ppermute x10, starting transfers between devices: 26.4 us -> 28.7 us  [on_device(): got_outer[t] = lax.ppermute(send_outer, 'tp', OUTER_PAIRS)]
    concatenate x2 -> x0, other arithmetic: 2.32 us -> none  [on_device(): coded = jnp.concatenate([finals[i] for i in members])]
    unnamed x64, local copies, waits for them, and re-layouts: 1.03 us -> 3.21 us
  transfers between devices with their start and end apart: 31 -> 31, of which waited for: 11 -> 8; matrix products, arithmetic and copies ran while one was open for 12% -> 9% of each run, Pallas kernels for 33% -> 33%
where the time goes in v3:
time: 178 us; the launch traced here: 176 us
  Pallas kernels  58.6 us (33%)
  starting transfers between devices  55.8 us (31%)
  waiting for transfers between devices  22.7 us (13%)
  other arithmetic  21.7 us (12%)
  blocking collectives  12.9 us (7%)
  local copies, waits for them, and re-layouts  4.11 us (2%)
    pallas_call x8, Pallas kernels, project(): pl.pallas_call(functools.partial(project_kernel, len(blocks), groups), gr...  44.2 us
    ppermute x10, starting transfers between devices, on_device(): got_outer[t] = lax.ppermute(send_outer, 'tp', OUTER_PAIRS)  28.7 us
    ppermute x10, waiting for transfers between devices, on_device(): got_outer[t] = lax.ppermute(send_outer, 'tp', OUTER_PAIRS)  16.6 us
    pallas_call x2, Pallas kernels, hyena(): pl.pallas_call(functools.partial(conv_kernel, blocks, block_rows, shorts,...  14.4 us
    all_to_all x1, blocking collectives, on_device(): lax.all_to_all(mine, 'seq', split_axis=0, concat_axis=0, tiled=True)  12.9 us
    convert_element_type x10, other arithmetic, on_device(): send_outer = send_outer.astype(WIRE)  8 us
    ppermute x2, starting transfers between devices, spread(): opposite = lax.ppermute(slice_for(3), 'tp', [(0, 3), (3, 0)])  7.78 us
    ppermute x8, starting transfers between devices, on_device(): got_inner[t] = lax.ppermute(send_inner, 'tp', INNER_PAIRS)  7.64 us
  transfers between devices with their start and end apart: 31, of which 8 were waited for; matrix products, arithmetic and copies ran while one was open for 9% of the time, Pallas kernels for 33%

profile of v3, /device:TPU:0, one launch (start us, length us, event | category | flops | bytes accessed | tf_op | source)
XLA Modules:
  0.0 176.4 jit_solution(15853739094709539991)
XLA Ops:
  0.0 1.3 convert_element_type.147.refs_0_
  1.8 2.6 %collective-permute-start.4 = (bf16[128,2048]{1,0:T(8,128)(2,1)S(1)}, bf16[128,2048]{1,0:T(8,128)(2,1)S(1)}, u32[]{:S(2)}, u32[]{:S(2)}) collective-permute-start(bf16[128,2048]{1,0:T(8,128)(2,1)S(1)} %convert_element_type.147.refs_0_), channel_id=1, source_target_pairs={{0,8},{4,12},{8,0},{12,4},{16,24},{20,28},{24,16},{28,20},{1,9},{5... | collective-permute-start | bytes 1572872 | tf_op jit(solution)/shard_map/ppermute | solution.py:212
  5.2 6.2 %shard_map.85 = (f32[256,768]{1,0:T(8,128)S(1)}, f32[256,768]{1,0:T(8,128)S(1)}) custom-call(s32[1]{0:T(128)} %bitcast.2.where_ref, bf16[128,2048]{1,0:T(8,128)(2,1)S(1)} %convert_element_type.147.refs_0_, bf16[128,2048]{1,0:T(8,128)(2,1)S(1)} %collective-permute-done.6.refs_1_, s32[3,2048,1024]{2,1,0:T(8,128)} %refs_4_.7, ...), custom_call_target="tpu_custom_call" | custom-call | flops 1 | bytes 1 | tf_op jit(solution)/shard_map/pallas_call | solution.py:63
  12.3 1.6 collective-permute-start.7
  13.9 1.5 collective-permute-start
  16.4 6.0 %shard_map.86 = (f32[256,768]{1,0:T(8,128)S(1)}, f32[256,768]{1,0:T(8,128)S(1)}) custom-call(s32[1]{0:T(128)} %bitcast.3.where_ref, bf16[128,2048]{1,0:T(8,128)(2,1)S(1)} %convert_element_type.147.refs_0_, bf16[128,2048]{1,0:T(8,128)(2,1)S(1)} %copy-done.27, s32[3,2048,1024]{2,1,0:T(8,128)} %refs_4_.7, f32[3,1,1024]{2,1,0:T(1,128)S(1)} %reshape.36.refs_5_.refs_3_, ...), custom_call_target="tpu_custom_call" | custom-call | flops 1 | bytes 1 | tf_op jit(solution)/shard_map/pallas_call | solution.py:63
  23.8 1.8 %add_convert_fusion.3 = f16[256,768]{1,0:T(8,128)(2,1)} fusion(f32[256,768]{1,0:T(8,128)S(1)} %get-tuple-element.47, f16[256,768]{1,0:T(8,128)(2,1)} %collective-permute-done.7), kind=kLoop, calls=%fused_computation.23 | loop fusion | flops 589824 | bytes 1572864 | tf_op jit(solution)/shard_map/convert_element_type | solution.py:278
  26.3 4.4 %collective-permute-start.9 = (f16[256,768]{1,0:T(8,128)(2,1)}, f16[256,768]{1,0:T(8,128)(2,1)}, u32[]{:S(2)}, u32[]{:S(2)}) collective-permute-start(f16[256,768]{1,0:T(8,128)(2,1)} %convert_element_type.150), channel_id=1, source_target_pairs={{0,1},{1,0},{2,3},{3,2},{4,5},{5,4},{6,7},{7,6},{8,9},{9,8},{10,11... | collective-permute-start | bytes 1179656 | tf_op jit(solution)/shard_map/ppermute | solution.py:287
  30.7 1.9 %collective-permute-start.2 = (bf16[128,2048]{1,0:T(8,128)(2,1)S(1)}, bf16[128,2048]{1,0:T(8,128)(2,1)S(1)}, u32[]{:S(2)}, u32[]{:S(2)}) collective-permute-start(bf16[128,2048]{1,0:T(8,128)(2,1)S(1)} %convert_element_type.147.refs_0_), channel_id=1, source_target_pairs={{0,24},{4,28},{8,16},{12,20},{16,8},{20,12},{24,0},{28,4},{1,25},{... | collective-permute-start | bytes 1572872 | tf_op jit(solution)/shard_map/ppermute | solution.py:212
  32.7 6.3 %shard_map.84 = (f32[256,768]{1,0:T(8,128)S(1)}, f32[256,768]{1,0:T(8,128)S(1)}) custom-call(s32[1]{0:T(128)} %bitcast.2.where_ref, bf16[128,2048]{1,0:T(8,128)(2,1)S(1)} %collective-permute-done.4.refs_0_, bf16[128,2048]{1,0:T(8,128)(2,1)} %collective-permute-done.5.refs_1_, s32[3,2048,1024]{2,1,0:T(8,128)} %refs_4_.7, ...), custom_call_target="tpu_custom_call" | custom-call | flops 1 | bytes 1 | tf_op jit(solution)/shard_map/pallas_call | solution.py:63
  40.1 1.1 add_convert_fusion.2
  41.2 1.8 %collective-permute-start.11 = (f16[256,768]{1,0:T(8,128)(2,1)S(1)}, f16[256,768]{1,0:T(8,128)(2,1)S(1)}, u32[]{:S(2)}, u32[]{:S(2)}) collective-permute-start(f16[256,768]{1,0:T(8,128)(2,1)S(1)} %select_convert_fusion.5), channel_id=1, source_target_pairs={{0,1},{1,0},{2,3},{3,2},{4,5},{5,4},{6,7},{7,6},{8,9},{9,8},{10,11... | collective-permute-start | bytes 1179656 | tf_op jit(solution)/shard_map/ppermute | solution.py:287
  43.8 1.2 collective-permute-done.2.refs_2_.refs_4_
  45.0 1.0 copy-done.25
  46.0 6.1 %shard_map.87 = (f32[256,768]{1,0:T(8,128)S(1)}, f32[256,768]{1,0:T(8,128)S(1)}) custom-call(s32[1]{0:T(128)} %bitcast.3.where_ref, bf16[128,2048]{1,0:T(8,128)(2,1)S(1)} %copy-done.25, bf16[128,2048]{1,0:T(8,128)(2,1)} %collective-permute-done.5.refs_1_, s32[3,2048,1024]{2,1,0:T(8,128)} %refs_4_.7, f32[3,1,1024]{2,1,0:T(1,128)S(1)} %reshape.36.refs_5_.refs_3_, ...), custom_call_target="tpu_custom_call" | custom-call | flops 1 | bytes 1 | tf_op jit(solution)/shard_map/pallas_call | solution.py:63
  53.3 4.4 %collective-permute-start.13 = (f16[256,768]{1,0:T(8,128)(2,1)S(1)}, f16[256,768]{1,0:T(8,128)(2,1)S(1)}, u32[]{:S(2)}, u32[]{:S(2)}) collective-permute-start(f16[256,768]{1,0:T(8,128)(2,1)S(1)} %select_convert_fusion.4), channel_id=1, source_target_pairs={{0,1},{1,0},{2,3},{3,2},{4,5},{5,4},{6,7},{7,6},{8,9},{9,8},{10,11... | collective-permute-start | bytes 1179656 | tf_op jit(solution)/shard_map/ppermute | solution.py:287
  57.6 4.8 %shard_map.83 = (f32[256,768]{1,0:T(8,128)S(1)}, f32[256,768]{1,0:T(8,128)S(1)}) custom-call(s32[1]{0:T(128)} %bitcast.1.where_ref, bf16[128,2048]{1,0:T(8,128)(2,1)S(1)} %collective-permute-done.refs_0_.refs_4_, bf16[128,2048]{1,0:T(8,128)(2,1)S(1)} %collective-permute-done.1.refs_1_, bf16[128,2048]{1,0:T(8,128)(2,1)S(1)} %collective-permute-done.2.refs_2_.refs_4_, ...), custom_call_target="tpu_custom_call" | custom-call | flops 1 | bytes 1 | tf_op jit(solution)/shard_map/pallas_call | solution.py:63
  62.6 3.9 %collective-permute-done.13 = f16[256,768]{1,0:T(8,128)(2,1)S(1)} collective-permute-done((f16[256,768]{1,0:T(8,128)(2,1)S(1)}, f16[256,768]{1,0:T(8,128)(2,1)S(1)}, u32[]{:S(2)}, u32[]{:S(2)}) %collective-permute-start.13) | collective-permute-done | bytes 393248 | tf_op jit(solution)/shard_map/ppermute | solution.py:287
  66.7 1.8 %collective-permute-start.15 = (f16[256,768]{1,0:T(8,128)(2,1)S(1)}, f16[256,768]{1,0:T(8,128)(2,1)S(1)}, u32[]{:S(2)}, u32[]{:S(2)}) collective-permute-start(f16[256,768]{1,0:T(8,128)(2,1)S(1)} %select_convert_fusion.3), channel_id=1, source_target_pairs={{0,1},{1,0},{2,3},{3,2},{4,5},{5,4},{6,7},{7,6},{8,9},{9,8},{10,11... | collective-permute-start | bytes 1179656 | tf_op jit(solution)/shard_map/ppermute | solution.py:287
  69.2 4.8 %shard_map.88 = (f32[256,768]{1,0:T(8,128)S(1)}, f32[256,768]{1,0:T(8,128)S(1)}) custom-call(s32[1]{0:T(128)} %bitcast.4.where_ref, bf16[128,2048]{1,0:T(8,128)(2,1)S(1)} %collective-permute-done.refs_0_.refs_4_, bf16[128,2048]{1,0:T(8,128)(2,1)S(1)} %collective-permute-done.1.refs_1_, bf16[128,2048]{1,0:T(8,128)(2,1)S(1)} %collective-permute-done.2.refs_2_.refs_4_, ...), custom_call_target="tpu_custom_call" | custom-call | flops 1 | bytes 1 | tf_op jit(solution)/shard_map/pallas_call | solution.py:63
  74.0 2.7 %collective-permute-done.15 = f16[256,768]{1,0:T(8,128)(2,1)S(1)} collective-permute-done((f16[256,768]{1,0:T(8,128)(2,1)S(1)}, f16[256,768]{1,0:T(8,128)(2,1)S(1)}, u32[]{:S(2)}, u32[]{:S(2)}) %collective-permute-start.15) | collective-permute-done | bytes 393248 | tf_op jit(solution)/shard_map/ppermute | solution.py:287
  76.7 1.1 clamp_convert_fusion.6
  78.7 1.4 collective-permute-start.16
  80.1 3.5 %collective-permute-start.17 = (f16[256,768]{1,0:T(8,128)(2,1)}, f16[256,768]{1,0:T(8,128)(2,1)}, u32[]{:S(2)}, u32[]{:S(2)}) collective-permute-start(f16[256,768]{1,0:T(8,128)(2,1)} %select_convert_fusion.2), channel_id=1, source_target_pairs={{0,1},{1,0},{2,3},{3,2},{4,5},{5,4},{6,7},{7,6},{8,9},{9,8},{10,11... | collective-permute-start | bytes 1179656 | tf_op jit(solution)/shard_map/ppermute | solution.py:287
  83.6 4.9 %shard_map.82 = (f32[256,768]{1,0:T(8,128)S(1)}, f32[256,768]{1,0:T(8,128)S(1)}) custom-call(s32[1]{0:T(128)} %bitcast.where_ref, bf16[128,2048]{1,0:T(8,128)(2,1)S(1)} %collective-permute-done.refs_0_.refs_4_, bf16[128,2048]{1,0:T(8,128)(2,1)S(1)} %collective-permute-done.1.refs_1_, bf16[128,2048]{1,0:T(8,128)(2,1)S(1)} %collective-permute-done.2.refs_2_.refs_4_, ...), custom_call_target="tpu_custom_call" | custom-call | flops 1 | bytes 1 | tf_op jit(solution)/shard_map/pallas_call | solution.py:63
  88.6 2.5 %select_convert_fusion.1 = f16[256,768]{1,0:T(8,128)(2,1)} fusion(f32[256,768]{1,0:T(8,128)S(1)} %get-tuple-element.40, f32[256,768]{1,0:T(8,128)S(1)} %copy-done.4, f16[256,768]{1,0:T(8,128)(2,1)} %collective-permute-done.16, pred[]{:T(512)S(6)} %or.3), kind=kLoop, calls=%fused_computation.14 | loop fusion | flops 786432 | bytes 2359297 | tf_op jit(solution)/shard_map/convert_element_type | solution.py:268
  91.1 1.9 %fusion.3 = (f16[256,768]{1,0:T(8,128)(2,1)}, bf16[256,768]{1,0:T(8,128)(2,1)S(1)}) fusion(f16[256,768]{1,0:T(8,128)(2,1)} %collective-permute-done.17, f32[256,768]{1,0:T(8,128)S(1)} %copy-done.18, f32[256,768]{1,0:T(8,128)S(1)} %copy-done.20, pred[]{:T(512)S(6)} %or.3), kind=kLoop, calls=%fused_computation.38 | loop fusion | flops 1376256 | bytes 2752513 | tf_op jit(solution)/shard_map/convert_element_type | solution.py:278
  93.0 3.0 %collective-permute-start.19 = (f16[256,768]{1,0:T(8,128)(2,1)}, f16[256,768]{1,0:T(8,128)(2,1)}, u32[]{:S(2)}, u32[]{:S(2)}) collective-permute-start(f16[256,768]{1,0:T(8,128)(2,1)} %select_convert_fusion.1), channel_id=1, source_target_pairs={{0,1},{1,0},{2,3},{3,2},{4,5},{5,4},{6,7},{7,6},{8,9},{9,8},{10,11... | collective-permute-start | bytes 1179656 | tf_op jit(solution)/shard_map/ppermute | solution.py:287
  96.1 1.4 collective-permute-start.18
  97.5 5.0 %shard_map.89 = (f32[256,768]{1,0:T(8,128)S(1)}, f32[256,768]{1,0:T(8,128)S(1)}) custom-call(s32[1]{0:T(128)} %bitcast.5.where_ref, bf16[128,2048]{1,0:T(8,128)(2,1)S(1)} %collective-permute-done.refs_0_.refs_4_, bf16[128,2048]{1,0:T(8,128)(2,1)S(1)} %collective-permute-done.1.refs_1_, bf16[128,2048]{1,0:T(8,128)(2,1)S(1)} %collective-permute-done.2.refs_2_.refs_4_, ...), custom_call_target="tpu_custom_call" | custom-call | flops 1 | bytes 1 | tf_op jit(solution)/shard_map/pallas_call | solution.py:63
  102.5 1.5 clamp_convert_fusion.5
  104.0 1.1 select_convert_fusion
  105.9 4.2 %collective-permute-start.21 = (f16[256,768]{1,0:T(8,128)(2,1)S(1)}, f16[256,768]{1,0:T(8,128)(2,1)S(1)}, u32[]{:S(2)}, u32[]{:S(2)}) collective-permute-start(f16[256,768]{1,0:T(8,128)(2,1)S(1)} %select_convert_fusion), channel_id=1, source_target_pairs={{0,1},{1,0},{2,3},{3,2},{4,5},{5,4},{6,7},{7,6},{8,9},{9,8},{10,11... | collective-permute-start | bytes 1179656 | tf_op jit(solution)/shard_map/ppermute | solution.py:287
  110.1 5.7 %collective-permute-done.21 = f16[256,768]{1,0:T(8,128)(2,1)S(1)} collective-permute-done((f16[256,768]{1,0:T(8,128)(2,1)S(1)}, f16[256,768]{1,0:T(8,128)(2,1)S(1)}, u32[]{:S(2)}, u32[]{:S(2)}) %collective-permute-start.21) | collective-permute-done | bytes 393248 | tf_op jit(solution)/shard_map/ppermute | solution.py:287
  116.7 1.4 collective-permute-start.22
  118.3 4.0 %collective-permute-start.26 = (f16[256,768]{1,0:T(8,128)(2,1)S(1)}, f16[256,768]{1,0:T(8,128)(2,1)}, u32[]{:S(2)}, u32[]{:S(2)}) collective-permute-start(f16[256,768]{1,0:T(8,128)(2,1)S(1)} %add_convert_fusion.1), channel_id=1, source_target_pairs={{0,1},{1,0},{2,3},{3,2},{4,5},{5,4},{6,7},{7,6},{8,9},{9,8},{10,11... | collective-permute-start | bytes 1179656 | tf_op jit(solution)/shard_map/ppermute | solution.py:287
  123.3 7.2 %shard_map.90 = bf16[8,128,256]{2,1,0:T(8,128)(2,1)S(1)} custom-call(s32[2]{0:T(128)S(1)} %pad_add_fusion.place_ref, bf16[256,768]{1,0:T(8,128)(2,1)S(1)} %get-tuple-element.79.refs_0_.refs_1_.refs_2_, bf16[256,768]{1,0:T(8,128)(2,1)S(1)} %get-tuple-element.79.refs_0_.refs_1_.refs_2_, bf16[256,768]{1,0:T(8,128)(2,1)S(1)} %get-tuple-element.79.refs_0_.refs_1_.refs_2_, ...), custom_call_target="tpu_custom_call" | custom-call | flops 1 | bytes 1 | tf_op jit(solution)/shard_map/pallas_call | solution.py:168
  130.6 1.3 add_convert_fusion
  132.1 2.1 %collective-permute-start.23 = (bf16[8,32,256]{2,1,0:T(8,128)(2,1)S(1)}, bf16[8,32,256]{2,1,0:T(8,128)(2,1)S(1)}, u32[]{:S(2)}, u32[]{:S(2)}) collective-permute-start(bf16[8,32,256]{2,1,0:T(8,128)(2,1)S(1)} %get-tuple-element.91), channel_id=1, source_target_pairs={{0,1},{1,0},{2,3},{3,2},{4,5},{5,4},{6,7},{7,6},{8,9},{9,8},{10,11... | collective-permute-start | bytes 393224 | tf_op jit(solution)/shard_map/ppermute | solution.py:313
  134.4 4.1 %collective-permute-start.25 = (bf16[8,32,256]{2,1,0:T(8,128)(2,1)S(1)}, bf16[8,32,256]{2,1,0:T(8,128)(2,1)S(1)}, u32[]{:S(2)}, u32[]{:S(2)}) collective-permute-start(bf16[8,32,256]{2,1,0:T(8,128)(2,1)S(1)} %get-tuple-element.89), channel_id=1, source_target_pairs={{0,3},{3,0},{4,7},{7,4},{8,11},{11,8},{12,15},{15,12},{16,19},{19,... | collective-permute-start | bytes 393224 | tf_op jit(solution)/shard_map/ppermute | solution.py:315
  138.5 1.4 clamp_convert_fusion.1.refs_6_.refs_7_.refs_8_
  139.9 3.0 %collective-permute-done.27 = f16[256,768]{1,0:T(8,128)(2,1)S(1)} collective-permute-done((f16[256,768]{1,0:T(8,128)(2,1)S(1)}, f16[256,768]{1,0:T(8,128)(2,1)S(1)}, u32[]{:S(2)}, u32[]{:S(2)}) %collective-permute-start.27) | collective-permute-done | bytes 393248 | tf_op jit(solution)/shard_map/ppermute | solution.py:287
  142.8 1.3 clamp_convert_fusion.refs_9_.refs_10_.refs_11_
  144.1 7.2 %shard_map.91 = bf16[8,128,256]{2,1,0:T(8,128)(2,1)S(1)} custom-call(s32[2]{0:T(128)S(1)} %pad_add_fusion.1.place_ref, bf16[256,768]{1,0:T(8,128)(2,1)S(1)} %get-tuple-element.84.refs_0_.refs_1_.refs_2_, bf16[256,768]{1,0:T(8,128)(2,1)S(1)} %get-tuple-element.84.refs_0_.refs_1_.refs_2_, bf16[256,768]{1,0:T(8,128)(2,1)S(1)} %get-tuple-element.84.refs_0_.refs_1_.refs_2_, ...), custom_call_target="tpu_custom_call" | custom-call | flops 1 | bytes 1 | tf_op jit(solution)/shard_map/pallas_call | solution.py:168
  151.4 2.5 %collective-permute-start.29 = (bf16[8,32,256]{2,1,0:T(8,128)(2,1)S(1)}, bf16[8,32,256]{2,1,0:T(8,128)(2,1)S(1)}, u32[]{:S(2)}, u32[]{:S(2)}) collective-permute-start(bf16[8,32,256]{2,1,0:T(8,128)(2,1)S(1)} %get-tuple-element.93), channel_id=1, source_target_pairs={{0,2},{2,0},{1,3},{3,1},{4,6},{6,4},{5,7},{7,5},{8,10},{10,8},{9,1... | collective-permute-start | bytes 393224 | tf_op jit(solution)/shard_map/ppermute | solution.py:314
  154.0 3.7 %collective-permute-start.30 = (bf16[8,32,256]{2,1,0:T(8,128)(2,1)S(1)}, bf16[8,32,256]{2,1,0:T(8,128)(2,1)S(1)}, u32[]{:S(2)}, u32[]{:S(2)}) collective-permute-start(bf16[8,32,256]{2,1,0:T(8,128)(2,1)S(1)} %get-tuple-element.92), channel_id=1, source_target_pairs={{0,3},{3,0},{4,7},{7,4},{8,11},{11,8},{12,15},{15,12},{16,19},{19,... | collective-permute-start | bytes 393224 | tf_op jit(solution)/shard_map/ppermute | solution.py:315
  157.8 4.8 %collective-permute-done.30 = bf16[8,32,256]{2,1,0:T(8,128)(2,1)S(1)} collective-permute-done((bf16[8,32,256]{2,1,0:T(8,128)(2,1)S(1)}, bf16[8,32,256]{2,1,0:T(8,128)(2,1)S(1)}, u32[]{:S(2)}, u32[]{:S(2)}) %collective-permute-start.30) | collective-permute-done | bytes 131104 | tf_op jit(solution)/shard_map/ppermute | solution.py:315
  162.7 12.9 %all_to_all.5 = bf16[8,32,1024]{2,1,0:T(8,128)(2,1)S(1)} all-to-all(bf16[8,32,1024]{2,1,0:T(8,128)(2,1)S(1)} %pad_maximum_fusion), channel_id=1, replica_groups=mesh['seq'=8,'tp'=4] {'seq'}, dimensions={0} | all-to-all | bytes 1048576 | tf_op jit(solution)/shard_map/all_to_all | solution.py:323
  (123 shorter events, 14.4 us)
Async XLA Ops:
  1.3 3.9 %collective-permute-start.6 = (bf16[128,2048]{1,0:T(8,128)(2,1)S(1)}, bf16[128,2048]{1,0:T(8,128)(2,1)S(1)}, u32[]{:S(2)}, u32[]{:S(2)}) collective-permute-start(bf16[128,2048]{1,0:T(8,128)(2,1)S(1)} %convert_element_type.147.refs_0_), channel_id=1, source_target_pairs={{0,4},{4,0},{8,12},{12,8},{16,20},{20,16},{24,28},{28,24},{1,5},{5... | collective-permute-start | bytes 1572872 | tf_op jit(solution)/shard_map/ppermute | solution.py:212
  1.8 21.5 %collective-permute-start.4 = (bf16[128,2048]{1,0:T(8,128)(2,1)S(1)}, bf16[128,2048]{1,0:T(8,128)(2,1)S(1)}, u32[]{:S(2)}, u32[]{:S(2)}) collective-permute-start(bf16[128,2048]{1,0:T(8,128)(2,1)S(1)} %convert_element_type.147.refs_0_), channel_id=1, source_target_pairs={{0,8},{4,12},{8,0},{12,4},{16,24},{20,28},{24,16},{28,20},{1,9},{5... | collective-permute-start | bytes 1572872 | tf_op jit(solution)/shard_map/ppermute | solution.py:212
  11.4 14.9 %copy-start.5 = (f32[256,768]{1,0:T(8,128)}, f32[256,768]{1,0:T(8,128)S(1)}, u32[]{:S(2)}) copy-start(f32[256,768]{1,0:T(8,128)S(1)} %get-tuple-element.45) | copy-start | bytes 2359300
  12.3 11.5 %collective-permute-start.7 = (f16[256,768]{1,0:T(8,128)(2,1)}, f16[256,768]{1,0:T(8,128)(2,1)}, u32[]{:S(2)}, u32[]{:S(2)}) collective-permute-start(f16[256,768]{1,0:T(8,128)(2,1)} %convert_element_type.151), channel_id=1, source_target_pairs={{0,1},{1,0},{2,3},{3,2},{4,5},{5,4},{6,7},{7,6},{8,9},{9,8},{10,11... | collective-permute-start | bytes 1179656 | tf_op jit(solution)/shard_map/ppermute | solution.py:287
  13.9 18.8 %collective-permute-start = (bf16[128,2048]{1,0:T(8,128)(2,1)S(1)}, bf16[128,2048]{1,0:T(8,128)(2,1)S(1)}, u32[]{:S(2)}, u32[]{:S(2)}) collective-permute-start(bf16[128,2048]{1,0:T(8,128)(2,1)S(1)} %convert_element_type.147.refs_0_), channel_id=1, source_target_pairs={{0,16},{4,20},{8,24},{12,28},{16,0},{20,4},{24,8},{28,12},{1,17},{... | collective-permute-start | bytes 1572872 | tf_op jit(solution)/shard_map/ppermute | solution.py:212
  22.4 8.3 %copy-start.13 = (f32[256,768]{1,0:T(8,128)}, f32[256,768]{1,0:T(8,128)S(1)}, u32[]{:S(2)}) copy-start(f32[256,768]{1,0:T(8,128)S(1)} %get-tuple-element.49) | copy-start | bytes 2359300
  22.5 8.3 %copy-start.15 = (f32[256,768]{1,0:T(8,128)}, f32[256,768]{1,0:T(8,128)S(1)}, u32[]{:S(2)}) copy-start(f32[256,768]{1,0:T(8,128)S(1)} %get-tuple-element.47) | copy-start | bytes 2359300
  23.3 20.5 %copy-start.24 = (bf16[128,2048]{1,0:T(8,128)(2,1)}, bf16[128,2048]{1,0:T(8,128)(2,1)S(1)}, u32[]{:S(2)}) copy-start(bf16[128,2048]{1,0:T(8,128)(2,1)S(1)} %collective-permute-done.4.refs_0_) | copy-start | bytes 1572868
  23.3 9.4 %collective-permute-start.5 = (bf16[128,2048]{1,0:T(8,128)(2,1)S(1)}, bf16[128,2048]{1,0:T(8,128)(2,1)}, u32[]{:S(2)}, u32[]{:S(2)}) collective-permute-start(bf16[128,2048]{1,0:T(8,128)(2,1)S(1)} %collective-permute-done.4.refs_0_), channel_id=1, source_target_pairs={{0,4},{4,0},{8,12},{12,8},{16,20},{20,16},{24,28},{28,24},{1,5},{5... | collective-permute-start | bytes 1572872 | tf_op jit(solution)/shard_map/ppermute | solution.py:212
  25.6 13.5 %collective-permute-start.8 = (f16[256,768]{1,0:T(8,128)(2,1)}, f16[256,768]{1,0:T(8,128)(2,1)S(1)}, u32[]{:S(2)}, u32[]{:S(2)}) collective-permute-start(f16[256,768]{1,0:T(8,128)(2,1)} %add_convert_fusion.3), channel_id=1, source_target_pairs={{1,2},{2,1},{5,6},{6,5},{9,10},{10,9},{13,14},{14,13},{17,18},{18,... | collective-permute-start | bytes 1179656 | tf_op jit(solution)/shard_map/ppermute | solution.py:289
  26.3 13.8 %collective-permute-start.9 = (f16[256,768]{1,0:T(8,128)(2,1)}, f16[256,768]{1,0:T(8,128)(2,1)}, u32[]{:S(2)}, u32[]{:S(2)}) collective-permute-start(f16[256,768]{1,0:T(8,128)(2,1)} %convert_element_type.150), channel_id=1, source_target_pairs={{0,1},{1,0},{2,3},{3,2},{4,5},{5,4},{6,7},{7,6},{8,9},{9,8},{10,11... | collective-permute-start | bytes 1179656 | tf_op jit(solution)/shard_map/ppermute | solution.py:287
  30.7 14.2 %collective-permute-start.2 = (bf16[128,2048]{1,0:T(8,128)(2,1)S(1)}, bf16[128,2048]{1,0:T(8,128)(2,1)S(1)}, u32[]{:S(2)}, u32[]{:S(2)}) collective-permute-start(bf16[128,2048]{1,0:T(8,128)(2,1)S(1)} %convert_element_type.147.refs_0_), channel_id=1, source_target_pairs={{0,24},{4,28},{8,16},{12,20},{16,8},{20,12},{24,0},{28,4},{1,25},{... | collective-permute-start | bytes 1572872 | tf_op jit(solution)/shard_map/ppermute | solution.py:212
  32.7 19.5 %copy-start.16 = (f32[256,768]{1,0:T(8,128)S(1)}, f32[256,768]{1,0:T(8,128)}, u32[]{:S(2)}) copy-start(f32[256,768]{1,0:T(8,128)} %copy-done.15) | copy-start | bytes 2359300
  32.7 19.7 %copy-start.6 = (f32[256,768]{1,0:T(8,128)S(1)}, f32[256,768]{1,0:T(8,128)}, u32[]{:S(2)}) copy-start(f32[256,768]{1,0:T(8,128)} %copy-done.5) | copy-start | bytes 2359300
  41.2 11.0 %collective-permute-start.11 = (f16[256,768]{1,0:T(8,128)(2,1)S(1)}, f16[256,768]{1,0:T(8,128)(2,1)S(1)}, u32[]{:S(2)}, u32[]{:S(2)}) collective-permute-start(f16[256,768]{1,0:T(8,128)(2,1)S(1)} %select_convert_fusion.5), channel_id=1, source_target_pairs={{0,1},{1,0},{2,3},{3,2},{4,5},{5,4},{6,7},{7,6},{8,9},{9,8},{10,11... | collective-permute-start | bytes 1179656 | tf_op jit(solution)/shard_map/ppermute | solution.py:287
  43.0 9.4 %collective-permute-start.10 = (f16[256,768]{1,0:T(8,128)(2,1)S(1)}, f16[256,768]{1,0:T(8,128)(2,1)S(1)}, u32[]{:S(2)}, u32[]{:S(2)}) collective-permute-start(f16[256,768]{1,0:T(8,128)(2,1)S(1)} %add_convert_fusion.2), channel_id=1, source_target_pairs={{1,2},{2,1},{5,6},{6,5},{9,10},{10,9},{13,14},{14,13},{17,18},{18,... | collective-permute-start | bytes 1179656 | tf_op jit(solution)/shard_map/ppermute | solution.py:289
  43.7 13.9 %collective-permute-start.1 = (bf16[128,2048]{1,0:T(8,128)(2,1)S(1)}, bf16[128,2048]{1,0:T(8,128)(2,1)S(1)}, u32[]{:S(2)}, u32[]{:S(2)}) collective-permute-start(bf16[128,2048]{1,0:T(8,128)(2,1)S(1)} %collective-permute-done.refs_0_.refs_4_), channel_id=1, source_target_pairs={{0,4},{4,0},{8,12},{12,8},{16,20},{20,16},{24,28},{28,24},{1,5},{5... | collective-permute-start | bytes 1572872 | tf_op jit(solution)/shard_map/ppermute | solution.py:212
  45.0 12.7 %collective-permute-start.3 = (bf16[128,2048]{1,0:T(8,128)(2,1)S(1)}, bf16[128,2048]{1,0:T(8,128)(2,1)S(1)}, u32[]{:S(2)}, u32[]{:S(2)}) collective-permute-start(bf16[128,2048]{1,0:T(8,128)(2,1)S(1)} %collective-permute-done.2.refs_2_.refs_4_), channel_id=1, source_target_pairs={{0,4},{4,0},{8,12},{12,8},{16,20},{20,16},{24,28},{28,24},{1,5},{5... | collective-permute-start | bytes 1572872 | tf_op jit(solution)/shard_map/ppermute | solution.py:212
  52.2 21.8 %copy-start.17 = (f32[256,768]{1,0:T(8,128)}, f32[256,768]{1,0:T(8,128)S(1)}, u32[]{:S(2)}) copy-start(f32[256,768]{1,0:T(8,128)S(1)} %get-tuple-element.55) | copy-start | bytes 2359300
  52.6 9.9 %collective-permute-start.12 = (f16[256,768]{1,0:T(8,128)(2,1)S(1)}, f16[256,768]{1,0:T(8,128)(2,1)S(1)}, u32[]{:S(2)}, u32[]{:S(2)}) collective-permute-start(f16[256,768]{1,0:T(8,128)(2,1)S(1)} %get-tuple-element.54), channel_id=1, source_target_pairs={{1,2},{2,1},{5,6},{6,5},{9,10},{10,9},{13,14},{14,13},{17,18},{18,... | collective-permute-start | bytes 1179656 | tf_op jit(solution)/shard_map/ppermute | solution.py:289
  53.3 13.2 %collective-permute-start.13 = (f16[256,768]{1,0:T(8,128)(2,1)S(1)}, f16[256,768]{1,0:T(8,128)(2,1)S(1)}, u32[]{:S(2)}, u32[]{:S(2)}) collective-permute-start(f16[256,768]{1,0:T(8,128)(2,1)S(1)} %select_convert_fusion.4), channel_id=1, source_target_pairs={{0,1},{1,0},{2,3},{3,2},{4,5},{5,4},{6,7},{7,6},{8,9},{9,8},{10,11... | collective-permute-start | bytes 1179656 | tf_op jit(solution)/shard_map/ppermute | solution.py:287
  62.5 16.2 %copy-start.1 = (f32[256,768]{1,0:T(8,128)}, f32[256,768]{1,0:T(8,128)S(1)}, u32[]{:S(2)}) copy-start(f32[256,768]{1,0:T(8,128)S(1)} %get-tuple-element.41) | copy-start | bytes 2359300
  66.7 10.1 %collective-permute-start.15 = (f16[256,768]{1,0:T(8,128)(2,1)S(1)}, f16[256,768]{1,0:T(8,128)(2,1)S(1)}, u32[]{:S(2)}, u32[]{:S(2)}) collective-permute-start(f16[256,768]{1,0:T(8,128)(2,1)S(1)} %select_convert_fusion.3), channel_id=1, source_target_pairs={{0,1},{1,0},{2,3},{3,2},{4,5},{5,4},{6,7},{7,6},{8,9},{9,8},{10,11... | collective-permute-start | bytes 1179656 | tf_op jit(solution)/shard_map/ppermute | solution.py:287
  68.5 9.3 %collective-permute-start.14 = (f16[256,768]{1,0:T(8,128)(2,1)S(1)}, f16[256,768]{1,0:T(8,128)(2,1)S(1)}, u32[]{:S(2)}, u32[]{:S(2)}) collective-permute-start(f16[256,768]{1,0:T(8,128)(2,1)S(1)} %get-tuple-element.57), channel_id=1, source_target_pairs={{1,2},{2,1},{5,6},{6,5},{9,10},{10,9},{13,14},{14,13},{17,18},{18,... | collective-permute-start | bytes 1179656 | tf_op jit(solution)/shard_map/ppermute | solution.py:289
  78.7 9.9 %collective-permute-start.16 = (f16[256,768]{1,0:T(8,128)(2,1)}, f16[256,768]{1,0:T(8,128)(2,1)}, u32[]{:S(2)}, u32[]{:S(2)}) collective-permute-start(f16[256,768]{1,0:T(8,128)(2,1)} %get-tuple-element.60), channel_id=1, source_target_pairs={{1,2},{2,1},{5,6},{6,5},{9,10},{10,9},{13,14},{14,13},{17,18},{18,... | collective-permute-start | bytes 1179656 | tf_op jit(solution)/shard_map/ppermute | solution.py:289
  80.1 11.0 %collective-permute-start.17 = (f16[256,768]{1,0:T(8,128)(2,1)}, f16[256,768]{1,0:T(8,128)(2,1)}, u32[]{:S(2)}, u32[]{:S(2)}) collective-permute-start(f16[256,768]{1,0:T(8,128)(2,1)} %select_convert_fusion.2), channel_id=1, source_target_pairs={{0,1},{1,0},{2,3},{3,2},{4,5},{5,4},{6,7},{7,6},{8,9},{9,8},{10,11... | collective-permute-start | bytes 1179656 | tf_op jit(solution)/shard_map/ppermute | solution.py:287
  83.6 7.5 %copy-start.20 = (f32[256,768]{1,0:T(8,128)S(1)}, f32[256,768]{1,0:T(8,128)}, u32[]{:S(2)}) copy-start(f32[256,768]{1,0:T(8,128)} %copy-done.19) | copy-start | bytes 2359300
  88.6 29.6 %copy-start.31 = (s32[3,3,1024]{2,1,0:T(4,128)S(1)}, s32[3,3,1024]{2,1,0:T(4,128)}, u32[]{:S(2)}) copy-start(s32[3,3,1024]{2,1,0:T(4,128)} %param.12) | copy-start | bytes 110596
  88.6 29.7 %copy-start.29 = (f32[16,1024]{1,0:T(8,128)S(1)}, f32[16,1024]{1,0:T(8,128)}, u32[]{:S(2)}) copy-start(f32[16,1024]{1,0:T(8,128)} %param.14) | copy-start | bytes 196612
  88.6 29.7 %copy-start.30 = (s32[16,1024]{1,0:T(8,128)S(1)}, s32[16,1024]{1,0:T(8,128)}, u32[]{:S(2)}) copy-start(s32[16,1024]{1,0:T(8,128)} %param.13) | copy-start | bytes 196612
  88.6 33.7 %copy-start.28 = (f32[1024]{0:T(1024)S(1)}, f32[1024]{0:T(1024)}, u32[]{:S(2)}) copy-start(f32[1024]{0:T(1024)} %param.15) | copy-start | bytes 12292
  93.0 9.4 %collective-permute-start.19 = (f16[256,768]{1,0:T(8,128)(2,1)}, f16[256,768]{1,0:T(8,128)(2,1)}, u32[]{:S(2)}, u32[]{:S(2)}) collective-permute-start(f16[256,768]{1,0:T(8,128)(2,1)} %select_convert_fusion.1), channel_id=1, source_target_pairs={{0,1},{1,0},{2,3},{3,2},{4,5},{5,4},{6,7},{7,6},{8,9},{9,8},{10,11... | collective-permute-start | bytes 1179656 | tf_op jit(solution)/shard_map/ppermute | solution.py:287
  96.1 8.0 %collective-permute-start.18 = (f16[256,768]{1,0:T(8,128)(2,1)}, f16[256,768]{1,0:T(8,128)(2,1)}, u32[]{:S(2)}, u32[]{:S(2)}) collective-permute-start(f16[256,768]{1,0:T(8,128)(2,1)} %get-tuple-element.63), channel_id=1, source_target_pairs={{1,2},{2,1},{5,6},{6,5},{9,10},{10,9},{13,14},{14,13},{17,18},{18,... | collective-permute-start | bytes 1179656 | tf_op jit(solution)/shard_map/ppermute | solution.py:289
  97.5 12.5 %copy-start.10 = (f32[256,768]{1,0:T(8,128)S(1)}, f32[256,768]{1,0:T(8,128)}, u32[]{:S(2)}) copy-start(f32[256,768]{1,0:T(8,128)} %copy-done.9) | copy-start | bytes 2359300
  97.5 18.3 %copy-start.21 = (f32[256,768]{1,0:T(8,128)S(1)}, f32[256,768]{1,0:T(8,128)}, u32[]{:S(2)}) copy-start(f32[256,768]{1,0:T(8,128)} %copy-done.19) | copy-start | bytes 2359300
  102.4 13.3 %copy-start.11 = (f32[256,768]{1,0:T(8,128)}, f32[256,768]{1,0:T(8,128)S(1)}, u32[]{:S(2)}) copy-start(f32[256,768]{1,0:T(8,128)S(1)} %get-tuple-element.67) | copy-start | bytes 2359300
  102.4 14.3 %copy-start.12 = (f32[256,768]{1,0:T(8,128)}, f32[256,768]{1,0:T(8,128)S(1)}, u32[]{:S(2)}) copy-start(f32[256,768]{1,0:T(8,128)S(1)} %get-tuple-element.64) | copy-start | bytes 2359300
  105.2 4.8 %collective-permute-start.20 = (f16[256,768]{1,0:T(8,128)(2,1)S(1)}, f16[256,768]{1,0:T(8,128)(2,1)S(1)}, u32[]{:S(2)}, u32[]{:S(2)}) collective-permute-start(f16[256,768]{1,0:T(8,128)(2,1)S(1)} %get-tuple-element.66), channel_id=1, source_target_pairs={{1,2},{2,1},{5,6},{6,5},{9,10},{10,9},{13,14},{14,13},{17,18},{18,... | collective-permute-start | bytes 1179656 | tf_op jit(solution)/shard_map/ppermute | solution.py:289
  105.9 9.9 %collective-permute-start.21 = (f16[256,768]{1,0:T(8,128)(2,1)S(1)}, f16[256,768]{1,0:T(8,128)(2,1)S(1)}, u32[]{:S(2)}, u32[]{:S(2)}) collective-permute-start(f16[256,768]{1,0:T(8,128)(2,1)S(1)} %select_convert_fusion), channel_id=1, source_target_pairs={{0,1},{1,0},{2,3},{3,2},{4,5},{5,4},{6,7},{7,6},{8,9},{9,8},{10,11... | collective-permute-start | bytes 1179656 | tf_op jit(solution)/shard_map/ppermute | solution.py:287
  116.7 13.8 %collective-permute-start.22 = (f16[256,768]{1,0:T(8,128)(2,1)}, f16[256,768]{1,0:T(8,128)(2,1)}, u32[]{:S(2)}, u32[]{:S(2)}) collective-permute-start(f16[256,768]{1,0:T(8,128)(2,1)} %get-tuple-element.69), channel_id=1, source_target_pairs={{1,2},{2,1},{5,6},{6,5},{9,10},{10,9},{13,14},{14,13},{17,18},{18,... | collective-permute-start | bytes 1179656 | tf_op jit(solution)/shard_map/ppermute | solution.py:289
  118.3 20.2 %collective-permute-start.26 = (f16[256,768]{1,0:T(8,128)(2,1)S(1)}, f16[256,768]{1,0:T(8,128)(2,1)}, u32[]{:S(2)}, u32[]{:S(2)}) collective-permute-start(f16[256,768]{1,0:T(8,128)(2,1)S(1)} %add_convert_fusion.1), channel_id=1, source_target_pairs={{0,1},{1,0},{2,3},{3,2},{4,5},{5,4},{6,7},{7,6},{8,9},{9,8},{10,11... | collective-permute-start | bytes 1179656 | tf_op jit(solution)/shard_map/ppermute | solution.py:287
  131.9 10.9 %collective-permute-start.27 = (f16[256,768]{1,0:T(8,128)(2,1)S(1)}, f16[256,768]{1,0:T(8,128)(2,1)S(1)}, u32[]{:S(2)}, u32[]{:S(2)}) collective-permute-start(f16[256,768]{1,0:T(8,128)(2,1)S(1)} %add_convert_fusion), channel_id=1, source_target_pairs={{0,1},{1,0},{2,3},{3,2},{4,5},{5,4},{6,7},{7,6},{8,9},{9,8},{10,11... | collective-permute-start | bytes 1179656 | tf_op jit(solution)/shard_map/ppermute | solution.py:287
  132.1 21.9 %collective-permute-start.23 = (bf16[8,32,256]{2,1,0:T(8,128)(2,1)S(1)}, bf16[8,32,256]{2,1,0:T(8,128)(2,1)S(1)}, u32[]{:S(2)}, u32[]{:S(2)}) collective-permute-start(bf16[8,32,256]{2,1,0:T(8,128)(2,1)S(1)} %get-tuple-element.91), channel_id=1, source_target_pairs={{0,1},{1,0},{2,3},{3,2},{4,5},{5,4},{6,7},{7,6},{8,9},{9,8},{10,11... | collective-permute-start | bytes 393224 | tf_op jit(solution)/shard_map/ppermute | solution.py:313
  134.1 23.6 %collective-permute-start.24 = (bf16[8,32,256]{2,1,0:T(8,128)(2,1)S(1)}, bf16[8,32,256]{2,1,0:T(8,128)(2,1)S(1)}, u32[]{:S(2)}, u32[]{:S(2)}) collective-permute-start(bf16[8,32,256]{2,1,0:T(8,128)(2,1)S(1)} %get-tuple-element.90), channel_id=1, source_target_pairs={{0,2},{2,0},{1,3},{3,1},{4,6},{6,4},{5,7},{7,5},{8,10},{10,8},{9,1... | collective-permute-start | bytes 393224 | tf_op jit(solution)/shard_map/ppermute | solution.py:314
  134.4 23.3 %collective-permute-start.25 = (bf16[8,32,256]{2,1,0:T(8,128)(2,1)S(1)}, bf16[8,32,256]{2,1,0:T(8,128)(2,1)S(1)}, u32[]{:S(2)}, u32[]{:S(2)}) collective-permute-start(bf16[8,32,256]{2,1,0:T(8,128)(2,1)S(1)} %get-tuple-element.89), channel_id=1, source_target_pairs={{0,3},{3,0},{4,7},{7,4},{8,11},{11,8},{12,15},{15,12},{16,19},{19,... | collective-permute-start | bytes 393224 | tf_op jit(solution)/shard_map/ppermute | solution.py:315
  151.4 6.4 %collective-permute-start.28 = (bf16[8,32,256]{2,1,0:T(8,128)(2,1)S(1)}, bf16[8,32,256]{2,1,0:T(8,128)(2,1)S(1)}, u32[]{:S(2)}, u32[]{:S(2)}) collective-permute-start(bf16[8,32,256]{2,1,0:T(8,128)(2,1)S(1)} %get-tuple-element.94), channel_id=1, source_target_pairs={{0,1},{1,0},{2,3},{3,2},{4,5},{5,4},{6,7},{7,6},{8,9},{9,8},{10,11... | collective-permute-start | bytes 393224 | tf_op jit(solution)/shard_map/ppermute | solution.py:313
  151.4 6.4 %collective-permute-start.29 = (bf16[8,32,256]{2,1,0:T(8,128)(2,1)S(1)}, bf16[8,32,256]{2,1,0:T(8,128)(2,1)S(1)}, u32[]{:S(2)}, u32[]{:S(2)}) collective-permute-start(bf16[8,32,256]{2,1,0:T(8,128)(2,1)S(1)} %get-tuple-element.93), channel_id=1, source_target_pairs={{0,2},{2,0},{1,3},{3,1},{4,6},{6,4},{5,7},{7,5},{8,10},{10,8},{9,1... | collective-permute-start | bytes 393224 | tf_op jit(solution)/shard_map/ppermute | solution.py:314
  154.0 8.6 %collective-permute-start.30 = (bf16[8,32,256]{2,1,0:T(8,128)(2,1)S(1)}, bf16[8,32,256]{2,1,0:T(8,128)(2,1)S(1)}, u32[]{:S(2)}, u32[]{:S(2)}) collective-permute-start(bf16[8,32,256]{2,1,0:T(8,128)(2,1)S(1)} %get-tuple-element.92), channel_id=1, source_target_pairs={{0,3},{3,0},{4,7},{7,4},{8,11},{11,8},{12,15},{15,12},{16,19},{19,... | collective-permute-start | bytes 393224 | tf_op jit(solution)/shard_map/ppermute | solution.py:315
  (15 other events, 68.3 us)

commit v4 on v3

--- a/solution.py
+++ b/solution.py
@@ -253,7 +253,8 @@
     got_outer, got_inner = {}, {}
     finals = {}
     token = jnp.zeros((8, LANES), jnp.float32)
-    partials(first, calls[0], half_first, token)
+    for g in range(groups):
+        partials(first, ([g], [0]), half_first, token)
     gated = [None] * groups
     ready = [max(i for i, piece in enumerate(pieces) if piece[0] == g) + 3 for g in range(groups)]
     for t in range(count + 3):

time: 178 us -> 177 us (level)
  Pallas kernels: 58.6 us -> 61.2 us
  other arithmetic: 21.7 us -> 19.9 us
    pallas_call x8 -> x9, Pallas kernels: 44.2 us -> 46.8 us  [project(): pl.pallas_call(functools.partial(project_kernel, len(blocks), groups), gr...]
    unnamed x64 -> x44, local copies, waits for them, and re-layouts: 3.21 us -> 3.99 us
  transfers between devices with their start and end apart: 31 -> 31, of which waited for: 8 -> 8; matrix products, arithmetic and copies ran while one was open for 9% -> 9% of each run, Pallas kernels for 33% -> 35%
where the time goes in v4:
time: 177 us; the launch traced here: 176 us
  Pallas kernels  61.2 us (35%)
  starting transfers between devices  55.3 us (31%)
  waiting for transfers between devices  21.5 us (12%)
  other arithmetic  19.9 us (11%)
  blocking collectives  12.2 us (7%)
  local copies, waits for them, and re-layouts  4.9 us (3%)
    pallas_call x9, Pallas kernels, project(): pl.pallas_call(functools.partial(project_kernel, len(blocks), groups), gr...  46.8 us
    ppermute x10, starting transfers between devices, on_device(): got_outer[t] = lax.ppermute(send_outer, 'tp', OUTER_PAIRS)  29.3 us
    ppermute x10, waiting for transfers between devices, on_device(): got_outer[t] = lax.ppermute(send_outer, 'tp', OUTER_PAIRS)  15.1 us
    pallas_call x2, Pallas kernels, hyena(): pl.pallas_call(functools.partial(conv_kernel, blocks, block_rows, shorts,...  14.4 us
    all_to_all x1, blocking collectives, on_device(): lax.all_to_all(mine, 'seq', split_axis=0, concat_axis=0, tiled=True)  12.2 us
    ppermute x8, starting transfers between devices, on_device(): got_inner[t] = lax.ppermute(send_inner, 'tp', INNER_PAIRS)  7.65 us
    convert_element_type x10, other arithmetic, on_device(): send_outer = send_outer.astype(WIRE)  6.67 us
    convert_element_type x6, other arithmetic, on_device(): jnp.clip(total * (1.0 / WIRE_SCALE), -127.0, 127.0).astype(jnp.bfloat16)  6.63 us
  transfers between devices with their start and end apart: 31, of which 8 were waited for; matrix products, arithmetic and copies ran while one was open for 9% of the time, Pallas kernels for 35%

profile of v4, /device:TPU:0, one launch (start us, length us, event | category | flops | bytes accessed | tf_op | source)
XLA Modules:
  0.0 175.7 jit_solution(14971906983430879017)
XLA Ops:
  0.0 1.3 convert_element_type.147.refs_0_
  1.8 2.6 %collective-permute-start.4 = (bf16[128,2048]{1,0:T(8,128)(2,1)S(1)}, bf16[128,2048]{1,0:T(8,128)(2,1)}, u32[]{:S(2)}, u32[]{:S(2)}) collective-permute-start(bf16[128,2048]{1,0:T(8,128)(2,1)S(1)} %convert_element_type.147.refs_0_), channel_id=1, source_target_pairs={{0,8},{4,12},{8,0},{12,4},{16,24},{20,28},{24,16},{28,20},{1,9},{5... | collective-permute-start | bytes 1572872 | tf_op jit(solution)/shard_map/ppermute | solution.py:212
  5.2 4.2 %shard_map.86 = f32[256,768]{1,0:T(8,128)S(1)} custom-call(s32[1]{0:T(128)} %bitcast.1.where_ref, bf16[128,2048]{1,0:T(8,128)(2,1)S(1)} %convert_element_type.147.refs_0_, bf16[128,2048]{1,0:T(8,128)(2,1)S(1)} %collective-permute-done.6.refs_1_, s32[3,2048,1024]{2,1,0:T(8,128)} %refs_4_.7, f32[3,1,1024]{2,1,0:T(1,128)S(1)} %reshape.37.refs_5_.refs_3_, ...), custom_call_target="tpu_custom_call" | custom-call | flops 1 | bytes 1 | tf_op jit(solution)/shard_map/pallas_call | solution.py:63
  10.2 1.6 collective-permute-start.7
  11.8 1.5 collective-permute-start
  13.3 6.0 %shard_map.87 = (f32[256,768]{1,0:T(8,128)S(1)}, f32[256,768]{1,0:T(8,128)S(1)}) custom-call(s32[1]{0:T(128)} %bitcast.3.where_ref, bf16[128,2048]{1,0:T(8,128)(2,1)S(1)} %convert_element_type.147.refs_0_, bf16[128,2048]{1,0:T(8,128)(2,1)S(1)} %collective-permute-done.6.refs_1_, s32[3,2048,1024]{2,1,0:T(8,128)} %refs_4_.7, ...), custom_call_target="tpu_custom_call" | custom-call | flops 1 | bytes 1 | tf_op jit(solution)/shard_map/pallas_call | solution.py:63
  20.2 4.5 %shard_map.85 = f32[256,768]{1,0:T(8,128)S(1)} custom-call(s32[1]{0:T(128)} %bitcast.where_ref, bf16[128,2048]{1,0:T(8,128)(2,1)S(1)} %convert_element_type.147.refs_0_, bf16[128,2048]{1,0:T(8,128)(2,1)S(1)} %collective-permute-done.6.refs_1_, s32[3,2048,1024]{2,1,0:T(8,128)} %refs_4_.7, f32[3,1,1024]{2,1,0:T(1,128)S(1)} %reshape.37.refs_5_.refs_3_, ...), custom_call_target="tpu_custom_call" | custom-call | flops 1 | bytes 1 | tf_op jit(solution)/shard_map/pallas_call | solution.py:63
  25.5 1.9 %add_convert_fusion.3 = f16[256,768]{1,0:T(8,128)(2,1)} fusion(f32[256,768]{1,0:T(8,128)S(1)} %get-tuple-element.43, f16[256,768]{1,0:T(8,128)(2,1)} %collective-permute-done.7), kind=kLoop, calls=%fused_computation.23 | loop fusion | flops 589824 | bytes 1572864 | tf_op jit(solution)/shard_map/convert_element_type | solution.py:279
  27.4 1.4 collective-permute-start.8
  28.8 3.7 %collective-permute-start.9 = (f16[256,768]{1,0:T(8,128)(2,1)}, f16[256,768]{1,0:T(8,128)(2,1)}, u32[]{:S(2)}, u32[]{:S(2)}) collective-permute-start(f16[256,768]{1,0:T(8,128)(2,1)} %convert_element_type.150), channel_id=1, source_target_pairs={{0,1},{1,0},{2,3},{3,2},{4,5},{5,4},{6,7},{7,6},{8,9},{9,8},{10,11... | collective-permute-start | bytes 1179656 | tf_op jit(solution)/shard_map/ppermute | solution.py:288
  33.5 6.4 %shard_map.84 = (f32[256,768]{1,0:T(8,128)S(1)}, f32[256,768]{1,0:T(8,128)S(1)}) custom-call(s32[1]{0:T(128)} %bitcast.2.where_ref, bf16[128,2048]{1,0:T(8,128)(2,1)} %collective-permute-done.4.refs_0_, bf16[128,2048]{1,0:T(8,128)(2,1)} %collective-permute-done.5.refs_1_, s32[3,2048,1024]{2,1,0:T(8,128)} %refs_4_.7, ...), custom_call_target="tpu_custom_call" | custom-call | flops 1 | bytes 1 | tf_op jit(solution)/shard_map/pallas_call | solution.py:63
  40.0 1.1 select_convert_fusion.5
  41.1 1.2 collective-permute-done.9
  42.3 1.1 add_convert_fusion.2
  43.4 1.8 %collective-permute-start.11 = (f16[256,768]{1,0:T(8,128)(2,1)S(1)}, f16[256,768]{1,0:T(8,128)(2,1)S(1)}, u32[]{:S(2)}, u32[]{:S(2)}) collective-permute-start(f16[256,768]{1,0:T(8,128)(2,1)S(1)} %select_convert_fusion.5), channel_id=1, source_target_pairs={{0,1},{1,0},{2,3},{3,2},{4,5},{5,4},{6,7},{7,6},{8,9},{9,8},{10,11... | collective-permute-start | bytes 1179656 | tf_op jit(solution)/shard_map/ppermute | solution.py:288
  46.0 1.2 collective-permute-done.2.refs_2_.refs_4_
  47.2 6.3 %shard_map.88 = (f32[256,768]{1,0:T(8,128)S(1)}, f32[256,768]{1,0:T(8,128)S(1)}) custom-call(s32[1]{0:T(128)} %bitcast.3.where_ref, bf16[128,2048]{1,0:T(8,128)(2,1)} %collective-permute-done.4.refs_0_, bf16[128,2048]{1,0:T(8,128)(2,1)} %collective-permute-done.5.refs_1_, s32[3,2048,1024]{2,1,0:T(8,128)} %refs_4_.7, ...), custom_call_target="tpu_custom_call" | custom-call | flops 1 | bytes 1 | tf_op jit(solution)/shard_map/pallas_call | solution.py:63
  56.0 5.3 %collective-permute-start.13 = (f16[256,768]{1,0:T(8,128)(2,1)S(1)}, f16[256,768]{1,0:T(8,128)(2,1)S(1)}, u32[]{:S(2)}, u32[]{:S(2)}) collective-permute-start(f16[256,768]{1,0:T(8,128)(2,1)S(1)} %select_convert_fusion.4), channel_id=1, source_target_pairs={{0,1},{1,0},{2,3},{3,2},{4,5},{5,4},{6,7},{7,6},{8,9},{9,8},{10,11... | collective-permute-start | bytes 1179656 | tf_op jit(solution)/shard_map/ppermute | solution.py:288
  61.3 4.8 %shard_map.83 = (f32[256,768]{1,0:T(8,128)S(1)}, f32[256,768]{1,0:T(8,128)S(1)}) custom-call(s32[1]{0:T(128)} %bitcast.1.where_ref, bf16[128,2048]{1,0:T(8,128)(2,1)S(1)} %collective-permute-done.refs_0_.refs_4_, bf16[128,2048]{1,0:T(8,128)(2,1)S(1)} %collective-permute-done.1.refs_1_, bf16[128,2048]{1,0:T(8,128)(2,1)S(1)} %collective-permute-done.2.refs_2_.refs_4_, ...), custom_call_target="tpu_custom_call" | custom-call | flops 1 | bytes 1 | tf_op jit(solution)/shard_map/pallas_call | solution.py:63
  66.3 2.9 %collective-permute-done.13 = f16[256,768]{1,0:T(8,128)(2,1)S(1)} collective-permute-done((f16[256,768]{1,0:T(8,128)(2,1)S(1)}, f16[256,768]{1,0:T(8,128)(2,1)S(1)}, u32[]{:S(2)}, u32[]{:S(2)}) %collective-permute-start.13) | collective-permute-done | bytes 393248 | tf_op jit(solution)/shard_map/ppermute | solution.py:288
  69.3 1.8 %collective-permute-start.15 = (f16[256,768]{1,0:T(8,128)(2,1)S(1)}, f16[256,768]{1,0:T(8,128)(2,1)S(1)}, u32[]{:S(2)}, u32[]{:S(2)}) collective-permute-start(f16[256,768]{1,0:T(8,128)(2,1)S(1)} %select_convert_fusion.3), channel_id=1, source_target_pairs={{0,1},{1,0},{2,3},{3,2},{4,5},{5,4},{6,7},{7,6},{8,9},{9,8},{10,11... | collective-permute-start | bytes 1179656 | tf_op jit(solution)/shard_map/ppermute | solution.py:288
  71.8 4.8 %shard_map.89 = (f32[256,768]{1,0:T(8,128)S(1)}, f32[256,768]{1,0:T(8,128)S(1)}) custom-call(s32[1]{0:T(128)} %bitcast.4.where_ref, bf16[128,2048]{1,0:T(8,128)(2,1)S(1)} %collective-permute-done.refs_0_.refs_4_, bf16[128,2048]{1,0:T(8,128)(2,1)S(1)} %collective-permute-done.1.refs_1_, bf16[128,2048]{1,0:T(8,128)(2,1)S(1)} %collective-permute-done.2.refs_2_.refs_4_, ...), custom_call_target="tpu_custom_call" | custom-call | flops 1 | bytes 1 | tf_op jit(solution)/shard_map/pallas_call | solution.py:63
  76.7 1.7 collective-permute-done.15
  80.1 4.4 %collective-permute-start.17 = (f16[256,768]{1,0:T(8,128)(2,1)S(1)}, f16[256,768]{1,0:T(8,128)(2,1)S(1)}, u32[]{:S(2)}, u32[]{:S(2)}) collective-permute-start(f16[256,768]{1,0:T(8,128)(2,1)S(1)} %select_convert_fusion.2), channel_id=1, source_target_pairs={{0,1},{1,0},{2,3},{3,2},{4,5},{5,4},{6,7},{7,6},{8,9},{9,8},{10,11... | collective-permute-start | bytes 1179656 | tf_op jit(solution)/shard_map/ppermute | solution.py:288
  84.5 4.8 %shard_map.82 = (f32[256,768]{1,0:T(8,128)S(1)}, f32[256,768]{1,0:T(8,128)S(1)}) custom-call(s32[1]{0:T(128)} %bitcast.where_ref, bf16[128,2048]{1,0:T(8,128)(2,1)S(1)} %collective-permute-done.refs_0_.refs_4_, bf16[128,2048]{1,0:T(8,128)(2,1)S(1)} %collective-permute-done.1.refs_1_, bf16[128,2048]{1,0:T(8,128)(2,1)S(1)} %collective-permute-done.2.refs_2_.refs_4_, ...), custom_call_target="tpu_custom_call" | custom-call | flops 1 | bytes 1 | tf_op jit(solution)/shard_map/pallas_call | solution.py:63
  90.3 1.1 fusion.3
  91.5 2.3 %collective-permute-start.19 = (f16[256,768]{1,0:T(8,128)(2,1)}, f16[256,768]{1,0:T(8,128)(2,1)}, u32[]{:S(2)}, u32[]{:S(2)}) collective-permute-start(f16[256,768]{1,0:T(8,128)(2,1)} %select_convert_fusion.1), channel_id=1, source_target_pairs={{0,1},{1,0},{2,3},{3,2},{4,5},{5,4},{6,7},{7,6},{8,9},{9,8},{10,11... | collective-permute-start | bytes 1179656 | tf_op jit(solution)/shard_map/ppermute | solution.py:288
  93.8 1.4 collective-permute-start.18
  95.2 5.0 %shard_map.90 = (f32[256,768]{1,0:T(8,128)S(1)}, f32[256,768]{1,0:T(8,128)S(1)}) custom-call(s32[1]{0:T(128)} %bitcast.5.where_ref, bf16[128,2048]{1,0:T(8,128)(2,1)S(1)} %collective-permute-done.refs_0_.refs_4_, bf16[128,2048]{1,0:T(8,128)(2,1)S(1)} %collective-permute-done.1.refs_1_, bf16[128,2048]{1,0:T(8,128)(2,1)S(1)} %collective-permute-done.2.refs_2_.refs_4_, ...), custom_call_target="tpu_custom_call" | custom-call | flops 1 | bytes 1 | tf_op jit(solution)/shard_map/pallas_call | solution.py:63
  100.2 1.5 clamp_convert_fusion.5
  101.7 1.2 select_convert_fusion
  103.6 5.0 %collective-permute-start.21 = (f16[256,768]{1,0:T(8,128)(2,1)S(1)}, f16[256,768]{1,0:T(8,128)(2,1)S(1)}, u32[]{:S(2)}, u32[]{:S(2)}) collective-permute-start(f16[256,768]{1,0:T(8,128)(2,1)S(1)} %select_convert_fusion), channel_id=1, source_target_pairs={{0,1},{1,0},{2,3},{3,2},{4,5},{5,4},{6,7},{7,6},{8,9},{9,8},{10,11... | collective-permute-start | bytes 1179656 | tf_op jit(solution)/shard_map/ppermute | solution.py:288
  108.7 5.6 %collective-permute-done.21 = f16[256,768]{1,0:T(8,128)(2,1)S(1)} collective-permute-done((f16[256,768]{1,0:T(8,128)(2,1)S(1)}, f16[256,768]{1,0:T(8,128)(2,1)S(1)}, u32[]{:S(2)}, u32[]{:S(2)}) %collective-permute-start.21) | collective-permute-done | bytes 393248 | tf_op jit(solution)/shard_map/ppermute | solution.py:288
  115.3 1.4 collective-permute-start.22
  116.9 3.3 %collective-permute-start.26 = (f16[256,768]{1,0:T(8,128)(2,1)S(1)}, f16[256,768]{1,0:T(8,128)(2,1)}, u32[]{:S(2)}, u32[]{:S(2)}) collective-permute-start(f16[256,768]{1,0:T(8,128)(2,1)S(1)} %add_convert_fusion.1), channel_id=1, source_target_pairs={{0,1},{1,0},{2,3},{3,2},{4,5},{5,4},{6,7},{7,6},{8,9},{9,8},{10,11... | collective-permute-start | bytes 1179656 | tf_op jit(solution)/shard_map/ppermute | solution.py:288
  122.2 7.2 %shard_map.91 = bf16[8,128,256]{2,1,0:T(8,128)(2,1)S(1)} custom-call(s32[2]{0:T(128)S(1)} %pad_add_fusion.place_ref, bf16[256,768]{1,0:T(8,128)(2,1)S(1)} %copy-done, bf16[256,768]{1,0:T(8,128)(2,1)S(1)} %copy-done, bf16[256,768]{1,0:T(8,128)(2,1)S(1)} %copy-done, bf16[256,768]{1,0:T(8,128)(2,1)S(1)} %copy-done.2, bf16[256,768]{1,0:T(8,128)(2,1)S(1)} %copy-done.2, ...), custom_call_target="tpu_custom_call" | custom-call | flops 1 | bytes 1 | tf_op jit(solution)/shard_map/pallas_call | solution.py:168
  129.4 1.3 add_convert_fusion
  130.9 2.1 %collective-permute-start.23 = (bf16[8,32,256]{2,1,0:T(8,128)(2,1)S(1)}, bf16[8,32,256]{2,1,0:T(8,128)(2,1)S(1)}, u32[]{:S(2)}, u32[]{:S(2)}) collective-permute-start(bf16[8,32,256]{2,1,0:T(8,128)(2,1)S(1)} %get-tuple-element.87), channel_id=1, source_target_pairs={{0,1},{1,0},{2,3},{3,2},{4,5},{5,4},{6,7},{7,6},{8,9},{9,8},{10,11... | collective-permute-start | bytes 393224 | tf_op jit(solution)/shard_map/ppermute | solution.py:314
  133.0 1.0 collective-permute-start.24
  134.0 3.3 %collective-permute-start.25 = (bf16[8,32,256]{2,1,0:T(8,128)(2,1)S(1)}, bf16[8,32,256]{2,1,0:T(8,128)(2,1)S(1)}, u32[]{:S(2)}, u32[]{:S(2)}) collective-permute-start(bf16[8,32,256]{2,1,0:T(8,128)(2,1)S(1)} %get-tuple-element.85), channel_id=1, source_target_pairs={{0,3},{3,0},{4,7},{7,4},{8,11},{11,8},{12,15},{15,12},{16,19},{19,... | collective-permute-start | bytes 393224 | tf_op jit(solution)/shard_map/ppermute | solution.py:316
  137.3 1.1 clamp_convert_fusion.1.refs_6_.refs_7_.refs_8_
  138.5 2.9 %collective-permute-done.27 = f16[256,768]{1,0:T(8,128)(2,1)S(1)} collective-permute-done((f16[256,768]{1,0:T(8,128)(2,1)S(1)}, f16[256,768]{1,0:T(8,128)(2,1)S(1)}, u32[]{:S(2)}, u32[]{:S(2)}) %collective-permute-start.27) | collective-permute-done | bytes 393248 | tf_op jit(solution)/shard_map/ppermute | solution.py:288
  141.4 1.3 clamp_convert_fusion.refs_9_.refs_10_.refs_11_
  143.6 7.2 %shard_map.92 = bf16[8,128,256]{2,1,0:T(8,128)(2,1)S(1)} custom-call(s32[2]{0:T(128)S(1)} %pad_add_fusion.1.place_ref, bf16[256,768]{1,0:T(8,128)(2,1)S(1)} %get-tuple-element.80.refs_0_.refs_1_.refs_2_, bf16[256,768]{1,0:T(8,128)(2,1)S(1)} %get-tuple-element.80.refs_0_.refs_1_.refs_2_, bf16[256,768]{1,0:T(8,128)(2,1)S(1)} %get-tuple-element.80.refs_0_.refs_1_.refs_2_, ...), custom_call_target="tpu_custom_call" | custom-call | flops 1 | bytes 1 | tf_op jit(solution)/shard_map/pallas_call | solution.py:168
  151.0 3.0 %collective-permute-start.29 = (bf16[8,32,256]{2,1,0:T(8,128)(2,1)S(1)}, bf16[8,32,256]{2,1,0:T(8,128)(2,1)S(1)}, u32[]{:S(2)}, u32[]{:S(2)}) collective-permute-start(bf16[8,32,256]{2,1,0:T(8,128)(2,1)S(1)} %get-tuple-element.89), channel_id=1, source_target_pairs={{0,2},{2,0},{1,3},{3,1},{4,6},{6,4},{5,7},{7,5},{8,10},{10,8},{9,1... | collective-permute-start | bytes 393224 | tf_op jit(solution)/shard_map/ppermute | solution.py:315
  153.9 3.3 %collective-permute-start.30 = (bf16[8,32,256]{2,1,0:T(8,128)(2,1)S(1)}, bf16[8,32,256]{2,1,0:T(8,128)(2,1)S(1)}, u32[]{:S(2)}, u32[]{:S(2)}) collective-permute-start(bf16[8,32,256]{2,1,0:T(8,128)(2,1)S(1)} %get-tuple-element.88), channel_id=1, source_target_pairs={{0,3},{3,0},{4,7},{7,4},{8,11},{11,8},{12,15},{15,12},{16,19},{19,... | collective-permute-start | bytes 393224 | tf_op jit(solution)/shard_map/ppermute | solution.py:316
  157.3 5.2 %collective-permute-done.30 = bf16[8,32,256]{2,1,0:T(8,128)(2,1)S(1)} collective-permute-done((bf16[8,32,256]{2,1,0:T(8,128)(2,1)S(1)}, bf16[8,32,256]{2,1,0:T(8,128)(2,1)S(1)}, u32[]{:S(2)}, u32[]{:S(2)}) %collective-permute-start.30) | collective-permute-done | bytes 131104 | tf_op jit(solution)/shard_map/ppermute | solution.py:316
  162.7 12.2 %all_to_all.5 = bf16[8,32,1024]{2,1,0:T(8,128)(2,1)S(1)} all-to-all(bf16[8,32,1024]{2,1,0:T(8,128)(2,1)S(1)} %pad_maximum_fusion), channel_id=1, replica_groups=mesh['seq'=8,'tp'=4] {'seq'}, dimensions={0} | all-to-all | bytes 1048576 | tf_op jit(solution)/shard_map/all_to_all | solution.py:324
  (104 shorter events, 17.9 us)
Async XLA Ops:
  1.3 3.9 %collective-permute-start.6 = (bf16[128,2048]{1,0:T(8,128)(2,1)S(1)}, bf16[128,2048]{1,0:T(8,128)(2,1)S(1)}, u32[]{:S(2)}, u32[]{:S(2)}) collective-permute-start(bf16[128,2048]{1,0:T(8,128)(2,1)S(1)} %convert_element_type.147.refs_0_), channel_id=1, source_target_pairs={{0,4},{4,0},{8,12},{12,8},{16,20},{20,16},{24,28},{28,24},{1,5},{5... | collective-permute-start | bytes 1572872 | tf_op jit(solution)/shard_map/ppermute | solution.py:212
  1.8 23.7 %collective-permute-start.4 = (bf16[128,2048]{1,0:T(8,128)(2,1)S(1)}, bf16[128,2048]{1,0:T(8,128)(2,1)}, u32[]{:S(2)}, u32[]{:S(2)}) collective-permute-start(bf16[128,2048]{1,0:T(8,128)(2,1)S(1)} %convert_element_type.147.refs_0_), channel_id=1, source_target_pairs={{0,8},{4,12},{8,0},{12,4},{16,24},{20,28},{24,16},{28,20},{1,9},{5... | collective-permute-start | bytes 1572872 | tf_op jit(solution)/shard_map/ppermute | solution.py:212
  10.2 15.3 %collective-permute-start.7 = (f16[256,768]{1,0:T(8,128)(2,1)}, f16[256,768]{1,0:T(8,128)(2,1)}, u32[]{:S(2)}, u32[]{:S(2)}) collective-permute-start(f16[256,768]{1,0:T(8,128)(2,1)} %convert_element_type.151), channel_id=1, source_target_pairs={{0,1},{1,0},{2,3},{3,2},{4,5},{5,4},{6,7},{7,6},{8,9},{9,8},{10,11... | collective-permute-start | bytes 1179656 | tf_op jit(solution)/shard_map/ppermute | solution.py:288
  11.8 21.7 %collective-permute-start = (bf16[128,2048]{1,0:T(8,128)(2,1)S(1)}, bf16[128,2048]{1,0:T(8,128)(2,1)S(1)}, u32[]{:S(2)}, u32[]{:S(2)}) collective-permute-start(bf16[128,2048]{1,0:T(8,128)(2,1)S(1)} %convert_element_type.147.refs_0_), channel_id=1, source_target_pairs={{0,16},{4,20},{8,24},{12,28},{16,0},{20,4},{24,8},{28,12},{1,17},{... | collective-permute-start | bytes 1572872 | tf_op jit(solution)/shard_map/ppermute | solution.py:212
  20.2 8.6 %copy-start.12 = (f32[256,768]{1,0:T(8,128)}, f32[256,768]{1,0:T(8,128)S(1)}, u32[]{:S(2)}) copy-start(f32[256,768]{1,0:T(8,128)S(1)} %get-tuple-element.43) | copy-start | bytes 2359300
  25.5 8.0 %collective-permute-start.5 = (bf16[128,2048]{1,0:T(8,128)(2,1)}, bf16[128,2048]{1,0:T(8,128)(2,1)}, u32[]{:S(2)}, u32[]{:S(2)}) collective-permute-start(bf16[128,2048]{1,0:T(8,128)(2,1)} %collective-permute-done.4.refs_0_), channel_id=1, source_target_pairs={{0,4},{4,0},{8,12},{12,8},{16,20},{20,16},{24,28},{28,24},{1,5},{5... | collective-permute-start | bytes 1572872 | tf_op jit(solution)/shard_map/ppermute | solution.py:212
  27.4 12.6 %collective-permute-start.8 = (f16[256,768]{1,0:T(8,128)(2,1)}, f16[256,768]{1,0:T(8,128)(2,1)}, u32[]{:S(2)}, u32[]{:S(2)}) collective-permute-start(f16[256,768]{1,0:T(8,128)(2,1)} %add_convert_fusion.3), channel_id=1, source_target_pairs={{1,2},{2,1},{5,6},{6,5},{9,10},{10,9},{13,14},{14,13},{17,18},{18,... | collective-permute-start | bytes 1179656 | tf_op jit(solution)/shard_map/ppermute | solution.py:290
  28.8 13.5 %collective-permute-start.9 = (f16[256,768]{1,0:T(8,128)(2,1)}, f16[256,768]{1,0:T(8,128)(2,1)}, u32[]{:S(2)}, u32[]{:S(2)}) collective-permute-start(f16[256,768]{1,0:T(8,128)(2,1)} %convert_element_type.150), channel_id=1, source_target_pairs={{0,1},{1,0},{2,3},{3,2},{4,5},{5,4},{6,7},{7,6},{8,9},{9,8},{10,11... | collective-permute-start | bytes 1179656 | tf_op jit(solution)/shard_map/ppermute | solution.py:288
  32.5 14.7 %collective-permute-start.2 = (bf16[128,2048]{1,0:T(8,128)(2,1)S(1)}, bf16[128,2048]{1,0:T(8,128)(2,1)S(1)}, u32[]{:S(2)}, u32[]{:S(2)}) collective-permute-start(bf16[128,2048]{1,0:T(8,128)(2,1)S(1)} %convert_element_type.147.refs_0_), channel_id=1, source_target_pairs={{0,24},{4,28},{8,16},{12,20},{16,8},{20,12},{24,0},{28,4},{1,25},{... | collective-permute-start | bytes 1572872 | tf_op jit(solution)/shard_map/ppermute | solution.py:212
  33.5 8.9 %copy-start.11 = (f32[256,768]{1,0:T(8,128)S(1)}, f32[256,768]{1,0:T(8,128)}, u32[]{:S(2)}) copy-start(f32[256,768]{1,0:T(8,128)} %copy-done.10) | copy-start | bytes 2359300
  33.5 20.8 %copy-start.13 = (f32[256,768]{1,0:T(8,128)S(1)}, f32[256,768]{1,0:T(8,128)}, u32[]{:S(2)}) copy-start(f32[256,768]{1,0:T(8,128)} %copy-done.12) | copy-start | bytes 2359300
  43.4 10.8 %collective-permute-start.11 = (f16[256,768]{1,0:T(8,128)(2,1)S(1)}, f16[256,768]{1,0:T(8,128)(2,1)S(1)}, u32[]{:S(2)}, u32[]{:S(2)}) collective-permute-start(f16[256,768]{1,0:T(8,128)(2,1)S(1)} %select_convert_fusion.5), channel_id=1, source_target_pairs={{0,1},{1,0},{2,3},{3,2},{4,5},{5,4},{6,7},{7,6},{8,9},{9,8},{10,11... | collective-permute-start | bytes 1179656 | tf_op jit(solution)/shard_map/ppermute | solution.py:288
  45.2 9.9 %collective-permute-start.10 = (f16[256,768]{1,0:T(8,128)(2,1)S(1)}, f16[256,768]{1,0:T(8,128)(2,1)S(1)}, u32[]{:S(2)}, u32[]{:S(2)}) collective-permute-start(f16[256,768]{1,0:T(8,128)(2,1)S(1)} %add_convert_fusion.2), channel_id=1, source_target_pairs={{1,2},{2,1},{5,6},{6,5},{9,10},{10,9},{13,14},{14,13},{17,18},{18,... | collective-permute-start | bytes 1179656 | tf_op jit(solution)/shard_map/ppermute | solution.py:290
  45.9 15.4 %collective-permute-start.1 = (bf16[128,2048]{1,0:T(8,128)(2,1)S(1)}, bf16[128,2048]{1,0:T(8,128)(2,1)S(1)}, u32[]{:S(2)}, u32[]{:S(2)}) collective-permute-start(bf16[128,2048]{1,0:T(8,128)(2,1)S(1)} %collective-permute-done.refs_0_.refs_4_), channel_id=1, source_target_pairs={{0,4},{4,0},{8,12},{12,8},{16,20},{20,16},{24,28},{28,24},{1,5},{5... | collective-permute-start | bytes 1572872 | tf_op jit(solution)/shard_map/ppermute | solution.py:212
  47.2 14.1 %collective-permute-start.3 = (bf16[128,2048]{1,0:T(8,128)(2,1)S(1)}, bf16[128,2048]{1,0:T(8,128)(2,1)S(1)}, u32[]{:S(2)}, u32[]{:S(2)}) collective-permute-start(bf16[128,2048]{1,0:T(8,128)(2,1)S(1)} %collective-permute-done.2.refs_2_.refs_4_), channel_id=1, source_target_pairs={{0,4},{4,0},{8,12},{12,8},{16,20},{20,16},{24,28},{28,24},{1,5},{5... | collective-permute-start | bytes 1572872 | tf_op jit(solution)/shard_map/ppermute | solution.py:212
  55.3 10.8 %collective-permute-start.12 = (f16[256,768]{1,0:T(8,128)(2,1)S(1)}, f16[256,768]{1,0:T(8,128)(2,1)S(1)}, u32[]{:S(2)}, u32[]{:S(2)}) collective-permute-start(f16[256,768]{1,0:T(8,128)(2,1)S(1)} %get-tuple-element.50), channel_id=1, source_target_pairs={{1,2},{2,1},{5,6},{6,5},{9,10},{10,9},{13,14},{14,13},{17,18},{18,... | collective-permute-start | bytes 1179656 | tf_op jit(solution)/shard_map/ppermute | solution.py:290
  56.0 13.2 %collective-permute-start.13 = (f16[256,768]{1,0:T(8,128)(2,1)S(1)}, f16[256,768]{1,0:T(8,128)(2,1)S(1)}, u32[]{:S(2)}, u32[]{:S(2)}) collective-permute-start(f16[256,768]{1,0:T(8,128)(2,1)S(1)} %select_convert_fusion.4), channel_id=1, source_target_pairs={{0,1},{1,0},{2,3},{3,2},{4,5},{5,4},{6,7},{7,6},{8,9},{9,8},{10,11... | collective-permute-start | bytes 1179656 | tf_op jit(solution)/shard_map/ppermute | solution.py:288
  66.1 23.2 %copy-start.3 = (f32[256,768]{1,0:T(8,128)}, f32[256,768]{1,0:T(8,128)S(1)}, u32[]{:S(2)}) copy-start(f32[256,768]{1,0:T(8,128)S(1)} %get-tuple-element.39) | copy-start | bytes 2359300
  69.3 9.0 %collective-permute-start.15 = (f16[256,768]{1,0:T(8,128)(2,1)S(1)}, f16[256,768]{1,0:T(8,128)(2,1)S(1)}, u32[]{:S(2)}, u32[]{:S(2)}) collective-permute-start(f16[256,768]{1,0:T(8,128)(2,1)S(1)} %select_convert_fusion.3), channel_id=1, source_target_pairs={{0,1},{1,0},{2,3},{3,2},{4,5},{5,4},{6,7},{7,6},{8,9},{9,8},{10,11... | collective-permute-start | bytes 1179656 | tf_op jit(solution)/shard_map/ppermute | solution.py:288
  71.1 8.1 %collective-permute-start.14 = (f16[256,768]{1,0:T(8,128)(2,1)S(1)}, f16[256,768]{1,0:T(8,128)(2,1)S(1)}, u32[]{:S(2)}, u32[]{:S(2)}) collective-permute-start(f16[256,768]{1,0:T(8,128)(2,1)S(1)} %get-tuple-element.53), channel_id=1, source_target_pairs={{1,2},{2,1},{5,6},{6,5},{9,10},{10,9},{13,14},{14,13},{17,18},{18,... | collective-permute-start | bytes 1179656 | tf_op jit(solution)/shard_map/ppermute | solution.py:290
  76.6 3.5 %copy-start.16 = (f32[256,768]{1,0:T(8,128)}, f32[256,768]{1,0:T(8,128)S(1)}, u32[]{:S(2)}) copy-start(f32[256,768]{1,0:T(8,128)S(1)} %get-tuple-element.54) | copy-start | bytes 2359300
  76.6 14.8 %copy-start.14 = (f32[256,768]{1,0:T(8,128)}, f32[256,768]{1,0:T(8,128)S(1)}, u32[]{:S(2)}) copy-start(f32[256,768]{1,0:T(8,128)S(1)} %get-tuple-element.57) | copy-start | bytes 2359300
  79.4 9.9 %collective-permute-start.16 = (f16[256,768]{1,0:T(8,128)(2,1)S(1)}, f16[256,768]{1,0:T(8,128)(2,1)S(1)}, u32[]{:S(2)}, u32[]{:S(2)}) collective-permute-start(f16[256,768]{1,0:T(8,128)(2,1)S(1)} %get-tuple-element.56), channel_id=1, source_target_pairs={{1,2},{2,1},{5,6},{6,5},{9,10},{10,9},{13,14},{14,13},{17,18},{18,... | collective-permute-start | bytes 1179656 | tf_op jit(solution)/shard_map/ppermute | solution.py:290
  80.1 10.2 %collective-permute-start.17 = (f16[256,768]{1,0:T(8,128)(2,1)S(1)}, f16[256,768]{1,0:T(8,128)(2,1)S(1)}, u32[]{:S(2)}, u32[]{:S(2)}) collective-permute-start(f16[256,768]{1,0:T(8,128)(2,1)S(1)} %select_convert_fusion.2), channel_id=1, source_target_pairs={{0,1},{1,0},{2,3},{3,2},{4,5},{5,4},{6,7},{7,6},{8,9},{9,8},{10,11... | collective-permute-start | bytes 1179656 | tf_op jit(solution)/shard_map/ppermute | solution.py:288
  89.3 5.9 %copy-start.7 = (f32[256,768]{1,0:T(8,128)}, f32[256,768]{1,0:T(8,128)S(1)}, u32[]{:S(2)}) copy-start(f32[256,768]{1,0:T(8,128)S(1)} %get-tuple-element.38) | copy-start | bytes 2359300
  89.3 27.4 %copy-start.21 = (s32[3,3,1024]{2,1,0:T(4,128)S(1)}, s32[3,3,1024]{2,1,0:T(4,128)}, u32[]{:S(2)}) copy-start(s32[3,3,1024]{2,1,0:T(4,128)} %param.12) | copy-start | bytes 110596
  89.3 27.5 %copy-start.19 = (f32[16,1024]{1,0:T(8,128)S(1)}, f32[16,1024]{1,0:T(8,128)}, u32[]{:S(2)}) copy-start(f32[16,1024]{1,0:T(8,128)} %param.14) | copy-start | bytes 196612
  89.3 27.5 %copy-start.20 = (s32[16,1024]{1,0:T(8,128)S(1)}, s32[16,1024]{1,0:T(8,128)}, u32[]{:S(2)}) copy-start(s32[16,1024]{1,0:T(8,128)} %param.13) | copy-start | bytes 196612
  89.4 30.8 %copy-start.18 = (f32[1024]{0:T(1024)S(1)}, f32[1024]{0:T(1024)}, u32[]{:S(2)}) copy-start(f32[1024]{0:T(1024)} %param.15) | copy-start | bytes 12292
  91.5 8.7 %collective-permute-start.19 = (f16[256,768]{1,0:T(8,128)(2,1)}, f16[256,768]{1,0:T(8,128)(2,1)}, u32[]{:S(2)}, u32[]{:S(2)}) collective-permute-start(f16[256,768]{1,0:T(8,128)(2,1)} %select_convert_fusion.1), channel_id=1, source_target_pairs={{0,1},{1,0},{2,3},{3,2},{4,5},{5,4},{6,7},{7,6},{8,9},{9,8},{10,11... | collective-permute-start | bytes 1179656 | tf_op jit(solution)/shard_map/ppermute | solution.py:288
  93.8 7.9 %collective-permute-start.18 = (f16[256,768]{1,0:T(8,128)(2,1)}, f16[256,768]{1,0:T(8,128)(2,1)}, u32[]{:S(2)}, u32[]{:S(2)}) collective-permute-start(f16[256,768]{1,0:T(8,128)(2,1)} %get-tuple-element.59), channel_id=1, source_target_pairs={{1,2},{2,1},{5,6},{6,5},{9,10},{10,9},{13,14},{14,13},{17,18},{18,... | collective-permute-start | bytes 1179656 | tf_op jit(solution)/shard_map/ppermute | solution.py:290
  95.2 5.0 %copy-start.17 = (f32[256,768]{1,0:T(8,128)S(1)}, f32[256,768]{1,0:T(8,128)}, u32[]{:S(2)}) copy-start(f32[256,768]{1,0:T(8,128)} %copy-done.16) | copy-start | bytes 2359300
  95.2 6.5 %copy-start.4 = (f32[256,768]{1,0:T(8,128)S(1)}, f32[256,768]{1,0:T(8,128)}, u32[]{:S(2)}) copy-start(f32[256,768]{1,0:T(8,128)} %copy-done.3) | copy-start | bytes 2359300
  95.2 6.5 %copy-start.6 = (f32[256,768]{1,0:T(8,128)S(1)}, f32[256,768]{1,0:T(8,128)}, u32[]{:S(2)}) copy-start(f32[256,768]{1,0:T(8,128)} %copy-done.5) | copy-start | bytes 2359300
  95.2 13.4 %copy-start.8 = (f32[256,768]{1,0:T(8,128)S(1)}, f32[256,768]{1,0:T(8,128)}, u32[]{:S(2)}) copy-start(f32[256,768]{1,0:T(8,128)} %copy-done.7) | copy-start | bytes 2359300
  95.2 19.1 %copy-start.15 = (f32[256,768]{1,0:T(8,128)S(1)}, f32[256,768]{1,0:T(8,128)}, u32[]{:S(2)}) copy-start(f32[256,768]{1,0:T(8,128)} %copy-done.14) | copy-start | bytes 2359300
  100.2 14.2 %copy-start.9 = (f32[256,768]{1,0:T(8,128)}, f32[256,768]{1,0:T(8,128)S(1)}, u32[]{:S(2)}) copy-start(f32[256,768]{1,0:T(8,128)S(1)} %get-tuple-element.63) | copy-start | bytes 2359300
  102.9 5.7 %collective-permute-start.20 = (f16[256,768]{1,0:T(8,128)(2,1)S(1)}, f16[256,768]{1,0:T(8,128)(2,1)S(1)}, u32[]{:S(2)}, u32[]{:S(2)}) collective-permute-start(f16[256,768]{1,0:T(8,128)(2,1)S(1)} %get-tuple-element.62), channel_id=1, source_target_pairs={{1,2},{2,1},{5,6},{6,5},{9,10},{10,9},{13,14},{14,13},{17,18},{18,... | collective-permute-start | bytes 1179656 | tf_op jit(solution)/shard_map/ppermute | solution.py:290
  103.6 10.8 %collective-permute-start.21 = (f16[256,768]{1,0:T(8,128)(2,1)S(1)}, f16[256,768]{1,0:T(8,128)(2,1)S(1)}, u32[]{:S(2)}, u32[]{:S(2)}) collective-permute-start(f16[256,768]{1,0:T(8,128)(2,1)S(1)} %select_convert_fusion), channel_id=1, source_target_pairs={{0,1},{1,0},{2,3},{3,2},{4,5},{5,4},{6,7},{7,6},{8,9},{9,8},{10,11... | collective-permute-start | bytes 1179656 | tf_op jit(solution)/shard_map/ppermute | solution.py:288
  115.3 14.1 %collective-permute-start.22 = (f16[256,768]{1,0:T(8,128)(2,1)}, f16[256,768]{1,0:T(8,128)(2,1)}, u32[]{:S(2)}, u32[]{:S(2)}) collective-permute-start(f16[256,768]{1,0:T(8,128)(2,1)} %get-tuple-element.65), channel_id=1, source_target_pairs={{1,2},{2,1},{5,6},{6,5},{9,10},{10,9},{13,14},{14,13},{17,18},{18,... | collective-permute-start | bytes 1179656 | tf_op jit(solution)/shard_map/ppermute | solution.py:290
  116.9 20.4 %collective-permute-start.26 = (f16[256,768]{1,0:T(8,128)(2,1)S(1)}, f16[256,768]{1,0:T(8,128)(2,1)}, u32[]{:S(2)}, u32[]{:S(2)}) collective-permute-start(f16[256,768]{1,0:T(8,128)(2,1)S(1)} %add_convert_fusion.1), channel_id=1, source_target_pairs={{0,1},{1,0},{2,3},{3,2},{4,5},{5,4},{6,7},{7,6},{8,9},{9,8},{10,11... | collective-permute-start | bytes 1179656 | tf_op jit(solution)/shard_map/ppermute | solution.py:288
  130.7 10.7 %collective-permute-start.27 = (f16[256,768]{1,0:T(8,128)(2,1)S(1)}, f16[256,768]{1,0:T(8,128)(2,1)S(1)}, u32[]{:S(2)}, u32[]{:S(2)}) collective-permute-start(f16[256,768]{1,0:T(8,128)(2,1)S(1)} %add_convert_fusion), channel_id=1, source_target_pairs={{0,1},{1,0},{2,3},{3,2},{4,5},{5,4},{6,7},{7,6},{8,9},{9,8},{10,11... | collective-permute-start | bytes 1179656 | tf_op jit(solution)/shard_map/ppermute | solution.py:288
  130.9 23.0 %collective-permute-start.23 = (bf16[8,32,256]{2,1,0:T(8,128)(2,1)S(1)}, bf16[8,32,256]{2,1,0:T(8,128)(2,1)S(1)}, u32[]{:S(2)}, u32[]{:S(2)}) collective-permute-start(bf16[8,32,256]{2,1,0:T(8,128)(2,1)S(1)} %get-tuple-element.87), channel_id=1, source_target_pairs={{0,1},{1,0},{2,3},{3,2},{4,5},{5,4},{6,7},{7,6},{8,9},{9,8},{10,11... | collective-permute-start | bytes 393224 | tf_op jit(solution)/shard_map/ppermute | solution.py:314
  133.0 24.3 %collective-permute-start.24 = (bf16[8,32,256]{2,1,0:T(8,128)(2,1)S(1)}, bf16[8,32,256]{2,1,0:T(8,128)(2,1)S(1)}, u32[]{:S(2)}, u32[]{:S(2)}) collective-permute-start(bf16[8,32,256]{2,1,0:T(8,128)(2,1)S(1)} %get-tuple-element.86), channel_id=1, source_target_pairs={{0,2},{2,0},{1,3},{3,1},{4,6},{6,4},{5,7},{7,5},{8,10},{10,8},{9,1... | collective-permute-start | bytes 393224 | tf_op jit(solution)/shard_map/ppermute | solution.py:315
  134.0 23.2 %collective-permute-start.25 = (bf16[8,32,256]{2,1,0:T(8,128)(2,1)S(1)}, bf16[8,32,256]{2,1,0:T(8,128)(2,1)S(1)}, u32[]{:S(2)}, u32[]{:S(2)}) collective-permute-start(bf16[8,32,256]{2,1,0:T(8,128)(2,1)S(1)} %get-tuple-element.85), channel_id=1, source_target_pairs={{0,3},{3,0},{4,7},{7,4},{8,11},{11,8},{12,15},{15,12},{16,19},{19,... | collective-permute-start | bytes 393224 | tf_op jit(solution)/shard_map/ppermute | solution.py:316
  150.9 6.4 %collective-permute-start.28 = (bf16[8,32,256]{2,1,0:T(8,128)(2,1)S(1)}, bf16[8,32,256]{2,1,0:T(8,128)(2,1)S(1)}, u32[]{:S(2)}, u32[]{:S(2)}) collective-permute-start(bf16[8,32,256]{2,1,0:T(8,128)(2,1)S(1)} %get-tuple-element.90), channel_id=1, source_target_pairs={{0,1},{1,0},{2,3},{3,2},{4,5},{5,4},{6,7},{7,6},{8,9},{9,8},{10,11... | collective-permute-start | bytes 393224 | tf_op jit(solution)/shard_map/ppermute | solution.py:314
  151.0 6.4 %collective-permute-start.29 = (bf16[8,32,256]{2,1,0:T(8,128)(2,1)S(1)}, bf16[8,32,256]{2,1,0:T(8,128)(2,1)S(1)}, u32[]{:S(2)}, u32[]{:S(2)}) collective-permute-start(bf16[8,32,256]{2,1,0:T(8,128)(2,1)S(1)} %get-tuple-element.89), channel_id=1, source_target_pairs={{0,2},{2,0},{1,3},{3,1},{4,6},{6,4},{5,7},{7,5},{8,10},{10,8},{9,1... | collective-permute-start | bytes 393224 | tf_op jit(solution)/shard_map/ppermute | solution.py:315
  153.9 8.6 %collective-permute-start.30 = (bf16[8,32,256]{2,1,0:T(8,128)(2,1)S(1)}, bf16[8,32,256]{2,1,0:T(8,128)(2,1)S(1)}, u32[]{:S(2)}, u32[]{:S(2)}) collective-permute-start(bf16[8,32,256]{2,1,0:T(8,128)(2,1)S(1)} %get-tuple-element.88), channel_id=1, source_target_pairs={{0,3},{3,0},{4,7},{7,4},{8,11},{11,8},{12,15},{15,12},{16,19},{19,... | collective-permute-start | bytes 393224 | tf_op jit(solution)/shard_map/ppermute | solution.py:316
  (5 other events, 4.9 us)
